TPU v7x, 128 devices: a whole 4x4x4 slice. The times are simulated.
128 devices in a mesh: row: 8 (over x, y_hi), col: 16 (over y_lo, z, core).
Axes of the slice: x: 4, y: 4 (y_hi: 2, y_lo: 2; y = y_hi * 2 + y_lo), z: 4, core: 2. Of those that a mesh axis runs over, the one named last changes fastest.
Arguments:
- field: float32 [256, 1024, 128], P('row', 'col'), may hold values from -6 to 6
- expand_weight: float32 [128, 512], replicated, may hold values from -0.5 to 0.5
- depth_weight: float32 [9, 512], replicated, may hold values from -2 to 2
- project_weight: float32 [512, 128], replicated, may hold values from -0.25 to 0.25
- qkv_weight: float32 [128, 384], replicated, may hold values from -0.5 to 0.5
- out_weight: float32 [128, 128], replicated, may hold values from -0.5 to 0.5
- pos_bias: float32 [4, 64, 64], replicated, may hold values from -4 to 300
- cotangent: float32 [256, 1024, 128], P('row', 'col'), may hold values from -6 to 6
Outputs:
- block_out: float32 [256, 1024, 128], P('row', 'col')
- grad_field: float32 [256, 1024, 128], P('row', 'col')
- grad_expand: float32 [128, 512], replicated
- grad_depth: float32 [9, 512], replicated
- grad_project: float32 [512, 128], replicated
- grad_qkv: float32 [128, 384], replicated
- grad_out: float32 [128, 128], replicated
- grad_bias: float32 [4, 64, 64], replicated
All inputs are finite; a program needn't handle non-finite values.
Results may differ from a plain program's by a relative error of at most 0.00013.
Values sent between devices are 32-bit elements; how exact they have to be, the bound alone decides.
No kernel may reach another device: no remote copies, remote signals or barrier semaphores. Data moves between devices by JAX's collectives and lax.ppermute only.
A program may use at most 128 MiB of HBM per device.

v0:
```python
import jax
import jax.numpy as jnp
from jax import lax
from jax.sharding import PartitionSpec as P

GRID = 8


def extended(cells, sides, width):
    for axis, dim in sides:
        count = lax.axis_size(axis)
        ends = count - 1
        head = lax.slice_in_dim(cells, 0, width, axis=dim)
        tail = lax.slice_in_dim(cells, cells.shape[dim] - width, cells.shape[dim], axis=dim)
        cells = jnp.concatenate(
            [
                lax.ppermute(tail, axis, [(i, (i + 1) % count) for i in range(ends)]),
                cells,
                lax.ppermute(head, axis, [((i + 1) % count, i) for i in range(ends)]),
            ],
            axis=dim,
        )
    return cells


def layer_norm(values):
    center = values - jnp.mean(values, axis=-1, keepdims=True)
    spread = jnp.mean(center * center, axis=-1, keepdims=True)
    return center * lax.rsqrt(spread + 1e-05)


def expand_part(tile, expand_weight):
    normed = layer_norm(tile)
    return jax.nn.gelu(
        jnp.einsum("ijc,cf->ijf", normed, expand_weight, precision=lax.Precision.HIGHEST)
    )


def project_part(depth_out, project_weight):
    return jnp.einsum(
        "ijf,fc->ijc", jax.nn.gelu(depth_out), project_weight, precision=lax.Precision.HIGHEST
    )


def depthwise(padded, depth_weight, out_rows, out_cols):
    total = jnp.zeros((out_rows, out_cols, padded.shape[2]), jnp.float32)
    for row_shift in range(3):
        for col_shift in range(3):
            total = (
                total
                + padded[row_shift : row_shift + out_rows, col_shift : col_shift + out_cols]
                * depth_weight[3 * row_shift + col_shift]
            )
    return total


def depthwise_back(grad_padded, depth_weight, out_rows, out_cols):
    total = jnp.zeros((out_rows, out_cols, grad_padded.shape[2]), jnp.float32)
    for row_shift in range(3):
        for col_shift in range(3):
            window = grad_padded[
                2 - row_shift : 2 - row_shift + out_rows, 2 - col_shift : 2 - col_shift + out_cols
            ]
            total = total + window * depth_weight[3 * row_shift + col_shift]
    return total


def depth_grads(padded, grad_depth_out, out_rows, out_cols):
    taps = []
    for row_shift in range(3):
        for col_shift in range(3):
            window = padded[row_shift : row_shift + out_rows, col_shift : col_shift + out_cols]
            taps.append(jnp.sum(window * grad_depth_out, axis=(0, 1)))
    return jnp.stack(taps)


def attend(grouped, qkv_weight, out_weight, pos_bias):
    groups, places, channels = grouped.shape
    head_count = pos_bias.shape[0]
    head_size = channels // head_count
    normed = layer_norm(grouped)
    packed = jnp.einsum("gpc,cf->gpf", normed, qkv_weight, precision=lax.Precision.HIGHEST)
    query_rows = packed[..., :channels].reshape(groups, places, head_count, head_size)
    key_rows = packed[..., channels : 2 * channels].reshape(groups, places, head_count, head_size)
    value_rows = packed[..., 2 * channels :].reshape(groups, places, head_count, head_size)
    scores = jnp.einsum(
        "gphd,gqhd->ghpq", query_rows, key_rows, precision=lax.Precision.HIGHEST
    ) * head_size ** (-0.5)
    scores = scores + pos_bias[None]
    weights = jax.nn.softmax(scores, axis=-1)
    mixture = jnp.einsum(
        "ghpq,gqhd->gphd", weights, value_rows, precision=lax.Precision.HIGHEST
    ).reshape(groups, places, channels)
    return jnp.einsum("gpc,cf->gpf", mixture, out_weight, precision=lax.Precision.HIGHEST)


def padded_hidden(hidden):
    return extended(hidden, (("row", 0), ("col", 1)), 1)


def grid_layout(tile_rows, tile_cols):
    row_count = lax.axis_size("row")
    col_count = lax.axis_size("col")
    row_span = tile_rows * min(row_count, GRID) // GRID
    col_span = tile_cols * min(col_count, GRID) // GRID
    row_outer = tile_rows // row_span
    col_outer = tile_cols // col_span
    row_block = row_span // row_count
    col_block = col_span // col_count
    row_repeat = max(row_count, GRID) // GRID
    col_repeat = max(col_count, GRID) // GRID
    return (
        row_count,
        col_count,
        row_outer,
        col_outer,
        row_block,
        col_block,
        row_repeat,
        col_repeat,
    )


def swap_blocks(blocks):
    flat = blocks.reshape((blocks.shape[0] * blocks.shape[1],) + blocks.shape[2:])
    moved = lax.all_to_all(flat, ("row", "col"), split_axis=0, concat_axis=0, tiled=True)
    return moved.reshape(blocks.shape)


def into_grid(tile):
    tile_rows, tile_cols, channels = tile.shape
    row_count, col_count, row_outer, col_outer, row_block, col_block, row_repeat, col_repeat = (
        grid_layout(tile_rows, tile_cols)
    )
    blocks = tile.reshape(
        row_outer, row_count, row_block, col_outer, col_count, col_block, channels
    )
    blocks = blocks.transpose(1, 4, 0, 2, 3, 5, 6)
    arrived = swap_blocks(blocks)
    arrived = arrived.transpose(0, 2, 1, 4, 3, 5, 6)
    arrived = arrived.reshape(GRID, row_repeat, GRID, col_repeat, row_block, col_block, channels)
    arrived = arrived.transpose(1, 4, 3, 5, 0, 2, 6)
    return arrived.reshape(-1, GRID * GRID, channels)


def from_grid(grouped, tile_rows, tile_cols):
    channels = grouped.shape[2]
    row_count, col_count, row_outer, col_outer, row_block, col_block, row_repeat, col_repeat = (
        grid_layout(tile_rows, tile_cols)
    )
    blocks = grouped.reshape(row_repeat, row_block, col_repeat, col_block, GRID, GRID, channels)
    blocks = blocks.transpose(4, 0, 5, 2, 1, 3, 6)
    blocks = blocks.reshape(
        row_count, row_outer, col_count, col_outer, row_block, col_block, channels
    )
    blocks = blocks.transpose(0, 2, 1, 4, 3, 5, 6)
    returned = swap_blocks(blocks)
    returned = returned.transpose(2, 0, 3, 4, 1, 5, 6)
    return returned.reshape(tile_rows, tile_cols, channels)


def on_device(
    field, expand_weight, depth_weight, project_weight, qkv_weight, out_weight, pos_bias, cotangent
):
    tile_rows, tile_cols = (field.shape[0], field.shape[1])
    hidden, expand_back = jax.vjp(expand_part, field, expand_weight)
    padded = padded_hidden(hidden)
    depth_out = depthwise(padded, depth_weight, tile_rows, tile_cols)
    branch, project_back = jax.vjp(project_part, depth_out, project_weight)
    mixed = field + branch
    grouped = into_grid(mixed)
    attended, attend_back = jax.vjp(attend, grouped, qkv_weight, out_weight, pos_bias)
    block_out = mixed + from_grid(attended, tile_rows, tile_cols)
    grad_grouped, grad_qkv, grad_out, grad_bias = attend_back(into_grid(cotangent))
    grad_mixed = cotangent + from_grid(grad_grouped, tile_rows, tile_cols)
    grad_depth_out, grad_project = project_back(grad_mixed)
    grad_padded = extended(grad_depth_out, (("row", 0), ("col", 1)), 1)
    grad_hidden = depthwise_back(grad_padded, depth_weight, tile_rows, tile_cols)
    grad_depth = depth_grads(padded, grad_depth_out, tile_rows, tile_cols)
    grad_inner, grad_expand = expand_back(grad_hidden)
    grad_field = grad_mixed + grad_inner
    grad_expand, grad_depth, grad_project, grad_qkv, grad_out, grad_bias = lax.psum(
        (grad_expand, grad_depth, grad_project, grad_qkv, grad_out, grad_bias), ("row", "col")
    )
    return (
        block_out,
        grad_field,
        grad_expand,
        grad_depth,
        grad_project,
        grad_qkv,
        grad_out,
        grad_bias,
    )


def solution(mesh):
    in_specs = (P("row", "col", None), P(), P(), P(), P(), P(), P(), P("row", "col", None))
    out_specs = (P("row", "col", None), P("row", "col", None), P(), P(), P(), P(), P(), P())
    return jax.shard_map(
        on_device, mesh=mesh, in_specs=in_specs, out_specs=out_specs, check_vma=False
    )
```

profile of v0, /device:TPU:1, one launch (start us, length us, event | category | flops | bytes accessed | tf_op | source)
XLA Modules:
  0.0 554.9 jit_solution(12982093761464108424)
XLA Ops:
  11.3 8.0 %multiply_multiply_fusion.5 = (f32[32,64,512]{2,1,0:T(8,128)S(1)}, f32[32,64,512]{2,1,0:T(8,128)}) fusion(f32[128,512]{1,0:T(8,128)S(1)} %copy-done, f32[32,64,128]{2,1,0:T(8,128)} %param.8, f32[32,64]{1,0:T(8,128)S(1)} %fusion.69, f32[32,64]{1,0:T(8,128)S(1)} %broadcast_multiply_fusion.1), kind=kOutput, calls=%fused_computation.59 | convolution fusion | flops 1619525632 | bytes 9715712 | tf_op jit(solution)/shard_map/jvp(ijc,cf->ijf)/dot_general | solution.py:35
  21.3 5.7 %collective-permute-start = (f32[1,64,512]{2,1,0:T(8,128)S(1)}, f32[1,64,512]{2,1,0:T(8,128)S(1)}, u32[]{:S(2)}, u32[]{:S(2)}) collective-permute-start(f32[1,64,512]{2,1,0:T(8,128)S(1)} %get-tuple-element.63), channel_id=1, source_target_pairs={{0,16},{16,32},{32,48},{48,64},{64,80},{80,96},{96,112},{1,17},{17... | collective-permute-start | bytes 393224 | tf_op jit(solution)/shard_map/ppermute | solution.py:17
  30.1 11.9 %all-to-all-start.2 = ((f32[128,1,4,1,4,128]{5,4,2,3,1,0:T(4,128)}), f32[128,1,4,1,4,128]{5,4,2,3,1,0:T(4,128)S(1)}, u32[]{:S(2)}, u32[]{:S(2)}) async-start(f32[128,1,4,1,4,128]{5,4,2,3,1,0:T(4,128)} %copy.158), calls=%async_computation.2 | async-start | bytes 2097152 | tf_op jit(solution)/shard_map/all_to_all | solution.py:126
  56.5 13.9 %multiply_add_fusion.1 = f32[32,64,512]{2,1,0:T(8,128)} fusion(f32[32,64,512]{2,1,0:T(8,128)} %copy-done.6, f32[34,65,512]{2,1,0:T(8,128)S(1)} %get-tuple-element.58, f32[34,65,512]{2,1,0:T(8,128)S(1)} %get-tuple-element.57, f32[1,64,512]{2,1,0:T(8,128)S(1)} %collective-permute-done, f32[1,64,512]{2,1,0:T(8,128)S(1)} %collective-permute-done.1, ...), kind=kLoop, calls=%fused_computation.53 | loop fusion | flops 19922944 | bytes 33835008 | tf_op jit(solution)/shard_map/add | solution.py:50
  70.5 6.4 %fusion.38 = f32[32,64,128]{2,1,0:T(8,128)S(1)} fusion(f32[32,64,128]{2,1,0:T(8,128)S(1)} %copy-done.8, f32[32,64,512]{2,1,0:T(8,128)} %multiply_add_fusion.1, f32[512,128]{1,0:T(8,128)S(1)} %copy-done.59), kind=kOutput, calls=%fused_computation.76 | convolution fusion | flops 1619263488 | bytes 6553600 | tf_op jit(solution)/shard_map/jvp(ijf,fc->ijc)/dot_general | solution.py:40
  79.7 11.2 %all-to-all-start = ((f32[128,1,4,1,4,128]{5,4,2,3,1,0:T(4,128)}), f32[128,1,4,1,4,128]{5,4,2,3,1,0:T(4,128)}, u32[]{:S(2)}, u32[]{:S(2)}) async-start(f32[128,1,4,1,4,128]{5,4,2,3,1,0:T(4,128)} %copy.141), calls=%async_computation | async-start | bytes 2097152 | tf_op jit(solution)/shard_map/all_to_all | solution.py:126
  96.9 12.7 %all-to-all-done = f32[128,1,4,1,4,128]{5,4,2,3,1,0:T(4,128)} async-done(((f32[128,1,4,1,4,128]{5,4,2,3,1,0:T(4,128)}), f32[128,1,4,1,4,128]{5,4,2,3,1,0:T(4,128)}, u32[]{:S(2)}, u32[]{:S(2)}) %all-to-all-start) | async-done | bytes 1048608 | tf_op jit(solution)/shard_map/all_to_all | solution.py:126
  137.7 8.9 %fusion.26 = (f32[32,4,64]{2,1,0:T(4,128)S(1)}, f32[32,4,64,64]{2,3,1,0:T(8,128)S(1)}) fusion(f32[4,64,64]{1,2,0:T(8,128)S(1)} %copy.150, f32[32,64,4,32]{1,3,2,0:T(8,128)} %bitcast.142, f32[32,64,4,32]{1,3,2,0:T(8,128)} %bitcast.140), kind=kOutput, calls=%fused_computation.60 | convolution fusion | flops 202891264 | bytes 4292608 | tf_op jit(solution)/shard_map/jvp(gphd,gqhd->ghpq)/dot_general | solution.py:86
  149.8 8.5 %fusion.31 = f32[32,4,32,64]{3,2,1,0:T(8,128)} fusion(f32[32,64,4,32]{1,3,2,0:T(8,128)S(1)} %copy-done.15, f32[32,4,64]{2,1,0:T(4,128)S(1)} %fusion.82, f32[32,4,64,64]{2,3,1,0:T(8,128)S(1)} %get-tuple-element.80, f32[32,4,64]{2,1,0:T(4,128)S(1)} %get-tuple-element.79, f32[4,64,64]{1,2,0:T(8,128)S(1)} %copy.150), kind=kOutput, calls=%fused_computation.66 | convolution fusion | flops 203423744 | bytes 4325376 | tf_op jit(solution)/shard_map/transpose(jvp(ghpq,gqhd->gphd))/dot_general | solution.py:91
  158.3 8.0 %multiply_reduce_fusion.9 = (f32[32,4,64]{2,1,0:T(4,128)S(1)}, f32[32,4,64,64]{2,3,1,0:T(8,128)S(1)}) fusion(f32[32,4,64]{2,1,0:T(4,128)S(1)} %multiply_divide_fusion, f32[32,4,64]{2,1,0:T(4,128)S(1)} %get-tuple-element.79, f32[4,64,64]{1,2,0:T(8,128)S(1)} %copy.150, f32[32,4,64,64]{2,3,1,0:T(8,128)S(1)} %get-tuple-element.80, ...), kind=kOutput, calls=%fused_computation.50 | convolution fusion | flops 204464128 | bytes 6455296 | tf_op jit(solution)/shard_map/transpose(jvp(ghpq,gqhd->gphd))/dot_general | solution.py:91
  168.9 5.3 fusion.22
  174.2 8.5 %fusion.24 = f32[32,4,64,32]{2,3,1,0:T(8,128)} fusion(f32[32,64,4,32]{1,3,2,0:T(8,128)S(1)} %bitcast.143, f32[32,4,64,64]{2,3,1,0:T(8,128)S(1)} %get-tuple-element.52), kind=kOutput, calls=%fused_computation.56 | convolution fusion | flops 201850880 | bytes 4194304 | tf_op jit(solution)/shard_map/transpose(jvp(gphd,gqhd->ghpq))/dot_general | solution.py:86
  192.2 5.0 multiply_reduce_fusion.11
  202.3 6.0 %all-to-all-start.3 = ((f32[128,1,4,1,4,128]{5,4,2,3,1,0:T(4,128)}), f32[128,1,4,1,4,128]{5,4,2,3,1,0:T(4,128)}, u32[]{:S(2)}, u32[]{:S(2)}) async-start(f32[128,1,4,1,4,128]{5,4,2,3,1,0:T(4,128)} %copy.168), calls=%async_computation.3 | async-start | bytes 2097152 | tf_op jit(solution)/shard_map/all_to_all | solution.py:126
  208.3 8.7 %fusion.37 = f32[32,4,32,64]{3,2,1,0:T(8,128)} fusion(f32[32,64,4,32]{1,3,2,0:T(8,128)} %bitcast.151, f32[32,4,64]{2,1,0:T(4,128)S(1)} %fusion.82, f32[32,4,64,64]{2,3,1,0:T(8,128)} %copy-done.1, f32[32,4,64]{2,1,0:T(4,128)S(1)} %get-tuple-element.79, f32[4,64,64]{1,2,0:T(8,128)S(1)} %copy.150), kind=kOutput, calls=%fused_computation.73 | convolution fusion | flops 203423744 | bytes 4325376 | tf_op jit(solution)/shard_map/jvp(ghpq,gqhd->gphd)/dot_general | solution.py:91
  217.0 4.8 copy.152
  221.8 4.6 reshape.175
  234.9 10.4 %all-to-all-start.1 = ((f32[128,1,4,1,4,128]{5,4,2,3,1,0:T(4,128)}), f32[128,1,4,1,4,128]{5,4,2,3,1,0:T(4,128)}, u32[]{:S(2)}, u32[]{:S(2)}) async-start(f32[128,1,4,1,4,128]{5,4,2,3,1,0:T(4,128)} %copy.154), calls=%async_computation.1 | async-start | bytes 2097152 | tf_op jit(solution)/shard_map/all_to_all | solution.py:126
  248.7 23.0 %multiply_reduce_fusion = (f32[512]{0:T(512)}, f32[512]{0:T(512)}, f32[512]{0:T(512)}, f32[512]{0:T(512)}, f32[512]{0:T(512)}, /*index=5*/f32[512]{0:T(512)}, f3...) fusion(f32[34,65,512]{2,1,0:T(8,128)} %copy-done.3, f32[32,64,512]{2,1,0:T(8,128)} %copy-done.6, ...), kind=kOutput, calls=%fused_computation.40 | convolution fusion | flops 1659891200 | bytes 43534336 | tf_op jit(solution)/shard_map/transpose(jvp(ijf,fc->ijc))/dot_general | solution.py:40
  271.7 5.1 collective-permute-start.4
  292.5 8.2 %fusion.39 = f32[512,128]{1,0:T(8,128)} fusion(f32[32,64,128]{2,1,0:T(8,128)S(1)} %copy-done.21, f32[32,64,512]{2,1,0:T(8,128)S(1)} %copy-done.25), kind=kOutput, calls=%fused_computation.78 | convolution fusion | flops 1619001344 | bytes 5505024 | tf_op jit(solution)/shard_map/transpose(jvp(ijf,fc->ijc))/dot_general | solution.py:40
  304.3 66.4 %psum.43 = f32[9,512]{1,0:T(8,128)} all-reduce(f32[9,512]{1,0:T(8,128)S(1)} %stack.39), channel_id=1, replica_groups=mesh['row'=8,'col'=16] {'row','col'}, use_global_device_ids=true, to_apply=%region_21.0 | all-reduce | flops 4608 | bytes 36864 | tf_op jit(solution)/shard_map/psum | solution.py:182
  376.8 7.6 %fusion.5 = f32[32,64,512]{2,1,0:T(8,128)S(1)} fusion(f32[32,64,512]{2,1,0:T(8,128)S(1)} %copy-done.16, f32[34,65,512]{2,1,0:T(8,128)S(1)} %get-tuple-element.54, f32[32,64,512]{2,1,0:T(8,128)S(1)} %copy-done.5, f32[1,64,512]{2,1,0:T(8,128)S(1)} %collective-permute-done.4, f32[34,65,512]{2,1,0:T(8,128)S(1)} %get-tuple-element.53, ...), kind=kLoop, calls=%fused_computation.13 | loop fusion | flops 39845888 | bytes 38029312 | tf_op jit(solution)/shard_map/transpose(jvp())/add_any | solution.py:34
  396.5 143.3 %all-reduce.6.cloned.1.call-done = (f32[128,512]{1,0:T(8,128)}, f32[512,128]{1,0:T(8,128)}, f32[128,384]{1,0:T(8,128)}, f32[128,128]{1,0:T(8,128)}, f32[4,64,64]{1,2,0:T(8,128)}) async-done(((f32[128,512]{1,0:T(8,128)}, f32[512,128]{1,0:T(8,128)}, f32[128,384]{1,0:T(8,128)}, f32[128,128]{1,0:T(8,128)}, f32[4,64,64]{1,2,0:T(8,128)}), (f32[128,512]{1,0:T(8,128)}, f32[512,128]{1,0:T(8,128)}, ...) | async-done | bytes 851984 | tf_op jit(solution)/shard_map/psum | solution.py:182
  (211 shorter events, 137.6 us)
Async XLA Ops:
  11.3 16.9 %copy-start.17 = (f32[32,64,128]{2,1,0:T(8,128)S(1)}, f32[32,64,128]{2,1,0:T(8,128)}, u32[]{:S(2)}) copy-start(f32[32,64,128]{2,1,0:T(8,128)} %param.15) | copy-start | bytes 3145732
  21.3 20.7 %collective-permute-start = (f32[1,64,512]{2,1,0:T(8,128)S(1)}, f32[1,64,512]{2,1,0:T(8,128)S(1)}, u32[]{:S(2)}, u32[]{:S(2)}) collective-permute-start(f32[1,64,512]{2,1,0:T(8,128)S(1)} %get-tuple-element.63), channel_id=1, source_target_pairs={{0,16},{16,32},{32,48},{48,64},{64,80},{80,96},{96,112},{1,17},{17... | collective-permute-start | bytes 393224 | tf_op jit(solution)/shard_map/ppermute | solution.py:17
  26.9 15.0 %collective-permute-start.1 = (f32[1,64,512]{2,1,0:T(8,128)S(1)}, f32[1,64,512]{2,1,0:T(8,128)S(1)}, u32[]{:S(2)}, u32[]{:S(2)}) collective-permute-start(f32[1,64,512]{2,1,0:T(8,128)S(1)} %get-tuple-element.64), channel_id=1, source_target_pairs={{16,0},{32,16},{48,32},{64,48},{80,64},{96,80},{112,96},{17,1},{33... | collective-permute-start | bytes 393224 | tf_op jit(solution)/shard_map/ppermute | solution.py:19
  28.4 21.1 %copy-start.49 = (f32[9,512]{1,0:T(8,128)S(1)}, f32[9,512]{1,0:T(8,128)}, u32[]{:S(2)}) copy-start(f32[9,512]{1,0:T(8,128)} %param.10) | copy-start | bytes 55300
  30.1 49.6 %all-to-all-start.2 = ((f32[128,1,4,1,4,128]{5,4,2,3,1,0:T(4,128)}), f32[128,1,4,1,4,128]{5,4,2,3,1,0:T(4,128)S(1)}, u32[]{:S(2)}, u32[]{:S(2)}) async-start(f32[128,1,4,1,4,128]{5,4,2,3,1,0:T(4,128)} %copy.158), calls=%async_computation.2 | async-start | bytes 2097152 | tf_op jit(solution)/shard_map/all_to_all | solution.py:126
  42.0 14.4 %copy-start.26 = (f32[1,64,512]{2,1,0:T(8,128)}, f32[1,64,512]{2,1,0:T(8,128)S(1)}, u32[]{:S(2)}) copy-start(f32[1,64,512]{2,1,0:T(8,128)S(1)} %collective-permute-done.1) | copy-start | bytes 393220
  43.5 10.5 %collective-permute-start.2 = (f32[34,1,512]{2,1,0:T(1,128)S(1)}, f32[34,1,512]{2,1,0:T(1,128)S(1)}, u32[]{:S(2)}, u32[]{:S(2)}) collective-permute-start(f32[34,1,512]{2,1,0:T(1,128)S(1)} %get-tuple-element.59), channel_id=1, source_target_pairs={{0,1},{1,2},{2,3},{3,4},{4,5},{5,6},{6,7},{7,8},{8,9},{9,10},{10,1... | collective-permute-start | bytes 208904 | tf_op jit(solution)/shard_map/ppermute | solution.py:17
  47.3 7.6 %collective-permute-start.3 = (f32[34,1,512]{2,1,0:T(1,128)S(1)}, f32[34,1,512]{2,1,0:T(1,128)S(1)}, u32[]{:S(2)}, u32[]{:S(2)}) collective-permute-start(f32[34,1,512]{2,1,0:T(1,128)S(1)} %get-tuple-element.60), channel_id=1, source_target_pairs={{1,0},{2,1},{3,2},{4,3},{5,4},{6,5},{7,6},{8,7},{9,8},{10,9},{11,1... | collective-permute-start | bytes 208904 | tf_op jit(solution)/shard_map/ppermute | solution.py:19
  56.4 14.1 %copy-start.2 = (f32[34,65,512]{2,1,0:T(8,128)}, f32[34,65,512]{2,1,0:T(8,128)S(1)}, u32[]{:S(2)}) copy-start(f32[34,65,512]{2,1,0:T(8,128)S(1)} %get-tuple-element.57) | copy-start | bytes 13578244
  56.4 14.1 %copy-start.3 = (f32[34,65,512]{2,1,0:T(8,128)}, f32[34,65,512]{2,1,0:T(8,128)S(1)}, u32[]{:S(2)}) copy-start(f32[34,65,512]{2,1,0:T(8,128)S(1)} %get-tuple-element.58) | copy-start | bytes 13578244
  78.0 14.5 %copy-start.30 = (f32[128,128]{1,0:T(8,128)S(1)}, f32[128,128]{1,0:T(8,128)}, u32[]{:S(2)}) copy-start(f32[128,128]{1,0:T(8,128)} %param.13) | copy-start | bytes 196612
  79.7 30.0 %all-to-all-start = ((f32[128,1,4,1,4,128]{5,4,2,3,1,0:T(4,128)}), f32[128,1,4,1,4,128]{5,4,2,3,1,0:T(4,128)}, u32[]{:S(2)}, u32[]{:S(2)}) async-start(f32[128,1,4,1,4,128]{5,4,2,3,1,0:T(4,128)} %copy.141), calls=%async_computation | async-start | bytes 2097152 | tf_op jit(solution)/shard_map/all_to_all | solution.py:126
  146.7 19.7 %copy-start.1 = (f32[32,4,64,64]{2,3,1,0:T(8,128)}, f32[32,4,64,64]{2,3,1,0:T(8,128)S(1)}, u32[]{:S(2)}) copy-start(f32[32,4,64,64]{2,3,1,0:T(8,128)S(1)} %get-tuple-element.80) | copy-start | bytes 6291460
  202.3 32.6 %all-to-all-start.3 = ((f32[128,1,4,1,4,128]{5,4,2,3,1,0:T(4,128)}), f32[128,1,4,1,4,128]{5,4,2,3,1,0:T(4,128)}, u32[]{:S(2)}, u32[]{:S(2)}) async-start(f32[128,1,4,1,4,128]{5,4,2,3,1,0:T(4,128)} %copy.168), calls=%async_computation.3 | async-start | bytes 2097152 | tf_op jit(solution)/shard_map/all_to_all | solution.py:126
  234.9 65.9 %all-to-all-start.1 = ((f32[128,1,4,1,4,128]{5,4,2,3,1,0:T(4,128)}), f32[128,1,4,1,4,128]{5,4,2,3,1,0:T(4,128)}, u32[]{:S(2)}, u32[]{:S(2)}) async-start(f32[128,1,4,1,4,128]{5,4,2,3,1,0:T(4,128)} %copy.154), calls=%async_computation.1 | async-start | bytes 2097152 | tf_op jit(solution)/shard_map/all_to_all | solution.py:126
  245.2 294.5 %all-reduce.6.cloned.1.call-start = ((), (), s32[]{:S(2)}) async-start(), calls=%async_computation.4 | async-start | bytes 1835008 | tf_op jit(solution)/shard_map/psum | solution.py:182
  248.7 29.4 %copy-start.13 = (f32[1,4,2,4,8,8,128]{6,5,4,3,2,1,0:T(8,128)S(1)}, f32[1,4,2,4,8,8,128]{6,5,4,3,2,1,0:T(8,128)}, u32[]{:S(2)}) copy-start(f32[1,4,2,4,8,8,128]{6,5,4,3,2,1,0:T(8,128)} %copy-done.12) | copy-start | bytes 3145732
  271.7 20.8 %copy-start.21 = (f32[32,64,128]{2,1,0:T(8,128)S(1)}, f32[32,64,128]{2,1,0:T(8,128)}, u32[]{:S(2)}) copy-start(f32[32,64,128]{2,1,0:T(8,128)} %add.142) | copy-start | bytes 3145732
  271.7 20.8 %copy-start.25 = (f32[32,64,512]{2,1,0:T(8,128)S(1)}, f32[32,64,512]{2,1,0:T(8,128)}, u32[]{:S(2)}) copy-start(f32[32,64,512]{2,1,0:T(8,128)} %multiply_add_fusion.1) | copy-start | bytes 12582916
  271.7 10.5 %collective-permute-start.4 = (f32[1,64,512]{2,1,0:T(8,128)S(1)}, f32[1,64,512]{2,1,0:T(8,128)S(1)}, u32[]{:S(2)}, u32[]{:S(2)}) collective-permute-start(f32[1,64,512]{2,1,0:T(8,128)S(1)} %get-tuple-element.61), channel_id=1, source_target_pairs={{0,16},{16,32},{32,48},{48,64},{64,80},{80,96},{96,112},{1,17},{17... | collective-permute-start | bytes 393224 | tf_op jit(solution)/shard_map/ppermute | solution.py:17
  276.8 7.8 %collective-permute-start.5 = (f32[1,64,512]{2,1,0:T(8,128)S(1)}, f32[1,64,512]{2,1,0:T(8,128)S(1)}, u32[]{:S(2)}, u32[]{:S(2)}) collective-permute-start(f32[1,64,512]{2,1,0:T(8,128)S(1)} %get-tuple-element.62), channel_id=1, source_target_pairs={{16,0},{32,16},{48,32},{64,48},{80,64},{96,80},{112,96},{17,1},{33... | collective-permute-start | bytes 393224 | tf_op jit(solution)/shard_map/ppermute | solution.py:19
  285.4 85.4 %collective-permute-start.6 = (f32[34,1,512]{2,1,0:T(1,128)}, f32[34,1,512]{2,1,0:T(1,128)S(1)}, u32[]{:S(2)}, u32[]{:S(2)}) collective-permute-start(f32[34,1,512]{2,1,0:T(1,128)} %get-tuple-element.55), channel_id=1, source_target_pairs={{1,0},{2,1},{3,2},{4,3},{5,4},{6,5},{7,6},{8,7},{9,8},{10,9},{11,1... | collective-permute-start | bytes 208904 | tf_op jit(solution)/shard_map/ppermute | solution.py:19
  288.8 82.0 %collective-permute-start.7 = (f32[34,1,512]{2,1,0:T(1,128)}, f32[34,1,512]{2,1,0:T(1,128)S(1)}, u32[]{:S(2)}, u32[]{:S(2)}) collective-permute-start(f32[34,1,512]{2,1,0:T(1,128)} %get-tuple-element.56), channel_id=1, source_target_pairs={{0,1},{1,2},{2,3},{3,4},{4,5},{5,6},{6,7},{7,8},{8,9},{9,10},{10,1... | collective-permute-start | bytes 208904 | tf_op jit(solution)/shard_map/ppermute | solution.py:17
  300.7 70.1 %copy-start.28 = (f32[1,64,512]{2,1,0:T(8,128)S(1)}, f32[1,64,512]{2,1,0:T(8,128)}, u32[]{:S(2)}) copy-start(f32[1,64,512]{2,1,0:T(8,128)} %copy-done.27) | copy-start | bytes 393220
  (49 other events, 283.9 us)
Sparse Core Ops, SparseCore 0:
  393.5 146.1 all-reduce.5
where the time goes:
time: 562 us; the launch traced here: 555 us
  waiting for transfers between devices  164 us (29%)
  matrix products  124 us (22%)
  local copies, waits for them, and re-layouts  67.1 us (12%)
  blocking collectives  66.4 us (12%)
  starting transfers between devices  65.8 us (12%)
  other arithmetic  52.8 us (9%)
  between operations  15.3 us (3%)
    psum x1, waiting for transfers between devices, on_device(): lax.psum((grad_expand, grad_depth, grad_project, grad_qkv, grad_out, grad...  143 us
    psum x1, blocking collectives, on_device(): lax.psum((grad_expand, grad_depth, grad_project, grad_qkv, grad_out, grad...  66.4 us
    all_to_all x4, starting transfers between devices, swap_blocks(): lax.all_to_all(flat, ('row', 'col'), split_axis=0, concat_axis=0, tiled=T...  39.5 us
    dot_general x3, matrix products, project_part(): jnp.einsum('ijf,fc->ijc', jax.nn.gelu(depth_out), project_weight, precisi...  37.6 us
    dot_general x3, matrix products, attend(): jnp.einsum('ghpq,gqhd->gphd', weights, value_rows, precision=lax.Precisio...  25.2 us
    dot_general x3, matrix products, attend(): jnp.einsum('gphd,gqhd->ghpq', query_rows, key_rows, precision=lax.Precisi...  22.7 us
    ppermute x4, starting transfers between devices, extended(): lax.ppermute(tail, axis, [(i, (i + 1) % count) for i in range(ends)])  18.2 us
    unnamed x126, local copies, waits for them, and re-layouts  16 us
  transfers between devices with their start and end apart: 13, of which 5 were waited for; matrix products, arithmetic and copies ran while one was open for 19% of the time, Pallas kernels for 0%

commit v1 on v0

v1 whole, which is shorter than its diff:
```python
import functools

import jax
import jax.numpy as jnp
from jax import lax
from jax.experimental import pallas as pl
from jax.experimental.pallas import tpu as pltpu
from jax.sharding import Mesh, PartitionSpec as P

GRID = 8
HEADS = 4
ALL = ("row", "ch", "core")
COLS = ("ch", "core")
PAIRS = ("row", "ch")
K0 = 0.7978845608028654
K1 = K0 * 0.044715
F32 = jnp.float32
BF16 = jnp.bfloat16
NN = (((1,), (0,)), ((), ()))
NT = (((1,), (1,)), ((), ()))
TN = (((0,), (0,)), ((), ()))


def split(values):
    high = values.astype(BF16)
    return high, (values - high.astype(F32)).astype(BF16)


def dot(a, b, dims):
    return lax.dot_general(a, b, dims, preferred_element_type=F32)


def dot3(a, b, dims):
    a_high, a_low = a if isinstance(a, tuple) else split(a)
    b_high, b_low = b if isinstance(b, tuple) else split(b)
    return dot(a_high, b_high, dims) + (dot(a_low, b_high, dims) + dot(a_high, b_low, dims))


def normalize(values):
    center = values - jnp.mean(values, axis=-1, keepdims=True)
    spread = jnp.mean(center * center, axis=-1, keepdims=True)
    scale = lax.rsqrt(spread + 1e-05)
    return center * scale, scale


def normalize_back(grad, normed, scale):
    grad_mean = jnp.mean(grad, axis=-1, keepdims=True)
    along = jnp.mean(grad * normed, axis=-1, keepdims=True)
    return scale * (grad - grad_mean - normed * along)


def gate(values):
    return 0.5 + 0.5 * jnp.tanh(values * (K0 + K1 * (values * values)))


def gelu(values):
    return values * gate(values)


def gelu_slope(values, gated):
    return gated + 2.0 * values * (gated - gated * gated) * (K0 + (3.0 * K1) * (values * values))


def call(body, grid, in_specs, out_specs, out_shape, scratch=(), flops=0, bytes_accessed=0, limit=56):
    return pl.pallas_call(
        body,
        grid=grid,
        in_specs=in_specs,
        out_specs=out_specs,
        out_shape=out_shape,
        scratch_shapes=list(scratch),
        compiler_params=pltpu.CompilerParams(vmem_limit_bytes=limit * 2**20),
        cost_estimate=pl.CostEstimate(
            flops=flops, bytes_accessed=bytes_accessed, transcendentals=0
        ),
    )


def shape(*dims):
    return jax.ShapeDtypeStruct(dims, F32)


def whole(*dims):
    return pl.BlockSpec(dims, lambda *_: (0,) * len(dims))


def rows(*dims):
    return pl.BlockSpec(dims, lambda i: (i,) + (0,) * (len(dims) - 1))


def expand_body(field_ref, weight_ref, pre_ref, hidden_ref):
    normed, _ = normalize(field_ref[...])
    pre = dot3(normed, weight_ref[...], NN)
    pre_ref[...] = pre
    hidden_ref[...] = gelu(pre)


def expand(field, weight):
    tokens, channels = field.shape
    wide = weight.shape[1]
    step = 256
    return call(
        expand_body,
        (tokens // step,),
        [rows(step, channels), whole(channels, wide)],
        [rows(step, wide), rows(step, wide)],
        [shape(tokens, wide), shape(tokens, wide)],
        flops=6 * tokens * channels * wide,
        bytes_accessed=4 * tokens * (channels + 2 * wide),
    )(field, weight)


def fill_padded(padded, step, last, body_ref, before_ref, after_ref, top, bottom, left, right):
    count, cols = body_ref.shape[0], body_ref.shape[1]
    padded[1 : 1 + count, 8 : 8 + cols, :] = body_ref[...]

    @pl.when(step == 0)
    def _():
        padded[0, 8 : 8 + cols, :] = top[...]

    @pl.when(step > 0)
    def _():
        padded[0, 8 : 8 + cols, :] = before_ref[0]

    @pl.when(step == last)
    def _():
        padded[count + 1, 8 : 8 + cols, :] = bottom[...]

    @pl.when(step < last)
    def _():
        padded[count + 1, 8 : 8 + cols, :] = after_ref[0]

    for k in range(count + 2):
        padded[k, 7:8, :] = left[pl.ds(step * count + k, 1), :]
        padded[k, 8 + cols : 9 + cols, :] = right[pl.ds(step * count + k, 1), :]


def project_body(
    hidden_ref, before_ref, after_ref, top_ref, bottom_ref, left_ref, right_ref, field_ref,
    expand_ref, depth_ref, weight_ref, mixed_ref, depth_out_ref,
    padded, top, bottom, left, right,
):
    step = pl.program_id(0)
    last = pl.num_programs(0) - 1

    @pl.when(step == 0)
    def _():
        weight = split(expand_ref[...])
        for source, target in (
            (top_ref, top), (bottom_ref, bottom), (left_ref, left), (right_ref, right)
        ):
            target[...] = gelu(dot3(normalize(source[...])[0], weight, NN))

    fill_padded(padded, step, last, hidden_ref, before_ref, after_ref, top, bottom, left, right)
    count, cols, wide = hidden_ref.shape
    for i in range(count):
        for lane in range(0, wide, 128):
            lanes = slice(lane, lane + 128)
            total = None
            for p in range(3):
                for q in range(3):
                    term = padded[i + p, 7 + q : 7 + q + cols, lanes] * depth_ref[3 * p + q : 3 * p + q + 1, lanes]
                    total = term if total is None else total + term
            depth_out_ref[i, :, lanes] = total
    activated = gelu(depth_out_ref[...].reshape(count * cols, wide))
    mixed = dot3(activated, weight_ref[...], NN) + field_ref[...].reshape(count * cols, -1)
    for i in range(count):
        for k in range(cols // 8):
            start = i * cols + 8 * k
            mixed_ref[0, k, i] = mixed[start : start + 8]


def neighbours(count, cols, wide, total):
    return [
        pl.BlockSpec((count, cols, wide), lambda i: (i, 0, 0)),
        pl.BlockSpec((1, cols, wide), lambda i: (jnp.maximum(count * i - 1, 0), 0, 0)),
        pl.BlockSpec((1, cols, wide), lambda i: (jnp.minimum(count * i + count, total - 1), 0, 0)),
    ]


def project(hidden, halo, field, expand_weight, depth_weight, weight):
    tile_rows, tile_cols, channels = field.shape
    wide = hidden.shape[2]
    count = tile_rows // GRID
    edge = tile_rows + 2
    return call(
        project_body,
        (GRID,),
        neighbours(count, tile_cols, wide, tile_rows)
        + [whole(tile_cols, channels)] * 2
        + [whole(edge, channels)] * 2
        + [rows(count, tile_cols, channels), whole(channels, wide), whole(9, wide), whole(wide, channels)],
        [rows(1, tile_cols // 8, count, 8, channels), rows(count, tile_cols, wide)],
        [shape(GRID, tile_cols // 8, count, 8, channels), shape(tile_rows, tile_cols, wide)],
        scratch=[
            pltpu.VMEM((count + 2, tile_cols + 16, wide), F32),
            pltpu.VMEM((tile_cols, wide), F32),
            pltpu.VMEM((tile_cols, wide), F32),
            pltpu.VMEM((edge, wide), F32),
            pltpu.VMEM((edge, wide), F32),
        ],
        flops=6 * tile_rows * tile_cols * channels * wide,
        bytes_accessed=4 * tile_rows * tile_cols * (3 * wide + 2 * channels),
    )(hidden, hidden, hidden, *halo, field, expand_weight, depth_weight, weight)


def attend_body(
    mixed_ref, cot_ref, qkv_ref, out_ref, bias_ref,
    attended_ref, grad_ref, grad_qkv_ref, grad_out_ref, grad_bias_ref,
    query_ref, key_ref, value_ref, delta_ref, mixture_ref, grad_query_ref, grad_key_ref, grad_value_ref,
    bias_total,
):
    tokens, channels = mixed_ref.shape
    places = bias_ref.shape[0]
    groups = tokens // places
    head = channels // HEADS
    scale = head ** (-0.5)
    step = 256

    def prepare(i, carry):
        here = pl.ds(pl.multiple_of(i * step, step), step)
        normed, _ = normalize(mixed_ref[here, :])
        packed = dot3(normed, qkv_ref[...], NN)
        query_ref[here, :] = packed[:, :channels] * scale
        key_ref[here, :] = packed[:, channels : 2 * channels]
        value_ref[here, :] = packed[:, 2 * channels :]
        delta_ref[here, :] = dot3(cot_ref[here, :], out_ref[...], NT)
        return carry

    lax.fori_loop(0, tokens // step, prepare, 0)
    bias_total[...] = jnp.zeros_like(bias_total)

    head_of = lax.broadcasted_iota(jnp.int32, (places, channels), 1) // head

    def spread(values):
        return jnp.concatenate(
            [jnp.where(head_of == h, values, 0.0).astype(BF16) for h in range(HEADS)], axis=0
        )

    def spread_split(values):
        high, low = split(values)
        return spread(high.astype(F32)), spread(low.astype(F32))

    def gather_heads(wide):
        total = jnp.where(head_of == 0, wide[:places], 0.0)
        for h in range(1, HEADS):
            total = total + jnp.where(head_of == h, wide[h * places : (h + 1) * places], 0.0)
        return total

    def cross(a, b):
        a_high, a_low = a
        b_high, b_low = b
        return dot(
            jnp.concatenate([a_high, a_low, a_high], axis=0),
            jnp.concatenate([b_high, b_high, b_low], axis=0),
            TN,
        )

    def one_group(g, carry):
        here = pl.ds(g, places, stride=groups)
        query = spread_split(query_ref[here, :])
        delta = spread_split(delta_ref[here, :])
        key = split(key_ref[here, :])
        value = split(value_ref[here, :])
        scores = dot3(key, query, NT) + bias_ref[...]
        powers = jnp.exp(scores - jnp.max(scores, axis=0, keepdims=True))
        weights = powers * (1.0 / jnp.sum(powers, axis=0, keepdims=True))
        weights_split = split(weights)
        mixture_ref[here, :] = gather_heads(cross(weights_split, value))
        grad_weights = dot3(value, delta, NT)
        along = jnp.sum(weights * grad_weights, axis=0, keepdims=True)
        grad_scores = weights * (grad_weights - along)
        bias_total[...] += grad_scores
        grad_split = split(grad_scores)
        grad_value_ref[here, :] = dot3(weights_split, delta, NN)
        grad_key_ref[here, :] = dot3(grad_split, query, NN)
        grad_query_ref[here, :] = gather_heads(cross(grad_split, key)) * scale
        return carry

    lax.fori_loop(0, groups, one_group, 0)

    grad_qkv_ref[...] = jnp.zeros_like(grad_qkv_ref)
    grad_out_ref[...] = jnp.zeros_like(grad_out_ref)
    half = bias_total.shape[1] // 2
    grad_bias_ref[:places, :] = bias_total[:, :half]
    grad_bias_ref[places:, :] = bias_total[:, half:]

    def finish(i, carry):
        here = pl.ds(pl.multiple_of(i * step, step), step)
        mixture = split(mixture_ref[here, :])
        attended_ref[here, :] = dot3(mixture, out_ref[...], NN)
        grad_out_ref[...] += dot3(mixture, cot_ref[here, :], TN)
        normed, spread_scale = normalize(mixed_ref[here, :])
        normed_split = split(normed)
        grad_normed = jnp.zeros((step, channels), F32)
        for k, ref in enumerate((grad_query_ref, grad_key_ref, grad_value_ref)):
            lanes = slice(k * channels, (k + 1) * channels)
            grad = split(ref[here, :])
            grad_qkv_ref[:, lanes] += dot3(normed_split, grad, TN)
            grad_normed = grad_normed + dot3(grad, qkv_ref[:, lanes], NT)
        grad_ref[here, :] = normalize_back(grad_normed, normed, spread_scale)
        return carry

    lax.fori_loop(0, tokens // step, finish, 0)


def attend(mixed, cot, qkv_weight, out_weight, bias):
    tokens, channels = mixed.shape
    places = bias.shape[0]
    return call(
        attend_body,
        (),
        [pl.BlockSpec(memory_space=pltpu.VMEM)] * 5,
        [pl.BlockSpec(memory_space=pltpu.VMEM)] * 5,
        [
            shape(tokens, channels), shape(tokens, channels), shape(channels, 3 * channels),
            shape(channels, channels), shape(2 * places, bias.shape[1] // 2),
        ],
        scratch=[pltpu.VMEM((tokens, channels), F32)] * 8 + [pltpu.VMEM(bias.shape, F32)],
        flops=6 * tokens * channels * (12 * channels + 6 * places),
        bytes_accessed=16 * tokens * channels,
    )(mixed, cot, qkv_weight, out_weight, bias)


def project_back_body(back_ref, cot_ref, depth_out_ref, weight_ref, grad_mixed_ref, grad_depth_ref):
    count, cols, wide = depth_out_ref.shape
    for i in range(count):
        for k in range(cols // 8):
            here = slice(8 * k, 8 * k + 8)
            grad_mixed_ref[i, here, :] = cot_ref[i, here, :] + back_ref[0, k, i]
    grad_mixed = grad_mixed_ref[...].reshape(count * cols, -1)
    depth_out = depth_out_ref[...].reshape(count * cols, wide)
    grad = dot3(grad_mixed, weight_ref[...], NT) * gelu_slope(depth_out, gate(depth_out))
    grad_depth_ref[...] = grad.reshape(count, cols, wide)


def project_back(back, cot, depth_out, weight):
    tile_rows, tile_cols, channels = cot.shape
    wide = depth_out.shape[2]
    count = tile_rows // GRID
    return call(
        project_back_body,
        (GRID,),
        [
            rows(1, tile_cols // 8, count, 8, channels), rows(count, tile_cols, channels),
            rows(count, tile_cols, wide), whole(wide, channels),
        ],
        [rows(count, tile_cols, channels), rows(count, tile_cols, wide)],
        [shape(tile_rows, tile_cols, channels), shape(tile_rows, tile_cols, wide)],
        flops=6 * tile_rows * tile_cols * channels * wide,
        bytes_accessed=4 * tile_rows * tile_cols * (2 * wide + 3 * channels),
    )(back, cot, depth_out, weight)


def project_grad_body(grad_mixed_ref, depth_out_ref, total_ref):
    @pl.when(pl.program_id(0) == 0)
    def _():
        total_ref[...] = jnp.zeros_like(total_ref)

    total_ref[...] += dot3(grad_mixed_ref[...], gelu(depth_out_ref[...]), TN)


def project_grad(grad_mixed, depth_out):
    tokens, channels = grad_mixed.shape
    wide = depth_out.shape[1]
    step = 256
    return call(
        project_grad_body,
        (tokens // step,),
        [rows(step, channels), rows(step, wide)],
        whole(channels, wide),
        shape(channels, wide),
        flops=6 * tokens * channels * wide,
        bytes_accessed=4 * tokens * (wide + channels),
    )(grad_mixed, depth_out)


def expand_back_body(
    grad_ref, before_ref, after_ref, top, bottom, left, right, pre_ref, field_ref, grad_mixed_ref,
    expand_ref, depth_ref, grad_field_ref, grad_expand_ref, grad_depth_ref, padded, grad_pre,
):
    step = pl.program_id(0)
    last = pl.num_programs(0) - 1

    @pl.when(step == 0)
    def _():
        grad_expand_ref[...] = jnp.zeros_like(grad_expand_ref)
        grad_depth_ref[...] = jnp.zeros_like(grad_depth_ref)

    fill_padded(padded, step, last, grad_ref, before_ref, after_ref, top, bottom, left, right)
    count, cols, wide = grad_ref.shape
    for lane in range(0, wide, 128):
        lanes = slice(lane, lane + 128)
        taps = [None] * 9
        for i in range(count):
            pre = pre_ref[i, :, lanes]
            gated = gate(pre)
            hidden = pre * gated
            total = None
            for tap in range(9):
                p, q = divmod(tap, 3)
                window = padded[i + 2 - p, 9 - q : 9 - q + cols, lanes]
                term = window * depth_ref[tap : tap + 1, lanes]
                total = term if total is None else total + term
                part = jnp.sum((window * hidden).reshape(cols // 8, 8, 128), axis=0)
                taps[tap] = part if taps[tap] is None else taps[tap] + part
            grad_pre[i * cols : (i + 1) * cols, lanes] = total * gelu_slope(pre, gated)
        for tap in range(9):
            grad_depth_ref[tap : tap + 1, lanes] += jnp.sum(taps[tap], axis=0, keepdims=True)
    field = field_ref[...].reshape(count * cols, -1)
    normed, scale = normalize(field)
    grad = split(grad_pre[...])
    grad_expand_ref[...] += dot3(normed, grad, TN)
    grad_normed = dot3(grad, expand_ref[...], NT)
    grad_field = normalize_back(grad_normed, normed, scale)
    grad_field_ref[...] = grad_mixed_ref[...] + grad_field.reshape(grad_mixed_ref.shape)


def expand_back(grad_depth_out, halo, pre, field, grad_mixed, expand_weight, depth_weight):
    tile_rows, tile_cols, channels = field.shape
    wide = pre.shape[2]
    count = tile_rows // GRID
    edge = tile_rows + 2
    return call(
        expand_back_body,
        (GRID,),
        neighbours(count, tile_cols, wide, tile_rows)
        + [whole(tile_cols, wide)] * 2
        + [whole(edge, wide)] * 2
        + [
            rows(count, tile_cols, wide), rows(count, tile_cols, channels), rows(count, tile_cols, channels),
            whole(channels, wide), whole(9, wide),
        ],
        [rows(count, tile_cols, channels), whole(channels, wide), whole(16, wide)],
        [shape(tile_rows, tile_cols, channels), shape(channels, wide), shape(16, wide)],
        scratch=[
            pltpu.VMEM((count + 2, tile_cols + 16, wide), F32),
            pltpu.VMEM((count * tile_cols, wide), F32),
        ],
        flops=12 * tile_rows * tile_cols * channels * wide,
        bytes_accessed=4 * tile_rows * tile_cols * (2 * wide + 3 * channels),
    )(grad_depth_out, grad_depth_out, grad_depth_out, *halo, pre, field, grad_mixed, expand_weight, depth_weight)


def shift(values, axes, count, by):
    ends = [(i, i + 1) for i in range(count - 1)]
    return lax.ppermute(values, axes, ends if by > 0 else [(j, i) for i, j in ends])


def surround(tile, row_count, col_count):
    top = shift(tile[-1], "row", row_count, 1)
    bottom = shift(tile[0], "row", row_count, -1)

    def column(j):
        return jnp.concatenate([top[j][None], tile[:, j], bottom[j][None]], axis=0)

    left = shift(column(-1), COLS, col_count, 1)
    right = shift(column(0), COLS, col_count, -1)
    return top, bottom, left, right


def swap(blocks):
    flat = blocks.reshape((-1,) + blocks.shape[-3:])
    return lax.all_to_all(flat, PAIRS, 0, 0, tiled=True)


def reduce_all(matrices, slots, devices):
    lanes = matrices[0].shape[-1]
    buffer = jnp.stack(matrices, axis=1)
    buffer = jnp.pad(buffer, ((0, 0), (0, slots - len(matrices)), (0, 0)))
    arrived = lax.all_to_all(buffer, ALL, 0, 0, tiled=True)
    total = jnp.sum(arrived, axis=0, keepdims=True)
    spread = jnp.broadcast_to(total, (devices, slots, lanes))
    return lax.all_to_all(spread, ALL, 0, 0, tiled=True)


def on_device(
    sizes, field, expand_weight, depth_weight, project_weight, qkv_weight, out_weight, pos_bias, cotangent
):
    row_count, col_count = sizes
    tile_rows, tile_cols, channels = field.shape
    wide = expand_weight.shape[1]
    tokens = tile_rows * tile_cols
    places = GRID * GRID
    span = tile_rows // GRID
    blocks = (GRID, tile_cols // 8, span, 8, channels)

    cot_grid = swap(
        cotangent.reshape(GRID, span, tile_cols // 8, 8, channels).transpose(0, 2, 1, 3, 4)
    ).reshape(tokens, channels)
    halo = surround(field, row_count, col_count)
    pre, hidden = expand(field.reshape(tokens, channels), expand_weight)
    pre = pre.reshape(tile_rows, tile_cols, wide)
    hidden = hidden.reshape(tile_rows, tile_cols, wide)
    mixed, depth_out = project(hidden, halo, field, expand_weight, depth_weight, project_weight)
    mixed_grid = swap(mixed).reshape(tokens, channels)
    bias = pos_bias.transpose(2, 0, 1).reshape(places, HEADS * places)
    attended, grad_grid, grad_qkv, grad_out, grad_bias = attend(
        mixed_grid, cot_grid, qkv_weight, out_weight, bias
    )
    back = swap(grad_grid.reshape(blocks)).reshape(blocks)
    grad_mixed, grad_depth_out = project_back(back, cotangent, depth_out, project_weight)
    grad_halo = surround(grad_depth_out, row_count, col_count)
    grad_project = project_grad(
        grad_mixed.reshape(tokens, channels), depth_out.reshape(tokens, wide)
    )
    placed = swap(attended.reshape(blocks)).reshape(blocks)
    block_out = (mixed + placed).transpose(0, 2, 1, 3, 4).reshape(field.shape)
    grad_field, grad_expand, grad_depth = expand_back(
        grad_depth_out, grad_halo, pre, field, grad_mixed, expand_weight, depth_weight
    )

    def parts(matrix):
        return [matrix[:, k : k + channels] for k in range(0, matrix.shape[1], channels)]

    depth_rows = jnp.pad(
        jnp.concatenate(parts(grad_depth[:9]), axis=0), ((0, channels - 9 * wide // channels), (0, 0))
    )
    total = reduce_all(
        parts(grad_expand) + parts(grad_project) + parts(grad_qkv) + [grad_out, grad_bias, depth_rows],
        16,
        channels,
    )
    grad_expand = total[:, 0:4].reshape(channels, wide)
    grad_project = total[:, 4:8].transpose(1, 2, 0).reshape(wide, channels)
    grad_qkv = total[:, 8:11].reshape(channels, 3 * channels)
    grad_out = total[:, 11]
    grad_bias = total[:, 12].reshape(2, places, 2, places).transpose(0, 2, 3, 1).reshape(pos_bias.shape)
    grad_depth = total[: 9 * wide // channels, 13].reshape(4, 9, channels).transpose(1, 0, 2).reshape(9, wide)
    return (
        block_out,
        grad_field,
        grad_expand,
        grad_depth,
        grad_project,
        grad_qkv,
        grad_out,
        grad_bias,
    )


def solution(mesh):
    row_count, col_count = mesh.devices.shape
    split_mesh = Mesh(mesh.devices.reshape(row_count, col_count // 2, 2), ALL)
    tile = P("row", COLS, None)
    return jax.shard_map(
        functools.partial(on_device, (row_count, col_count)),
        mesh=split_mesh,
        in_specs=(tile, P(), P(), P(), P(), P(), P(), tile),
        out_specs=(tile, tile, P(), P(), P(), P(), P(), P()),
        check_vma=False,
    )
```

time: 562 us -> 295 us (0.52)
  matrix products: 124 us -> 0 us
  waiting for transfers between devices: 164 us -> 53.5 us
  Pallas kernels: 0 us -> 102 us
  other arithmetic: 52.8 us -> 0.41 us
  local copies, waits for them, and re-layouts: 67.1 us -> 24.9 us
  blocking collectives: 66.4 us -> 49.6 us
  between operations: 15.3 us -> 1.12 us
    psum x1 -> x0, waiting for transfers between devices: 143 us -> none  [on_device(): lax.psum((grad_expand, grad_depth, grad_project, grad_qkv, grad_out, grad...]
    dot_general x18 -> x0, matrix products: 124 us -> none  [the longest x3 37.6 us: project_part(): jnp.einsum('ijf,fc->ijc', jax.nn.gelu(depth_out), project_weight, precisi...]
    pallas_call x0 -> x6, Pallas kernels: none -> 102 us  [the longest x1 42.2 us: attend(): call(attend_body, (), [pl.BlockSpec(memory_space=pltpu.VMEM)] * 5, [pl.Bl...]
    psum x1 -> x0, blocking collectives: 66.4 us -> none  [on_device(): lax.psum((grad_expand, grad_depth, grad_project, grad_qkv, grad_out, grad...]
    all_to_all x0 -> x2, blocking collectives: none -> 49.6 us  [the longest x1 28 us: reduce_all(): arrived = lax.all_to_all(buffer, ALL, 0, 0, tiled=True)]
    all_to_all x4, waiting for transfers between devices: 12.7 us -> 50.2 us  [the longest x3 32.1 us: swap(): return lax.all_to_all(flat, PAIRS, 0, 0, tiled=True)]
    add x5 -> x0, other arithmetic: 19.3 us -> none  [the longest x1 13.9 us: depthwise(): total + padded[row_shift:row_shift + out_rows, col_shift:col_shift + out_...]
    reduce_sum x8 -> x1, other arithmetic: 15.4 us -> 0.14 us  [reduce_all(): total = jnp.sum(arrived, axis=0, keepdims=True)]
  transfers between devices with their start and end apart: 13 -> 12, of which waited for: 5 -> 5; matrix products, arithmetic and copies ran while one was open for 19% -> 2% of each run, Pallas kernels for 0% -> 10%
where the time goes in v1:
time: 295 us; the launch traced here: 293 us
  Pallas kernels  102 us (35%)
  starting transfers between devices  61.5 us (21%)
  waiting for transfers between devices  53.5 us (18%)
  blocking collectives  49.6 us (17%)
  local copies, waits for them, and re-layouts  24.9 us (8%)
    pallas_call x1, Pallas kernels, attend(): call(attend_body, (), [pl.BlockSpec(memory_space=pltpu.VMEM)] * 5, [pl.Bl...  42.2 us
    all_to_all x3, waiting for transfers between devices, swap(): return lax.all_to_all(flat, PAIRS, 0, 0, tiled=True)  32.1 us
    ppermute x8, starting transfers between devices, shift(): lax.ppermute(values, axes, ends if by > 0 else [(j, i) for i, j in ends])  28.6 us
    all_to_all x1, blocking collectives, reduce_all(): arrived = lax.all_to_all(buffer, ALL, 0, 0, tiled=True)  28 us
    all_to_all x3, starting transfers between devices, swap(): return lax.all_to_all(flat, PAIRS, 0, 0, tiled=True)  26.4 us
    pallas_call x1, Pallas kernels, expand_back(): call(expand_back_body, (GRID,), neighbours(count, tile_cols, wide, tile_r...  22.2 us
    all_to_all x1, blocking collectives, swap(): return lax.all_to_all(flat, PAIRS, 0, 0, tiled=True)  21.6 us
    all_to_all x1, waiting for transfers between devices, reduce_all(): return lax.all_to_all(spread, ALL, 0, 0, tiled=True)  18.1 us
  transfers between devices with their start and end apart: 12, of which 5 were waited for; matrix products, arithmetic and copies ran while one was open for 2% of the time, Pallas kernels for 10%

profile of v1, /device:TPU:1, one launch (start us, length us, event | category | flops | bytes accessed | tf_op | source)
XLA Modules:
  0.0 292.7 jit_solution(6078846805979403874)
XLA Ops:
  2.7 6.3 %collective-permute-start = (f32[64,128]{1,0:T(8,128)S(1)}, f32[64,128]{1,0:T(8,128)S(1)}, u32[]{:S(2)}, u32[]{:S(2)}) collective-permute-start(f32[64,128]{1,0:T(8,128)S(1)} %get-tuple-element.71), channel_id=1, source_target_pairs={{0,16},{16,32},{32,48},{48,64},{64,80},{80,96},{96,112},{1,17},{17... | collective-permute-start | bytes 98312 | tf_op jit(solution)/shard_map/ppermute | solution.py:447
  9.0 2.3 copy.51
  11.3 12.1 %all-to-all-start.1 = ((f32[64,4,8,128]{3,2,1,0:T(8,128)}), f32[64,4,8,128]{3,2,1,0:T(8,128)S(1)}, u32[]{:S(2)}, u32[]{:S(2)}) async-start(f32[64,4,8,128]{3,2,1,0:T(8,128)} %bitcast.10), calls=%async_computation.1 | async-start | bytes 2097152 | tf_op jit(solution)/shard_map/all_to_all | solution.py:464
  24.5 4.6 %collective-permute-start.2 = (f32[34,128]{1,0:T(8,128)S(1)}, f32[34,128]{1,0:T(8,128)S(1)}, u32[]{:S(2)}, u32[]{:S(2)}) collective-permute-start(f32[34,128]{1,0:T(8,128)S(1)} %pad_maximum_fusion.2), channel_id=1, source_target_pairs={{0,1},{1,2},{2,3},{3,4},{4,5},{5,6},{6,7},{7,8},{8,9},{9,10},{10,1... | collective-permute-start | bytes 52232 | tf_op jit(solution)/shard_map/ppermute | solution.py:447
  29.1 1.9 collective-permute-start.3
  31.0 8.6 %shard_map.143 = (f32[2048,512]{1,0:T(8,128)}, f32[2048,512]{1,0:T(8,128)}) custom-call(f32[2048,128]{1,0:T(8,128)} %bitcast.94, f32[128,512]{1,0:T(8,128)} %expand_ref.3), custom_call_target="tpu_custom_call" | custom-call | flops 805306368 | bytes 9437184 | tf_op jit(solution)/shard_map/pallas_call | solution.py:102
  40.3 12.3 %shard_map.144 = (f32[8,8,4,8,128]{4,3,2,1,0:T(8,128)}, f32[32,64,512]{2,1,0:T(8,128)}) custom-call(f32[32,64,512]{2,1,0:T(8,128)} %bitcast.90, f32[32,64,512]{2,1,0:T(8,128)} %bitcast.91, f32[32,64,512]{2,1,0:T(8,128)} %bitcast.92, f32[64,128]{1,0:T(8,128)} %copy-done.13, f32[64,128]{1,0:T(8,128)} %copy-done.12, f32[34,128]{1,0:T(8,128)} %copy-done.14, ...), custom_call_target="tpu_custom_call" | custom-call | flops 805306368 | bytes 14680064 | tf_op jit(solution)/shard_map/pallas_call | solution.py:186
  52.6 9.7 %all-to-all-start = ((f32[64,4,8,128]{3,2,1,0:T(8,128)}), f32[64,4,8,128]{3,2,1,0:T(8,128)S(1)}, u32[]{:S(2)}, u32[]{:S(2)}) async-start(f32[64,4,8,128]{3,2,1,0:T(8,128)} %bitcast.97), calls=%async_computation | async-start | bytes 2097152 | tf_op jit(solution)/shard_map/all_to_all | solution.py:464
  63.0 15.8 %all-to-all-done = f32[64,4,8,128]{3,2,1,0:T(8,128)S(1)} async-done(((f32[64,4,8,128]{3,2,1,0:T(8,128)}), f32[64,4,8,128]{3,2,1,0:T(8,128)S(1)}, u32[]{:S(2)}, u32[]{:S(2)}) %all-to-all-start) | async-done | bytes 1048608 | tf_op jit(solution)/shard_map/all_to_all | solution.py:464
  79.8 42.2 %shard_map.145 = (f32[2048,128]{1,0:T(8,128)}, f32[2048,128]{1,0:T(8,128)}, f32[128,384]{1,0:T(8,128)}, f32[128,128]{1,0:T(8,128)}, f32[128,128]{1,0:T(8,128)}) custom-call(f32[2048,128]{1,0:T(8,128)} %bitcast.104, f32[2048,128]{1,0:T(8,128)} %bitcast.102, f32[128,384]{1,0:T(8,128)} %qkv_ref.1, f32[128,128]{1,0:T(8,128)} %out_ref.1, f32[64,256]{1,0:T(8,128)} %copy.64.bias_ref), custom_call_target="tpu_custom_call" | custom-call | flops 3019898880 | bytes 4194304 | tf_op jit(solution)/shard_map/pallas_call | solution.py:310
  122.0 21.6 %all_to_all.30 = f32[64,4,8,128]{3,2,1,0:T(8,128)} all-to-all(f32[64,4,8,128]{3,2,1,0:T(8,128)} %bitcast.105), channel_id=1, replica_groups=mesh['row'=8,'ch'=8,'core'=2] {'row','ch'}, dimensions={0} | all-to-all | bytes 2097152 | tf_op jit(solution)/shard_map/all_to_all | solution.py:464
  143.6 8.9 %shard_map.146 = (f32[32,64,128]{2,1,0:T(8,128)}, f32[32,64,512]{2,1,0:T(8,128)}) custom-call(f32[8,8,4,8,128]{4,3,2,1,0:T(8,128)} %bitcast.99, f32[32,64,128]{2,1,0:T(8,128)} %cot_ref.1, f32[32,64,512]{2,1,0:T(8,128)} %get-tuple-element.26.depth_out_ref, f32[512,128]{1,0:T(8,128)} %weight_ref.5), custom_call_target="tpu_custom_call" | custom-call | flops 805306368 | bytes 11534336 | tf_op jit(solution)/shard_map/pallas_call | solution.py:341
  153.5 4.6 %copy.54 = f32[32,64,512]{2,0,1:T(8,128)S(1)} copy(f32[32,64,512]{2,1,0:T(8,128)} %get-tuple-element.27.grad_ref.before_ref.after_ref) | data formatting | bytes 8388608 | tf_op jit(solution)/shard_map/pallas_call | solution.py:341
  159.4 5.5 %collective-permute-start.4 = (f32[64,512]{1,0:T(8,128)S(1)}, f32[64,512]{1,0:T(8,128)S(1)}, u32[]{:S(2)}, u32[]{:S(2)}) collective-permute-start(f32[64,512]{1,0:T(8,128)S(1)} %get-tuple-element.63), channel_id=1, source_target_pairs={{0,16},{16,32},{32,48},{48,64},{64,80},{80,96},{96,112},{1,17},{17... | collective-permute-start | bytes 393224 | tf_op jit(solution)/shard_map/ppermute | solution.py:447
  165.4 2.9 collective-permute-done.4.top
  168.3 5.6 %collective-permute-start.6 = (f32[34,512]{1,0:T(8,128)S(1)}, f32[34,512]{1,0:T(8,128)S(1)}, u32[]{:S(2)}, u32[]{:S(2)}) collective-permute-start(f32[34,512]{1,0:T(8,128)S(1)} %pad_maximum_fusion), channel_id=1, source_target_pairs={{0,1},{1,2},{2,3},{3,4},{4,5},{5,6},{6,7},{7,8},{8,9},{9,10},{10,1... | collective-permute-start | bytes 208904 | tf_op jit(solution)/shard_map/ppermute | solution.py:447
  173.9 2.1 collective-permute-start.7
  176.0 7.5 %shard_map.148 = f32[128,512]{1,0:T(8,128)} custom-call(f32[2048,128]{1,0:T(8,128)} %bitcast.100, f32[2048,512]{1,0:T(8,128)} %bitcast.93), custom_call_target="tpu_custom_call" | custom-call | flops 805306368 | bytes 5242880 | tf_op jit(solution)/shard_map/pallas_call | solution.py:367
  184.3 22.2 %shard_map.147 = (f32[32,64,128]{2,1,0:T(8,128)}, f32[128,512]{1,0:T(8,128)}, f32[16,512]{1,0:T(8,128)}) custom-call(f32[32,64,512]{2,1,0:T(8,128)} %get-tuple-element.27.grad_ref.before_ref.after_ref, f32[32,64,512]{2,1,0:T(8,128)} %get-tuple-element.27.grad_ref.before_ref.after_ref, f32[32,64,512]{2,1,0:T(8,128)} %get-tuple-element.27.grad_ref.before_ref.after_ref, ...), custom_call_target="tpu_custom_call" | custom-call | flops 1610612736 | bytes 11534336 | tf_op jit(solution)/shard_map/pallas_call | solution.py:424
  211.4 28.0 %all_to_all.31 = f32[128,16,128]{2,1,0:T(8,128)S(1)} all-to-all(f32[128,16,128]{2,1,0:T(8,128)S(1)} %pad.9.clone), channel_id=1, replica_groups=mesh['row'=8,'ch'=8,'core'=2] {'row','ch','core'}, dimensions={0} | all-to-all | bytes 2097152 | tf_op jit(solution)/shard_map/all_to_all | solution.py:471
  239.4 4.7 %all-to-all-start.2 = ((f32[64,4,8,128]{3,2,1,0:T(8,128)}), f32[64,4,8,128]{3,2,1,0:T(8,128)S(1)}, u32[]{:S(2)}, u32[]{:S(2)}) async-start(f32[64,4,8,128]{3,2,1,0:T(8,128)} %bitcast.101), calls=%async_computation.2 | async-start | bytes 2097152 | tf_op jit(solution)/shard_map/all_to_all | solution.py:464
  244.2 16.4 %all-to-all-done.2 = f32[64,4,8,128]{3,2,1,0:T(8,128)S(1)} async-done(((f32[64,4,8,128]{3,2,1,0:T(8,128)}), f32[64,4,8,128]{3,2,1,0:T(8,128)S(1)}, u32[]{:S(2)}, u32[]{:S(2)}) %all-to-all-start.2) | async-done | bytes 1048608 | tf_op jit(solution)/shard_map/all_to_all | solution.py:464
  261.6 6.4 %all-to-all-start.5 = ((f32[128,16,128]{2,1,0:T(8,128)}), f32[128,16,128]{2,1,0:T(8,128)S(1)}, u32[]{:S(2)}, u32[]{:S(2)}) async-start(f32[128,16,128]{2,1,0:T(8,128)} %broadcast_in_dim.2), calls=%async_computation.5 | async-start | bytes 2097152 | tf_op jit(solution)/shard_map/all_to_all | solution.py:474
  269.4 18.1 %all-to-all-done.5 = f32[128,16,128]{2,1,0:T(8,128)S(1)} async-done(((f32[128,16,128]{2,1,0:T(8,128)}), f32[128,16,128]{2,1,0:T(8,128)S(1)}, u32[]{:S(2)}, u32[]{:S(2)}) %all-to-all-start.5) | async-done | bytes 1048608 | tf_op jit(solution)/shard_map/all_to_all | solution.py:474
  (91 shorter events, 21.3 us)
Async XLA Ops:
  1.4 23.0 %collective-permute-start.1 = (f32[64,128]{1,0:T(8,128)S(1)}, f32[64,128]{1,0:T(8,128)S(1)}, u32[]{:S(2)}, u32[]{:S(2)}) collective-permute-start(f32[64,128]{1,0:T(8,128)S(1)} %get-tuple-element.70), channel_id=1, source_target_pairs={{16,0},{32,16},{48,32},{64,48},{80,64},{96,80},{112,96},{17,1},{33... | collective-permute-start | bytes 98312 | tf_op jit(solution)/shard_map/ppermute | solution.py:447
  2.7 21.7 %collective-permute-start = (f32[64,128]{1,0:T(8,128)S(1)}, f32[64,128]{1,0:T(8,128)S(1)}, u32[]{:S(2)}, u32[]{:S(2)}) collective-permute-start(f32[64,128]{1,0:T(8,128)S(1)} %get-tuple-element.71), channel_id=1, source_target_pairs={{0,16},{16,32},{32,48},{48,64},{64,80},{80,96},{96,112},{1,17},{17... | collective-permute-start | bytes 98312 | tf_op jit(solution)/shard_map/ppermute | solution.py:447
  11.3 41.3 %all-to-all-start.1 = ((f32[64,4,8,128]{3,2,1,0:T(8,128)}), f32[64,4,8,128]{3,2,1,0:T(8,128)S(1)}, u32[]{:S(2)}, u32[]{:S(2)}) async-start(f32[64,4,8,128]{3,2,1,0:T(8,128)} %bitcast.10), calls=%async_computation.1 | async-start | bytes 2097152 | tf_op jit(solution)/shard_map/all_to_all | solution.py:464
  24.4 15.2 %copy-start.12 = (f32[64,128]{1,0:T(8,128)}, f32[64,128]{1,0:T(8,128)S(1)}, u32[]{:S(2)}) copy-start(f32[64,128]{1,0:T(8,128)S(1)} %collective-permute-done.1.bottom_ref) | copy-start | bytes 98308
  24.5 15.2 %copy-start.13 = (f32[64,128]{1,0:T(8,128)}, f32[64,128]{1,0:T(8,128)S(1)}, u32[]{:S(2)}) copy-start(f32[64,128]{1,0:T(8,128)S(1)} %collective-permute-done.top_ref) | copy-start | bytes 98308
  24.5 15.1 %collective-permute-start.2 = (f32[34,128]{1,0:T(8,128)S(1)}, f32[34,128]{1,0:T(8,128)S(1)}, u32[]{:S(2)}, u32[]{:S(2)}) collective-permute-start(f32[34,128]{1,0:T(8,128)S(1)} %pad_maximum_fusion.2), channel_id=1, source_target_pairs={{0,1},{1,2},{2,3},{3,4},{4,5},{5,6},{6,7},{7,8},{8,9},{9,10},{10,1... | collective-permute-start | bytes 52232 | tf_op jit(solution)/shard_map/ppermute | solution.py:447
  29.1 10.5 %collective-permute-start.3 = (f32[34,128]{1,0:T(8,128)S(1)}, f32[34,128]{1,0:T(8,128)S(1)}, u32[]{:S(2)}, u32[]{:S(2)}) collective-permute-start(f32[34,128]{1,0:T(8,128)S(1)} %pad_maximum_fusion.3), channel_id=1, source_target_pairs={{1,0},{2,1},{3,2},{4,3},{5,4},{6,5},{7,6},{8,7},{9,8},{10,9},{11,1... | collective-permute-start | bytes 52232 | tf_op jit(solution)/shard_map/ppermute | solution.py:447
  40.3 22.0 %copy-start.7 = (f32[4,64,64]{2,1,0:T(8,128)S(1)}, f32[4,64,64]{2,1,0:T(8,128)}, u32[]{:S(2)}) copy-start(f32[4,64,64]{2,1,0:T(8,128)} %param.14) | copy-start | bytes 196612
  52.6 26.2 %copy-start.1 = (f32[64,4,8,128]{3,2,1,0:T(8,128)}, f32[64,4,8,128]{3,2,1,0:T(8,128)S(1)}, u32[]{:S(2)}) copy-start(f32[64,4,8,128]{3,2,1,0:T(8,128)S(1)} %all-to-all-done.1) | copy-start | bytes 3145732
  52.6 26.2 %all-to-all-start = ((f32[64,4,8,128]{3,2,1,0:T(8,128)}), f32[64,4,8,128]{3,2,1,0:T(8,128)S(1)}, u32[]{:S(2)}, u32[]{:S(2)}) async-start(f32[64,4,8,128]{3,2,1,0:T(8,128)} %bitcast.97), calls=%async_computation | async-start | bytes 2097152 | tf_op jit(solution)/shard_map/all_to_all | solution.py:464
  78.8 1.0 copy-start.2
  158.1 7.2 %collective-permute-start.5 = (f32[64,512]{1,0:T(8,128)S(1)}, f32[64,512]{1,0:T(8,128)S(1)}, u32[]{:S(2)}, u32[]{:S(2)}) collective-permute-start(f32[64,512]{1,0:T(8,128)S(1)} %get-tuple-element.62), channel_id=1, source_target_pairs={{16,0},{32,16},{48,32},{64,48},{80,64},{96,80},{112,96},{17,1},{33... | collective-permute-start | bytes 393224 | tf_op jit(solution)/shard_map/ppermute | solution.py:447
  159.4 8.8 %collective-permute-start.4 = (f32[64,512]{1,0:T(8,128)S(1)}, f32[64,512]{1,0:T(8,128)S(1)}, u32[]{:S(2)}, u32[]{:S(2)}) collective-permute-start(f32[64,512]{1,0:T(8,128)S(1)} %get-tuple-element.63), channel_id=1, source_target_pairs={{0,16},{16,32},{32,48},{48,64},{64,80},{80,96},{96,112},{1,17},{17... | collective-permute-start | bytes 393224 | tf_op jit(solution)/shard_map/ppermute | solution.py:447
  165.4 18.3 %copy-start.5 = (f32[64,512]{1,0:T(8,128)}, f32[64,512]{1,0:T(8,128)S(1)}, u32[]{:S(2)}) copy-start(f32[64,512]{1,0:T(8,128)S(1)} %collective-permute-done.5.bottom) | copy-start | bytes 393220
  168.2 15.4 %copy-start.6 = (f32[64,512]{1,0:T(8,128)}, f32[64,512]{1,0:T(8,128)S(1)}, u32[]{:S(2)}) copy-start(f32[64,512]{1,0:T(8,128)S(1)} %collective-permute-done.4.top) | copy-start | bytes 393220
  168.3 15.3 %collective-permute-start.6 = (f32[34,512]{1,0:T(8,128)S(1)}, f32[34,512]{1,0:T(8,128)S(1)}, u32[]{:S(2)}, u32[]{:S(2)}) collective-permute-start(f32[34,512]{1,0:T(8,128)S(1)} %pad_maximum_fusion), channel_id=1, source_target_pairs={{0,1},{1,2},{2,3},{3,4},{4,5},{5,6},{6,7},{7,8},{8,9},{9,10},{10,1... | collective-permute-start | bytes 208904 | tf_op jit(solution)/shard_map/ppermute | solution.py:447
  173.9 9.7 %collective-permute-start.7 = (f32[34,512]{1,0:T(8,128)S(1)}, f32[34,512]{1,0:T(8,128)S(1)}, u32[]{:S(2)}, u32[]{:S(2)}) collective-permute-start(f32[34,512]{1,0:T(8,128)S(1)} %pad_maximum_fusion.1), channel_id=1, source_target_pairs={{1,0},{2,1},{3,2},{4,3},{5,4},{6,5},{7,6},{8,7},{9,8},{10,9},{11,1... | collective-permute-start | bytes 208904 | tf_op jit(solution)/shard_map/ppermute | solution.py:447
  184.3 26.4 %copy-start.3 = (f32[128,512]{1,0:T(8,128)S(1)}, f32[128,512]{1,0:T(8,128)}, u32[]{:S(2)}) copy-start(f32[128,512]{1,0:T(8,128)} %shard_map.148) | copy-start | bytes 786436
  184.3 26.4 %copy-start.4 = (f32[128,384]{1,0:T(8,128)S(1)}, f32[128,384]{1,0:T(8,128)}, u32[]{:S(2)}) copy-start(f32[128,384]{1,0:T(8,128)} %get-tuple-element.32) | copy-start | bytes 589828
  184.3 26.5 %copy-start.11 = (f32[128,128]{1,0:T(8,128)S(1)}, f32[128,128]{1,0:T(8,128)}, u32[]{:S(2)}) copy-start(f32[128,128]{1,0:T(8,128)} %get-tuple-element.33) | copy-start | bytes 196612
  184.3 26.5 %copy-start.10 = (f32[128,128]{1,0:T(8,128)S(1)}, f32[128,128]{1,0:T(8,128)}, u32[]{:S(2)}) copy-start(f32[128,128]{1,0:T(8,128)} %get-tuple-element.34) | copy-start | bytes 196612
  211.4 56.6 %copy-start = (f32[8,8,4,8,128]{4,3,2,1,0:T(8,128)S(1)}, f32[8,8,4,8,128]{4,3,2,1,0:T(8,128)}, u32[]{:S(2)}) copy-start(f32[8,8,4,8,128]{4,3,2,1,0:T(8,128)} %get-tuple-element.23) | copy-start | bytes 3145732
  239.4 21.2 %all-to-all-start.2 = ((f32[64,4,8,128]{3,2,1,0:T(8,128)}), f32[64,4,8,128]{3,2,1,0:T(8,128)S(1)}, u32[]{:S(2)}, u32[]{:S(2)}) async-start(f32[64,4,8,128]{3,2,1,0:T(8,128)} %bitcast.101), calls=%async_computation.2 | async-start | bytes 2097152 | tf_op jit(solution)/shard_map/all_to_all | solution.py:464
  261.6 25.8 %all-to-all-start.5 = ((f32[128,16,128]{2,1,0:T(8,128)}), f32[128,16,128]{2,1,0:T(8,128)S(1)}, u32[]{:S(2)}, u32[]{:S(2)}) async-start(f32[128,16,128]{2,1,0:T(8,128)} %broadcast_in_dim.2), calls=%async_computation.5 | async-start | bytes 2097152 | tf_op jit(solution)/shard_map/all_to_all | solution.py:474
  (4 other events, 2.5 us)

commit v2 on v1

v2 whole, which is shorter than its diff:
```python
import functools

import jax
import jax.numpy as jnp
from jax import lax
from jax.experimental import pallas as pl
from jax.experimental.pallas import tpu as pltpu
from jax.sharding import Mesh, PartitionSpec as P

GRID = 8
HEADS = 4
ALL = ("row", "ch", "core")
COLS = ("ch", "core")
PAIRS = ("row", "ch")
K0 = 0.7978845608028654
K1 = K0 * 0.044715
F32 = jnp.float32
BF16 = jnp.bfloat16
NN = (((1,), (0,)), ((), ()))
NT = (((1,), (1,)), ((), ()))
TN = (((0,), (0,)), ((), ()))


def split(values):
    high = values.astype(BF16)
    return high, (values - high.astype(F32)).astype(BF16)


def dot(a, b, dims):
    return lax.dot_general(a, b, dims, preferred_element_type=F32)


def dot3(a, b, dims):
    a_high, a_low = a if isinstance(a, tuple) else split(a)
    b_high, b_low = b if isinstance(b, tuple) else split(b)
    (a_axis,), (b_axis,) = dims[0]
    return dot(
        jnp.concatenate([a_high, a_low, a_high], axis=a_axis),
        jnp.concatenate([b_high, b_high, b_low], axis=b_axis),
        dims,
    )


def normalize(values):
    center = values - jnp.mean(values, axis=-1, keepdims=True)
    spread = jnp.mean(center * center, axis=-1, keepdims=True)
    scale = lax.rsqrt(spread + 1e-05)
    return center * scale, scale


def normalize_back(grad, normed, scale):
    grad_mean = jnp.mean(grad, axis=-1, keepdims=True)
    along = jnp.mean(grad * normed, axis=-1, keepdims=True)
    return scale * (grad - grad_mean - normed * along)


def gate(values):
    return 0.5 + 0.5 * jnp.tanh(values * (K0 + K1 * (values * values)))


def gelu(values):
    return values * gate(values)


def gelu_slope(values, gated):
    return gated + 2.0 * values * (gated - gated * gated) * (K0 + (3.0 * K1) * (values * values))


def call(body, grid, in_specs, out_specs, out_shape, scratch=(), flops=0, bytes_accessed=0, limit=56):
    return pl.pallas_call(
        body,
        grid=grid,
        in_specs=in_specs,
        out_specs=out_specs,
        out_shape=out_shape,
        scratch_shapes=list(scratch),
        compiler_params=pltpu.CompilerParams(vmem_limit_bytes=limit * 2**20),
        cost_estimate=pl.CostEstimate(
            flops=flops, bytes_accessed=bytes_accessed, transcendentals=0
        ),
    )


def shape(*dims):
    return jax.ShapeDtypeStruct(dims, F32)


def whole(*dims):
    return pl.BlockSpec(dims, lambda *_: (0,) * len(dims))


def rows(*dims):
    return pl.BlockSpec(dims, lambda i: (i,) + (0,) * (len(dims) - 1))


def load_row(ref, lead, cols):
    return [ref[lead + (pl.ds(k, cols // 8, stride=8),)] for k in range(8)]


def load_rows(ref, cols):
    return jnp.concatenate(
        [part for i in range(ref.shape[0]) for part in load_row(ref, (i,), cols)], axis=0
    )


def fill_row(padded, at, row, left, right):
    cols = row.shape[0]
    padded[at, 8 : 8 + cols, :] = row
    padded[at, 0:1, :] = left
    padded[at, 1:8, :] = row[cols - 8 : cols - 1]
    padded[at, 8 + cols : 15 + cols, :] = row[1:8]
    padded[at, 15 + cols : 16 + cols, :] = right


def forward_body(
    field_ref, late_ref, cot_ref, top_ref, bottom_ref, left_ref, right_ref, expand_ref, depth_ref, weight_ref,
    sent_ref, pre_ref, depth_out_ref, padded, left, right,
):
    step = pl.program_id(0)
    last = pl.num_programs(0) - 1
    count, cols, channels = field_ref.shape
    wide = expand_ref.shape[1]
    total_rows = padded.shape[0] - 2

    @pl.when(step == 0)
    def _():
        weight = split(expand_ref[...])

        def hidden(values):
            return gelu(dot3(normalize(values)[0], weight, NN))

        left[...] = hidden(left_ref[...])
        right[...] = hidden(right_ref[...])
        for at, ref in ((0, top_ref), (total_rows + 1, bottom_ref)):
            row = hidden(jnp.concatenate(load_row(ref, (), cols), axis=0))
            fill_row(padded, at, row, left[at : at + 1, :], right[at : at + 1, :])

    @pl.when(step < last)
    def _():
        normed, _ = normalize(load_rows(field_ref, cols))
        pre = dot3(normed, expand_ref[...], NN)
        pre_ref[...] = pre.reshape(count, cols, wide)
        hidden = gelu(pre)
        for i in range(count):
            at = step * count + i + 1
            row = hidden[i * cols : (i + 1) * cols]
            fill_row(padded, at, row, left[pl.ds(at, 1), :], right[pl.ds(at, 1), :])

    @pl.when(step > 0)
    def _():
        start = (step - 1) * count
        for lane in range(0, wide, 128):
            lanes = slice(lane, lane + 128)
            for i in range(count):
                total = None
                for p in range(3):
                    for q in range(3):
                        term = padded[start + i + p, 8 * q : 8 * q + cols, lanes] * depth_ref[3 * p + q : 3 * p + q + 1, lanes]
                        total = term if total is None else total + term
                depth_out_ref[i, :, lanes] = total
        activated = gelu(depth_out_ref[...].reshape(count * cols, wide))
        mixed = dot3(activated, weight_ref[...], NN) + load_rows(late_ref, cols)
        span = total_rows // GRID
        for i in range(count):
            block, inner = divmod(i, span)
            for k in range(8):
                here = i * cols + k * (cols // 8)
                sent_ref[block, pl.ds(inner * 8 + k, cols // 8, stride=2 * span * 8), :] = mixed[
                    here : here + cols // 8
                ]
            for c in range(cols // 8):
                there = (2 * c + 1) * span * 8 + inner * 8
                sent_ref[block, there : there + 8, :] = cot_ref[i, 8 * c : 8 * c + 8, :]


def forward(field, cot, halo, expand_weight, depth_weight, weight, count=8):
    tile_rows, tile_cols, channels = field.shape
    wide = expand_weight.shape[1]
    span = tile_rows // GRID
    steps = tile_rows // count
    edge = tile_rows + 2

    def early(*dims):
        return pl.BlockSpec(dims, lambda i: (jnp.minimum(i, steps - 1),) + (0,) * (len(dims) - 1))

    def late(*dims):
        return pl.BlockSpec(dims, lambda i: (jnp.maximum(i - 1, 0),) + (0,) * (len(dims) - 1))

    return call(
        forward_body,
        (steps + 1,),
        [early(count, tile_cols, channels), late(count, tile_cols, channels), late(count, tile_cols, channels)]
        + [whole(tile_cols, channels)] * 2
        + [whole(edge, channels)] * 2
        + [whole(channels, wide), whole(9, wide), whole(wide, channels)],
        [
            late(count // span, 2 * span * tile_cols, channels),
            early(count, tile_cols, wide),
            late(count, tile_cols, wide),
        ],
        [
            shape(GRID, 2 * span * tile_cols, channels),
            shape(tile_rows, tile_cols, wide),
            shape(tile_rows, tile_cols, wide),
        ],
        scratch=[
            pltpu.VMEM((edge, tile_cols + 16, wide), F32),
            pltpu.VMEM((edge, wide), F32),
            pltpu.VMEM((edge, wide), F32),
        ],
        flops=12 * tile_rows * tile_cols * channels * wide,
        bytes_accessed=4 * tile_rows * tile_cols * (2 * wide + 5 * channels),
    )(field, field, cot, *halo, expand_weight, depth_weight, weight)


def attend_body(
    came_ref, qkv_ref, out_ref, bias_ref,
    leave_ref, grad_qkv_ref, grad_out_ref, grad_bias_ref,
    packed_ref, delta_ref, mixture_ref, grad_packed_ref, bias_total,
):
    places, both, channels = came_ref.shape
    groups = both // 2
    head = channels // HEADS
    scale = head ** (-0.5)
    step = 8
    rows_in = step * groups
    together = 4

    def chunk(i, which):
        part = came_ref[pl.ds(i * step, step), which * groups : (which + 1) * groups, :]
        return part.reshape(rows_in, channels)

    def prepare(i, carry):
        here = pl.ds(pl.multiple_of(i * rows_in, rows_in), rows_in)
        normed, _ = normalize(chunk(i, 0))
        packed = dot3(normed, qkv_ref[...], NN)
        packed_ref[0, here, :] = packed[:, :channels] * scale
        packed_ref[1, here, :] = packed[:, channels : 2 * channels]
        packed_ref[2, here, :] = packed[:, 2 * channels :]
        delta_ref[here, :] = dot3(chunk(i, 1), out_ref[...], NT)
        return carry

    lax.fori_loop(0, places // step, prepare, 0)
    bias_total[...] = jnp.zeros_like(bias_total)

    head_of = lax.broadcasted_iota(jnp.int32, (places, channels), 1) // head

    def spread(values):
        return jnp.concatenate(
            [jnp.where(head_of == h, values, 0.0).astype(BF16) for h in range(HEADS)], axis=0
        )

    def spread_split(values):
        high, low = split(values)
        return spread(high.astype(F32)), spread(low.astype(F32))

    def gather_heads(wide):
        total = jnp.where(head_of == 0, wide[:places], 0.0)
        for h in range(1, HEADS):
            total = total + jnp.where(head_of == h, wide[h * places : (h + 1) * places], 0.0)
        return total

    def some_groups(i, carry):
        here = [pl.ds(i * together + k, places, stride=groups) for k in range(together)]
        query = [spread_split(packed_ref[0, h, :]) for h in here]
        delta = [spread_split(delta_ref[h, :]) for h in here]
        key = [split(packed_ref[1, h, :]) for h in here]
        value = [split(packed_ref[2, h, :]) for h in here]
        scores = [dot3(a, b, NT) + bias_ref[...] for a, b in zip(key, query)]
        grad_weights = [dot3(a, b, NT) for a, b in zip(value, delta)]
        powers = [jnp.exp(s - jnp.max(s, axis=0, keepdims=True)) for s in scores]
        weights = [p * (1.0 / jnp.sum(p, axis=0, keepdims=True)) for p in powers]
        along = [jnp.sum(w * g, axis=0, keepdims=True) for w, g in zip(weights, grad_weights)]
        grad_scores = [w * (g - a) for w, g, a in zip(weights, grad_weights, along)]
        weights = [split(w) for w in weights]
        grad_split = [split(g) for g in grad_scores]
        mixture = [gather_heads(dot3(w, v, TN)) for w, v in zip(weights, value)]
        grad_value = [dot3(w, d, NN) for w, d in zip(weights, delta)]
        grad_key = [dot3(g, q, NN) for g, q in zip(grad_split, query)]
        grad_query = [gather_heads(dot3(g, k, TN)) * scale for g, k in zip(grad_split, key)]
        for k, h in enumerate(here):
            mixture_ref[h, :] = mixture[k]
            grad_packed_ref[0, h, :] = grad_query[k]
            grad_packed_ref[1, h, :] = grad_key[k]
            grad_packed_ref[2, h, :] = grad_value[k]
        bias_total[...] += functools.reduce(jnp.add, grad_scores)
        return carry

    lax.fori_loop(0, groups // together, some_groups, 0)

    grad_qkv_ref[...] = jnp.zeros_like(grad_qkv_ref)
    grad_out_ref[...] = jnp.zeros_like(grad_out_ref)
    half = bias_total.shape[1] // 2
    grad_bias_ref[:places, :] = bias_total[:, :half]
    grad_bias_ref[places:, :] = bias_total[:, half:]

    def finish(i, carry):
        here = pl.ds(pl.multiple_of(i * rows_in, rows_in), rows_in)
        mixture = split(mixture_ref[here, :])
        normed, spread_scale = normalize(chunk(i, 0))
        grad = split(jnp.concatenate([grad_packed_ref[k, here, :] for k in range(3)], axis=1))
        grad_normed = dot3(grad, qkv_ref[...], NT)
        grad_in = normalize_back(grad_normed, normed, spread_scale)
        attended = dot3(mixture, out_ref[...], NN)
        leave_ref[pl.ds(i * step, step), :groups, :] = grad_in.reshape(step, groups, channels)
        leave_ref[pl.ds(i * step, step), groups:, :] = attended.reshape(step, groups, channels)
        grad_out_ref[...] += dot3(mixture, chunk(i, 1), TN)
        grad_qkv_ref[...] += dot3(normed, grad, TN)
        return carry

    lax.fori_loop(0, places // step, finish, 0)


def attend(came, qkv_weight, out_weight, bias):
    places, both, channels = came.shape
    tokens = places * both // 2
    return call(
        attend_body,
        (),
        [pl.BlockSpec(memory_space=pltpu.VMEM)] * 4,
        [pl.BlockSpec(memory_space=pltpu.VMEM)] * 4,
        [
            shape(places, both, channels), shape(channels, 3 * channels),
            shape(channels, channels), shape(2 * places, bias.shape[1] // 2),
        ],
        scratch=[
            pltpu.VMEM((3, tokens, channels), F32),
            pltpu.VMEM((tokens, channels), F32),
            pltpu.VMEM((tokens, channels), F32),
            pltpu.VMEM((3, tokens, channels), F32),
            pltpu.VMEM(bias.shape, F32),
        ],
        flops=6 * tokens * channels * (12 * channels + 6 * places),
        bytes_accessed=16 * tokens * channels,
    )(came, qkv_weight, out_weight, bias)


def project_back_body(
    came_ref, sent_ref, depth_out_ref, weight_ref,
    block_out_ref, grad_mixed_ref, grad_depth_ref, top_ref, bottom_ref, left_ref, right_ref, total_ref,
):
    step = pl.program_id(0)
    last = pl.num_programs(0) - 1
    count, cols, wide = depth_out_ref.shape
    span = count // came_ref.shape[0]
    piece = span * 8

    @pl.when(step == 0)
    def _():
        total_ref[...] = jnp.zeros_like(total_ref)

    parts = []
    for i in range(count):
        block, inner = divmod(i, span)
        for c in range(cols // 8):
            at = 2 * c * piece + inner * 8
            block_out_ref[i, 8 * c : 8 * c + 8, :] = (
                sent_ref[block, at : at + 8, :] + came_ref[block, at + piece : at + piece + 8, :]
            )
        for k in range(8):
            at = inner * 8 + k
            parts.append(
                came_ref[block, pl.ds(at, cols // 8, stride=2 * piece), :]
                + sent_ref[block, pl.ds(at + piece, cols // 8, stride=2 * piece), :]
            )
    grad_mixed = jnp.concatenate(parts, axis=0)
    grad_mixed_ref[...] = grad_mixed.reshape(grad_mixed_ref.shape)
    mixed_split = split(grad_mixed)
    depth_out = depth_out_ref[...].reshape(count * cols, wide)
    gated = gate(depth_out)
    grad = dot3(mixed_split, weight_ref[...], NT) * gelu_slope(depth_out, gated)
    grad_depth_ref[...] = grad.reshape(count, cols, wide)
    total_ref[...] += dot3(mixed_split, depth_out * gated, TN)
    left_ref[...] = grad_depth_ref[:, 0, :]
    right_ref[...] = grad_depth_ref[:, cols - 1, :]

    @pl.when(step == 0)
    def _():
        top_ref[...] = grad_depth_ref[0]

    @pl.when(step == last)
    def _():
        bottom_ref[...] = grad_depth_ref[count - 1]


def project_back(came, sent, depth_out, weight, count=8):
    tile_rows, tile_cols, wide = depth_out.shape
    channels = weight.shape[1]
    span = tile_rows // GRID
    tile = rows(count, tile_cols, channels)
    return call(
        project_back_body,
        (tile_rows // count,),
        [rows(count // span, 2 * span * tile_cols, channels)] * 2
        + [rows(count, tile_cols, wide), whole(wide, channels)],
        [tile, tile, rows(count, tile_cols, wide)]
        + [whole(tile_cols, wide)] * 2
        + [rows(count, wide)] * 2
        + [whole(channels, wide)],
        [shape(tile_rows, tile_cols, channels)] * 2
        + [shape(tile_rows, tile_cols, wide)]
        + [shape(tile_cols, wide)] * 2
        + [shape(tile_rows, wide)] * 2
        + [shape(channels, wide)],
        flops=12 * tile_rows * tile_cols * channels * wide,
        bytes_accessed=4 * tile_rows * tile_cols * (2 * wide + 6 * channels),
    )(came, sent, depth_out, weight)


def expand_back_body(
    grad_ref, before_ref, after_ref, top, bottom, left, right, pre_ref, field_ref, grad_mixed_ref,
    expand_ref, depth_ref, grad_field_ref, grad_expand_ref, grad_depth_ref, padded, grad_pre,
):
    step = pl.program_id(0)
    last = pl.num_programs(0) - 1
    count, cols, wide = grad_ref.shape

    @pl.when(step == 0)
    def _():
        grad_expand_ref[...] = jnp.zeros_like(grad_expand_ref)
        grad_depth_ref[...] = jnp.zeros_like(grad_depth_ref)

    def fill(at, row):
        edge = pl.ds(step * count + at, 1)
        fill_row(padded, at, row, left[edge, :], right[edge, :])

    fill(0, jnp.where(step == 0, top[...], before_ref[0]))
    fill(count + 1, jnp.where(step == last, bottom[...], after_ref[0]))
    for i in range(count):
        fill(i + 1, grad_ref[i])
    for lane in range(0, wide, 128):
        lanes = slice(lane, lane + 128)
        taps = [None] * 9
        for i in range(count):
            pre = pre_ref[i, :, lanes]
            gated = gate(pre)
            hidden = pre * gated
            total = None
            for tap in range(9):
                p, q = divmod(tap, 3)
                window = padded[i + 2 - p, 8 * (2 - q) : 8 * (2 - q) + cols, lanes]
                term = window * depth_ref[tap : tap + 1, lanes]
                total = term if total is None else total + term
                part = jnp.sum((window * hidden).reshape(cols // 8, 8, 128), axis=0)
                taps[tap] = part if taps[tap] is None else taps[tap] + part
            grad_pre[i * cols : (i + 1) * cols, lanes] = total * gelu_slope(pre, gated)
        for tap in range(9):
            grad_depth_ref[tap : tap + 1, lanes] += jnp.sum(taps[tap], axis=0, keepdims=True)
    normed, scale = normalize(load_rows(field_ref, cols))
    grad = split(grad_pre[...])
    grad_expand_ref[...] += dot3(normed, grad, TN)
    grad_normed = dot3(grad, expand_ref[...], NT)
    grad_field = normalize_back(grad_normed, normed, scale) + grad_mixed_ref[...].reshape(count * cols, -1)
    for i in range(count):
        for k in range(8):
            here = i * cols + k * (cols // 8)
            grad_field_ref[i, pl.ds(k, cols // 8, stride=8), :] = grad_field[here : here + cols // 8]


def expand_back(grad_depth_out, halo, pre, field, grad_mixed, expand_weight, depth_weight, count=8):
    tile_rows, tile_cols, channels = field.shape
    wide = pre.shape[2]
    edge = tile_rows + 2
    return call(
        expand_back_body,
        (tile_rows // count,),
        [
            rows(count, tile_cols, wide),
            pl.BlockSpec((1, tile_cols, wide), lambda i: (jnp.maximum(count * i - 1, 0), 0, 0)),
            pl.BlockSpec((1, tile_cols, wide), lambda i: (jnp.minimum(count * i + count, tile_rows - 1), 0, 0)),
        ]
        + [whole(tile_cols, wide)] * 2
        + [whole(edge, wide)] * 2
        + [
            rows(count, tile_cols, wide), rows(count, tile_cols, channels), rows(count, tile_cols, channels),
            whole(channels, wide), whole(9, wide),
        ],
        [rows(count, tile_cols, channels), whole(channels, wide), whole(16, wide)],
        [shape(tile_rows, tile_cols, channels), shape(channels, wide), shape(16, wide)],
        scratch=[
            pltpu.VMEM((count + 2, tile_cols + 16, wide), F32),
            pltpu.VMEM((count * tile_cols, wide), F32),
        ],
        flops=12 * tile_rows * tile_cols * channels * wide,
        bytes_accessed=4 * tile_rows * tile_cols * (2 * wide + 3 * channels),
    )(grad_depth_out, grad_depth_out, grad_depth_out, *halo, pre, field, grad_mixed, expand_weight, depth_weight)


SLOTS = 16


def pack_body(expand_ref, project_ref, qkv_ref, out_ref, bias_ref, depth_ref, packed_ref):
    size = out_ref.shape[0]
    slot = 0
    for ref in (expand_ref, project_ref, qkv_ref, out_ref, bias_ref):
        for lane in range(0, ref.shape[1], size):
            packed_ref[pl.ds(slot, size, stride=SLOTS), :] = ref[:, lane : lane + size]
            slot += 1
    taps = depth_ref.shape[0]
    empty = jnp.zeros((size, size), F32)
    packed_ref[pl.ds(slot, size, stride=SLOTS), :] = empty
    for k in range(depth_ref.shape[1] // size):
        packed_ref[pl.ds(slot + SLOTS * taps * k, taps, stride=SLOTS), :] = depth_ref[:, k * size : (k + 1) * size]
    for spare in range(slot + 1, SLOTS):
        packed_ref[pl.ds(spare, size, stride=SLOTS), :] = empty


def total_body(came_ref, total_ref):
    total = jnp.sum(came_ref[...], axis=0, keepdims=True)
    total_ref[...] = jnp.broadcast_to(total, total_ref.shape)


def unpack_body(packed_ref, expand_ref, project_ref, qkv_ref, out_ref, bias_ref, depth_ref):
    size = out_ref.shape[0]
    places = bias_ref.shape[1]

    def matrix(slot, count=size, first=0):
        return packed_ref[pl.ds(slot + SLOTS * first, count, stride=SLOTS), :]

    slot = 0
    for k in range(expand_ref.shape[1] // size):
        expand_ref[:, k * size : (k + 1) * size] = matrix(slot)
        slot += 1
    for k in range(project_ref.shape[0] // size):
        project_ref[k * size : (k + 1) * size, :] = matrix(slot).T
        slot += 1
    for k in range(qkv_ref.shape[1] // size):
        qkv_ref[:, k * size : (k + 1) * size] = matrix(slot)
        slot += 1
    out_ref[...] = matrix(slot)
    bias = matrix(slot + 1)
    for h in range(HEADS):
        at, lane = divmod(h, 2)
        bias_ref[h] = bias[at * places : (at + 1) * places, lane * places : (lane + 1) * places].T
    taps = 16
    for k in range(depth_ref.shape[1] // size):
        depth_ref[:, k * size : (k + 1) * size] = matrix(slot + 2, taps, taps * k)[: depth_ref.shape[0]]


def reduce_all(grads, like):
    size = grads[3].shape[0]
    vmem = pl.BlockSpec(memory_space=pltpu.VMEM)
    packed = call(pack_body, (), [vmem] * 6, vmem, shape(size * SLOTS, size))(*grads)
    came = lax.all_to_all(packed.reshape(size, SLOTS, size), ALL, 0, 0, tiled=True)
    total = call(total_body, (), [vmem], vmem, shape(size, SLOTS, size))(came)
    came = lax.all_to_all(total, ALL, 0, 0, tiled=True)
    return call(unpack_body, (), [vmem], [vmem] * 6, [shape(*a.shape) for a in like])(
        came.reshape(size * SLOTS, size)
    )


def shift(values, axes, count, by):
    ends = [(i, i + 1) for i in range(count - 1)]
    return lax.ppermute(values, axes, ends if by > 0 else [(j, i) for i, j in ends])


def surround(first, last, left, right, row_count, col_count):
    top = shift(last, "row", row_count, 1)
    bottom = shift(first, "row", row_count, -1)

    def column(edge, j):
        return jnp.concatenate([top[j : j + 1], edge, bottom[j : j + 1]], axis=0)

    end = first.shape[0] - 1
    return (
        top,
        bottom,
        shift(column(right, end), COLS, col_count, 1),
        shift(column(left, 0), COLS, col_count, -1),
    )


def swap(blocks):
    places = GRID * GRID
    flat = blocks.reshape(places, -1, blocks.shape[-1])
    return lax.all_to_all(flat, PAIRS, 0, 0, tiled=True)


def on_device(
    sizes, field, expand_weight, depth_weight, project_weight, qkv_weight, out_weight, pos_bias, cotangent
):
    places = GRID * GRID
    halo = surround(field[0], field[-1], field[:, 0], field[:, -1], *sizes)
    sent, pre, depth_out = forward(field, cotangent, halo, expand_weight, depth_weight, project_weight)
    bias = pos_bias.transpose(2, 0, 1).reshape(places, HEADS * places)
    leave, grad_qkv, grad_out, grad_bias = attend(swap(sent), qkv_weight, out_weight, bias)
    came = swap(leave).reshape(sent.shape)
    block_out, grad_mixed, grad_depth_out, *edges, grad_project = project_back(
        came, sent, depth_out, project_weight
    )
    halo = surround(*edges, *sizes)
    grad_field, grad_expand, grad_depth = expand_back(
        grad_depth_out, halo, pre, field, grad_mixed, expand_weight, depth_weight
    )
    grad_expand, grad_project, grad_qkv, grad_out, grad_bias, grad_depth = reduce_all(
        (grad_expand, grad_project, grad_qkv, grad_out, grad_bias, grad_depth),
        (expand_weight, project_weight, qkv_weight, out_weight, pos_bias, depth_weight),
    )
    return (
        block_out,
        grad_field,
        grad_expand,
        grad_depth,
        grad_project,
        grad_qkv,
        grad_out,
        grad_bias,
    )


def solution(mesh):
    row_count, col_count = mesh.devices.shape
    split_mesh = Mesh(mesh.devices.reshape(row_count, col_count // 2, 2), ALL)
    tile = P("row", COLS, None)
    return jax.shard_map(
        functools.partial(on_device, (row_count, col_count)),
        mesh=split_mesh,
        in_specs=(tile, P(), P(), P(), P(), P(), P(), tile),
        out_specs=(tile, tile, P(), P(), P(), P(), P(), P()),
        check_vma=False,
    )
```

time: 295 us -> 247 us (0.84)
  blocking collectives: 49.6 us -> 89.2 us
  Pallas kernels: 102 us -> 68.7 us
  starting transfers between devices: 61.5 us -> 39.3 us
  local copies, waits for them, and re-layouts: 24.9 us -> 5.12 us
  waiting for transfers between devices: 53.5 us -> 41.2 us
    pallas_call x6 -> x7, Pallas kernels: 102 us -> 68.7 us  [the longest x1 23.4 us: attend(): call(attend_body, (), [pl.BlockSpec(memory_space=pltpu.VMEM)] * 4, [pl.Bl...]
    all_to_all x1 -> x2, blocking collectives: 28 us -> 55.6 us  [the longest x1 30.7 us: reduce_all(): lax.all_to_all(packed.reshape(size, SLOTS, size), ALL, 0, 0, tiled=True)]
    all_to_all x1 -> x0, waiting for transfers between devices: 18.1 us -> none  [reduce_all(): return lax.all_to_all(spread, ALL, 0, 0, tiled=True)]
    all_to_all x3 -> x1, starting transfers between devices: 26.4 us -> 12.9 us  [swap(): return lax.all_to_all(flat, PAIRS, 0, 0, tiled=True)]
    all_to_all x1, blocking collectives: 21.6 us -> 33.6 us  [swap(): return lax.all_to_all(flat, PAIRS, 0, 0, tiled=True)]
    ppermute x8, waiting for transfers between devices: 3.28 us -> 12.9 us  [shift(): lax.ppermute(values, axes, ends if by > 0 else [(j, i) for i, j in ends])]
    unnamed x53 -> x20, local copies, waits for them, and re-layouts: 9.62 us -> 2.61 us
    all_to_all x1 -> x0, starting transfers between devices: 6.41 us -> none  [reduce_all(): return lax.all_to_all(spread, ALL, 0, 0, tiled=True)]
  transfers between devices with their start and end apart: 12 -> 9, of which waited for: 5 -> 5; matrix products, arithmetic and copies ran while one was open for 2% -> 1% of each run, Pallas kernels for 10% -> 0%
where the time goes in v2:
time: 247 us; the launch traced here: 246 us
  blocking collectives  89.2 us (36%)
  Pallas kernels  68.7 us (28%)
  waiting for transfers between devices  41.2 us (17%)
  starting transfers between devices  39.3 us (16%)
  local copies, waits for them, and re-layouts  5.12 us (2%)
    all_to_all x1, blocking collectives, swap(): return lax.all_to_all(flat, PAIRS, 0, 0, tiled=True)  33.6 us
    all_to_all x1, blocking collectives, reduce_all(): lax.all_to_all(packed.reshape(size, SLOTS, size), ALL, 0, 0, tiled=True)  30.7 us
    all_to_all x1, waiting for transfers between devices, swap(): return lax.all_to_all(flat, PAIRS, 0, 0, tiled=True)  28.3 us
    ppermute x8, starting transfers between devices, shift(): lax.ppermute(values, axes, ends if by > 0 else [(j, i) for i, j in ends])  26.4 us
    all_to_all x1, blocking collectives, reduce_all(): came = lax.all_to_all(total, ALL, 0, 0, tiled=True)  24.9 us
    pallas_call x1, Pallas kernels, attend(): call(attend_body, (), [pl.BlockSpec(memory_space=pltpu.VMEM)] * 4, [pl.Bl...  23.4 us
    pallas_call x1, Pallas kernels, expand_back(): call(expand_back_body, (tile_rows // count,), [rows(count, tile_cols, wid...  15.3 us
    pallas_call x1, Pallas kernels, forward(): call(forward_body, (steps + 1,), [early(count, tile_cols, channels), late...  13.1 us
  transfers between devices with their start and end apart: 9, of which 5 were waited for; matrix products, arithmetic and copies ran while one was open for 1% of the time, Pallas kernels for 0%

profile of v2, /device:TPU:1, one launch (start us, length us, event | category | flops | bytes accessed | tf_op | source)
XLA Modules:
  0.0 246.1 jit_solution(7441807196580906455)
XLA Ops:
  1.4 1.3 collective-permute-start.1
  2.7 6.3 %collective-permute-start = (f32[64,128]{1,0:T(8,128)S(1)}, f32[64,128]{1,0:T(8,128)S(1)}, u32[]{:S(2)}, u32[]{:S(2)}) collective-permute-start(f32[64,128]{1,0:T(8,128)S(1)} %get-tuple-element.59), channel_id=1, source_target_pairs={{0,16},{16,32},{32,48},{48,64},{64,80},{80,96},{96,112},{1,17},{17... | collective-permute-start | bytes 98312 | tf_op jit(solution)/shard_map/ppermute | solution.py:554
  10.1 5.2 %collective-permute-start.2 = (f32[34,128]{1,0:T(8,128)S(1)}, f32[34,128]{1,0:T(8,128)S(1)}, u32[]{:S(2)}, u32[]{:S(2)}) collective-permute-start(f32[34,128]{1,0:T(8,128)S(1)} %pad_maximum_fusion.2), channel_id=1, source_target_pairs={{0,1},{1,2},{2,3},{3,4},{4,5},{5,6},{6,7},{7,8},{8,9},{9,10},{10,1... | collective-permute-start | bytes 52232 | tf_op jit(solution)/shard_map/ppermute | solution.py:554
  15.3 1.9 collective-permute-start.3
  17.3 3.2 %collective-permute-done.3.right_ref = f32[34,128]{1,0:T(8,128)S(1)} collective-permute-done((f32[34,128]{1,0:T(8,128)S(1)}, f32[34,128]{1,0:T(8,128)S(1)}, u32[]{:S(2)}, u32[]{:S(2)}) %collective-permute-start.3) | collective-permute-done | bytes 17440 | tf_op jit(solution)/shard_map/ppermute | solution.py:554
  21.0 13.1 %shard_map.143 = (f32[8,512,128]{2,1,0:T(8,128)}, f32[32,64,512]{2,1,0:T(8,128)}, f32[32,64,512]{2,1,0:T(8,128)}) custom-call(f32[32,64,128]{2,1,0:T(8,128)} %field_ref.3, f32[32,64,128]{2,1,0:T(8,128)} %field_ref.3, f32[32,64,128]{2,1,0:T(8,128)} %cot_ref.1, f32[64,128]{1,0:T(8,128)} %copy-done.7, f32[64,128]{1,0:T(8,128)} %copy-done.6, ...), custom_call_target="tpu_custom_call" | custom-call | flops 1610612736 | bytes 13631488 | tf_op jit(solution)/shard_map/pallas_call | solution.py:189
  34.1 12.9 %all-to-all-start = ((f32[64,64,128]{2,1,0:T(8,128)}), f32[64,64,128]{2,1,0:T(8,128)S(1)}, u32[]{:S(2)}, u32[]{:S(2)}) async-start(f32[64,64,128]{2,1,0:T(8,128)} %bitcast.17), calls=%async_computation | async-start | bytes 4194304 | tf_op jit(solution)/shard_map/all_to_all | solution.py:576
  47.8 28.3 %all-to-all-done.came_ref = f32[64,64,128]{2,1,0:T(8,128)S(1)} async-done(((f32[64,64,128]{2,1,0:T(8,128)}), f32[64,64,128]{2,1,0:T(8,128)S(1)}, u32[]{:S(2)}, u32[]{:S(2)}) %all-to-all-start) | async-done | bytes 2097184 | tf_op jit(solution)/shard_map/all_to_all | solution.py:576
  76.0 1.4 copy-done
  77.4 23.4 %shard_map.144 = (f32[64,64,128]{2,1,0:T(8,128)}, f32[128,384]{1,0:T(8,128)}, f32[128,128]{1,0:T(8,128)}, f32[128,128]{1,0:T(8,128)}) custom-call(f32[64,64,128]{2,1,0:T(8,128)} %copy-done, f32[128,384]{1,0:T(8,128)} %qkv_ref.1, f32[128,128]{1,0:T(8,128)} %out_ref.1, f32[64,256]{1,0:T(8,128)} %copy.19.bias_ref), custom_call_target="tpu_custom_call" | custom-call | flops 3019898880 | bytes 4194304 | tf_op jit(solution)/shard_map/pallas_call | solution.py:317
  100.8 33.6 %all_to_all.20 = f32[64,64,128]{2,1,0:T(8,128)} all-to-all(f32[64,64,128]{2,1,0:T(8,128)} %get-tuple-element.33), channel_id=1, replica_groups=mesh['row'=8,'ch'=8,'core'=2] {'row','ch'}, dimensions={0} | all-to-all | bytes 4194304 | tf_op jit(solution)/shard_map/all_to_all | solution.py:576
  134.4 9.5 %shard_map.145 = (f32[32,64,128]{2,1,0:T(8,128)}, f32[32,64,128]{2,1,0:T(8,128)}, f32[32,64,512]{2,1,0:T(8,128)}, f32[64,512]{1,0:T(8,128)}, f32[64,512]{1,0:T(8...) custom-call(f32[8,512,128]{2,1,0:T(8,128)} %bitcast.18, ...), custom_call_target="tpu_custom_call" | custom-call | flops 1610612736 | bytes 14680064 | tf_op jit(solution)/shard_map/pallas_call | solution.py:391
  144.0 2.2 collective-permute-start.4
  146.2 1.3 collective-permute-start.5
  148.5 5.2 %collective-permute-done.5.bottom = f32[64,512]{1,0:T(8,128)S(1)} collective-permute-done((f32[64,512]{1,0:T(8,128)}, f32[64,512]{1,0:T(8,128)S(1)}, u32[]{:S(2)}, u32[]{:S(2)}) %collective-permute-start.5) | collective-permute-done | bytes 131104 | tf_op jit(solution)/shard_map/ppermute | solution.py:554
  154.6 6.1 %collective-permute-start.6 = (f32[34,512]{1,0:T(8,128)S(1)}, f32[34,512]{1,0:T(8,128)S(1)}, u32[]{:S(2)}, u32[]{:S(2)}) collective-permute-start(f32[34,512]{1,0:T(8,128)S(1)} %pad_maximum_fusion), channel_id=1, source_target_pairs={{0,1},{1,2},{2,3},{3,4},{4,5},{5,6},{6,7},{7,8},{8,9},{9,10},{10,1... | collective-permute-start | bytes 208904 | tf_op jit(solution)/shard_map/ppermute | solution.py:554
  161.5 2.1 collective-permute-start.7
  163.6 3.6 %collective-permute-done.7.right = f32[34,512]{1,0:T(8,128)S(1)} collective-permute-done((f32[34,512]{1,0:T(8,128)S(1)}, f32[34,512]{1,0:T(8,128)S(1)}, u32[]{:S(2)}, u32[]{:S(2)}) %collective-permute-start.7) | collective-permute-done | bytes 69664 | tf_op jit(solution)/shard_map/ppermute | solution.py:554
  167.9 15.3 %shard_map.146 = (f32[32,64,128]{2,1,0:T(8,128)}, f32[128,512]{1,0:T(8,128)}, f32[16,512]{1,0:T(8,128)}) custom-call(f32[32,64,512]{2,1,0:T(8,128)} %get-tuple-element.36.grad_ref.before_ref.after_ref, f32[32,64,512]{2,1,0:T(8,128)} %get-tuple-element.36.grad_ref.before_ref.after_ref, f32[32,64,512]{2,1,0:T(8,128)} %get-tuple-element.36.grad_ref.before_ref.after_ref, ...), custom_call_target="tpu_custom_call" | custom-call | flops 1610612736 | bytes 11534336 | tf_op jit(solution)/shard_map/pallas_call | solution.py:464
  183.2 2.6 %shard_map.147 = f32[2048,128]{1,0:T(8,128)} custom-call(f32[128,512]{1,0:T(8,128)} %get-tuple-element.44.expand_ref, f32[128,512]{1,0:T(8,128)} %get-tuple-element.45.project_ref, f32[128,384]{1,0:T(8,128)} %get-tuple-element.46.qkv_ref, f32[128,128]{1,0:T(8,128)} %get-tuple-element.47.out_ref, f32[128,128]{1,0:T(8,128)} %get-tuple-element.48.bias_ref, ...), custom_call_target="tpu_custom_call" | custom-call | tf_op jit(solution)/shard_map/pallas_call | solution.py:543
  185.8 30.7 %all_to_all.21.came_ref = f32[128,16,128]{2,1,0:T(8,128)} all-to-all(f32[128,16,128]{2,1,0:T(8,128)} %bitcast.20), channel_id=1, replica_groups=mesh['row'=8,'ch'=8,'core'=2] {'row','ch','core'}, dimensions={0} | all-to-all | bytes 2097152 | tf_op jit(solution)/shard_map/all_to_all | solution.py:544
  216.5 2.4 shard_map.148
  218.9 24.9 %all_to_all.22 = f32[128,16,128]{2,1,0:T(8,128)} all-to-all(f32[128,16,128]{2,1,0:T(8,128)} %shard_map.148), channel_id=1, replica_groups=mesh['row'=8,'ch'=8,'core'=2] {'row','ch','core'}, dimensions={0} | all-to-all | bytes 2097152 | tf_op jit(solution)/shard_map/all_to_all | solution.py:546
  243.8 2.3 shard_map.149
  (35 shorter events, 6.5 us)
Async XLA Ops:
  1.4 8.6 %collective-permute-start.1 = (f32[64,128]{1,0:T(8,128)S(1)}, f32[64,128]{1,0:T(8,128)S(1)}, u32[]{:S(2)}, u32[]{:S(2)}) collective-permute-start(f32[64,128]{1,0:T(8,128)S(1)} %get-tuple-element.58), channel_id=1, source_target_pairs={{16,0},{32,16},{48,32},{64,48},{80,64},{96,80},{112,96},{17,1},{33... | collective-permute-start | bytes 98312 | tf_op jit(solution)/shard_map/ppermute | solution.py:554
  2.7 7.3 %collective-permute-start = (f32[64,128]{1,0:T(8,128)S(1)}, f32[64,128]{1,0:T(8,128)S(1)}, u32[]{:S(2)}, u32[]{:S(2)}) collective-permute-start(f32[64,128]{1,0:T(8,128)S(1)} %get-tuple-element.59), channel_id=1, source_target_pairs={{0,16},{16,32},{32,48},{48,64},{64,80},{80,96},{96,112},{1,17},{17... | collective-permute-start | bytes 98312 | tf_op jit(solution)/shard_map/ppermute | solution.py:554
  10.0 10.4 %copy-start.6 = (f32[64,128]{1,0:T(8,128)}, f32[64,128]{1,0:T(8,128)S(1)}, u32[]{:S(2)}) copy-start(f32[64,128]{1,0:T(8,128)S(1)} %collective-permute-done.1.bottom_ref) | copy-start | bytes 98308
  10.0 10.4 %copy-start.7 = (f32[64,128]{1,0:T(8,128)}, f32[64,128]{1,0:T(8,128)S(1)}, u32[]{:S(2)}) copy-start(f32[64,128]{1,0:T(8,128)S(1)} %collective-permute-done.top_ref) | copy-start | bytes 98308
  10.1 7.2 %collective-permute-start.2 = (f32[34,128]{1,0:T(8,128)S(1)}, f32[34,128]{1,0:T(8,128)S(1)}, u32[]{:S(2)}, u32[]{:S(2)}) collective-permute-start(f32[34,128]{1,0:T(8,128)S(1)} %pad_maximum_fusion.2), channel_id=1, source_target_pairs={{0,1},{1,2},{2,3},{3,4},{4,5},{5,6},{6,7},{7,8},{8,9},{9,10},{10,1... | collective-permute-start | bytes 52232 | tf_op jit(solution)/shard_map/ppermute | solution.py:554
  15.3 5.1 %collective-permute-start.3 = (f32[34,128]{1,0:T(8,128)S(1)}, f32[34,128]{1,0:T(8,128)S(1)}, u32[]{:S(2)}, u32[]{:S(2)}) collective-permute-start(f32[34,128]{1,0:T(8,128)S(1)} %pad_maximum_fusion.3), channel_id=1, source_target_pairs={{1,0},{2,1},{3,2},{4,3},{5,4},{6,5},{7,6},{8,7},{9,8},{10,9},{11,1... | collective-permute-start | bytes 52232 | tf_op jit(solution)/shard_map/ppermute | solution.py:554
  17.3 3.2 %copy-start.8 = (f32[34,128]{1,0:T(8,128)}, f32[34,128]{1,0:T(8,128)S(1)}, u32[]{:S(2)}) copy-start(f32[34,128]{1,0:T(8,128)S(1)} %collective-permute-done.2.left_ref) | copy-start | bytes 52228
  20.4 0.6 copy-start.9
  34.1 12.9 %copy-start.3 = (f32[4,64,64]{2,1,0:T(8,128)S(1)}, f32[4,64,64]{2,1,0:T(8,128)}, u32[]{:S(2)}) copy-start(f32[4,64,64]{2,1,0:T(8,128)} %param.14) | copy-start | bytes 196612
  34.1 41.9 %all-to-all-start = ((f32[64,64,128]{2,1,0:T(8,128)}), f32[64,64,128]{2,1,0:T(8,128)S(1)}, u32[]{:S(2)}, u32[]{:S(2)}) async-start(f32[64,64,128]{2,1,0:T(8,128)} %bitcast.17), calls=%async_computation | async-start | bytes 4194304 | tf_op jit(solution)/shard_map/all_to_all | solution.py:576
  76.0 1.4 copy-start
  144.0 4.5 %collective-permute-start.4 = (f32[64,512]{1,0:T(8,128)}, f32[64,512]{1,0:T(8,128)S(1)}, u32[]{:S(2)}, u32[]{:S(2)}) collective-permute-start(f32[64,512]{1,0:T(8,128)} %get-tuple-element.37), channel_id=1, source_target_pairs={{0,16},{16,32},{32,48},{48,64},{64,80},{80,96},{96,112},{1,17},{17... | collective-permute-start | bytes 393224 | tf_op jit(solution)/shard_map/ppermute | solution.py:554
  146.2 7.4 %collective-permute-start.5 = (f32[64,512]{1,0:T(8,128)}, f32[64,512]{1,0:T(8,128)S(1)}, u32[]{:S(2)}, u32[]{:S(2)}) collective-permute-start(f32[64,512]{1,0:T(8,128)} %get-tuple-element.38), channel_id=1, source_target_pairs={{16,0},{32,16},{48,32},{64,48},{80,64},{96,80},{112,96},{17,1},{33... | collective-permute-start | bytes 393224 | tf_op jit(solution)/shard_map/ppermute | solution.py:554
  148.4 18.8 %copy-start.1 = (f32[64,512]{1,0:T(8,128)}, f32[64,512]{1,0:T(8,128)S(1)}, u32[]{:S(2)}) copy-start(f32[64,512]{1,0:T(8,128)S(1)} %collective-permute-done.4.top) | copy-start | bytes 393220
  153.6 13.6 %copy-start.2 = (f32[64,512]{1,0:T(8,128)}, f32[64,512]{1,0:T(8,128)S(1)}, u32[]{:S(2)}) copy-start(f32[64,512]{1,0:T(8,128)S(1)} %collective-permute-done.5.bottom) | copy-start | bytes 393220
  154.6 9.1 %collective-permute-start.6 = (f32[34,512]{1,0:T(8,128)S(1)}, f32[34,512]{1,0:T(8,128)S(1)}, u32[]{:S(2)}, u32[]{:S(2)}) collective-permute-start(f32[34,512]{1,0:T(8,128)S(1)} %pad_maximum_fusion), channel_id=1, source_target_pairs={{0,1},{1,2},{2,3},{3,4},{4,5},{5,6},{6,7},{7,8},{8,9},{9,10},{10,1... | collective-permute-start | bytes 208904 | tf_op jit(solution)/shard_map/ppermute | solution.py:554
  161.5 5.8 %collective-permute-start.7 = (f32[34,512]{1,0:T(8,128)S(1)}, f32[34,512]{1,0:T(8,128)S(1)}, u32[]{:S(2)}, u32[]{:S(2)}) collective-permute-start(f32[34,512]{1,0:T(8,128)S(1)} %pad_maximum_fusion.1), channel_id=1, source_target_pairs={{1,0},{2,1},{3,2},{4,3},{5,4},{6,5},{7,6},{8,7},{9,8},{10,9},{11,1... | collective-permute-start | bytes 208904 | tf_op jit(solution)/shard_map/ppermute | solution.py:554
  163.6 3.7 %copy-start.4 = (f32[34,512]{1,0:T(8,128)}, f32[34,512]{1,0:T(8,128)S(1)}, u32[]{:S(2)}) copy-start(f32[34,512]{1,0:T(8,128)S(1)} %collective-permute-done.6.left) | copy-start | bytes 208900
  167.3 0.6 copy-start.5

commit v3 on v2

--- a/solution.py
+++ b/solution.py
@@ -66,7 +66,7 @@
     return gated + 2.0 * values * (gated - gated * gated) * (K0 + (3.0 * K1) * (values * values))
 
 
-def call(body, grid, in_specs, out_specs, out_shape, scratch=(), flops=0, bytes_accessed=0, limit=56):
+def call(body, grid, in_specs, out_specs, out_shape, scratch=(), flops=0, bytes_accessed=0, limit=22):
     return pl.pallas_call(
         body,
         grid=grid,
@@ -113,8 +113,9 @@
 
 
 def forward_body(
-    field_ref, late_ref, cot_ref, top_ref, bottom_ref, left_ref, right_ref, expand_ref, depth_ref, weight_ref,
-    sent_ref, pre_ref, depth_out_ref, padded, left, right,
+    field_ref, late_ref, top_ref, bottom_ref, left_ref, right_ref, expand_ref, depth_ref, weight_ref,
+    sent_ref, pre_ref, depth_out_ref, depth_top_ref, depth_bottom_ref, depth_left_ref, depth_right_ref,
+    padded, left, right,
 ):
     step = pl.program_id(0)
     last = pl.num_programs(0) - 1
@@ -158,6 +159,8 @@
                         term = padded[start + i + p, 8 * q : 8 * q + cols, lanes] * depth_ref[3 * p + q : 3 * p + q + 1, lanes]
                         total = term if total is None else total + term
                 depth_out_ref[i, :, lanes] = total
+        depth_left_ref[...] = depth_out_ref[:, 0, :]
+        depth_right_ref[...] = depth_out_ref[:, cols - 1, :]
         activated = gelu(depth_out_ref[...].reshape(count * cols, wide))
         mixed = dot3(activated, weight_ref[...], NN) + load_rows(late_ref, cols)
         span = total_rows // GRID
@@ -165,15 +168,20 @@
             block, inner = divmod(i, span)
             for k in range(8):
                 here = i * cols + k * (cols // 8)
-                sent_ref[block, pl.ds(inner * 8 + k, cols // 8, stride=2 * span * 8), :] = mixed[
+                sent_ref[block, pl.ds(inner * 8 + k, cols // 8, stride=span * 8), :] = mixed[
                     here : here + cols // 8
                 ]
-            for c in range(cols // 8):
-                there = (2 * c + 1) * span * 8 + inner * 8
-                sent_ref[block, there : there + 8, :] = cot_ref[i, 8 * c : 8 * c + 8, :]
-
-
-def forward(field, cot, halo, expand_weight, depth_weight, weight, count=8):
+
+    @pl.when(step == 1)
+    def _():
+        depth_top_ref[...] = depth_out_ref[0]
+
+    @pl.when(step == last)
+    def _():
+        depth_bottom_ref[...] = depth_out_ref[count - 1]
+
+
+def forward(field, halo, expand_weight, depth_weight, weight, count=8):
     tile_rows, tile_cols, channels = field.shape
     wide = expand_weight.shape[1]
     span = tile_rows // GRID
@@ -189,19 +197,27 @@
     return call(
         forward_body,
         (steps + 1,),
-        [early(count, tile_cols, channels), late(count, tile_cols, channels), late(count, tile_cols, channels)]
+        [early(count, tile_cols, channels), late(count, tile_cols, channels)]
         + [whole(tile_cols, channels)] * 2
         + [whole(edge, channels)] * 2
         + [whole(channels, wide), whole(9, wide), whole(wide, channels)],
         [
-            late(count // span, 2 * span * tile_cols, channels),
+            late(count // span, span * tile_cols, channels),
             early(count, tile_cols, wide),
             late(count, tile_cols, wide),
+            whole(tile_cols, wide),
+            whole(tile_cols, wide),
+            late(count, wide),
+            late(count, wide),
         ],
         [
-            shape(GRID, 2 * span * tile_cols, channels),
-            shape(tile_rows, tile_cols, wide),
-            shape(tile_rows, tile_cols, wide),
+            shape(GRID, span * tile_cols, channels),
+            pltpu.HBM((tile_rows, tile_cols, wide), F32),
+            pltpu.HBM((tile_rows, tile_cols, wide), F32),
+            pltpu.HBM((tile_cols, wide), F32),
+            pltpu.HBM((tile_cols, wide), F32),
+            pltpu.HBM((tile_rows, wide), F32),
+            pltpu.HBM((tile_rows, wide), F32),
         ],
         scratch=[
             pltpu.VMEM((edge, tile_cols + 16, wide), F32),
@@ -209,35 +225,49 @@
             pltpu.VMEM((edge, wide), F32),
         ],
         flops=12 * tile_rows * tile_cols * channels * wide,
-        bytes_accessed=4 * tile_rows * tile_cols * (2 * wide + 5 * channels),
-    )(field, field, cot, *halo, expand_weight, depth_weight, weight)
+        bytes_accessed=4 * tile_rows * tile_cols * (2 * wide + 3 * channels),
+    )(field, field, *halo, expand_weight, depth_weight, weight)
+
+
+def arrange_body(tile_ref, sent_ref):
+    tile_rows, cols, _ = tile_ref.shape
+    span = tile_rows // GRID
+    for i in range(tile_rows):
+        block, inner = divmod(i, span)
+        for c in range(cols // 8):
+            there = c * span * 8 + inner * 8
+            sent_ref[block, there : there + 8, :] = tile_ref[i, 8 * c : 8 * c + 8, :]
+
+
+def arrange(tile):
+    tile_rows, tile_cols, channels = tile.shape
+    vmem = pl.BlockSpec(memory_space=pltpu.VMEM)
+    return call(arrange_body, (), [vmem], vmem, shape(GRID, tile_rows * tile_cols // GRID, channels))(tile)
 
 
 def attend_body(
-    came_ref, qkv_ref, out_ref, bias_ref,
-    leave_ref, grad_qkv_ref, grad_out_ref, grad_bias_ref,
-    packed_ref, delta_ref, mixture_ref, grad_packed_ref, bias_total,
+    mixed_ref, cot_ref, qkv_ref, out_ref, bias_ref,
+    leave_ref, mixture_out, grad_packed_out, grad_bias_ref,
+    packed_ref, delta_ref, mixture_ref, grad_packed_ref, bias_total, done,
 ):
-    places, both, channels = came_ref.shape
-    groups = both // 2
+    places, groups, channels = mixed_ref.shape
     head = channels // HEADS
     scale = head ** (-0.5)
-    step = 8
+    step = 32
     rows_in = step * groups
     together = 4
 
-    def chunk(i, which):
-        part = came_ref[pl.ds(i * step, step), which * groups : (which + 1) * groups, :]
-        return part.reshape(rows_in, channels)
+    def chunk(i, ref):
+        return ref[pl.ds(i * step, step)].reshape(rows_in, channels)
 
     def prepare(i, carry):
         here = pl.ds(pl.multiple_of(i * rows_in, rows_in), rows_in)
-        normed, _ = normalize(chunk(i, 0))
+        normed, _ = normalize(chunk(i, mixed_ref))
         packed = dot3(normed, qkv_ref[...], NN)
         packed_ref[0, here, :] = packed[:, :channels] * scale
         packed_ref[1, here, :] = packed[:, channels : 2 * channels]
         packed_ref[2, here, :] = packed[:, 2 * channels :]
-        delta_ref[here, :] = dot3(chunk(i, 1), out_ref[...], NT)
+        delta_ref[here, :] = dot3(chunk(i, cot_ref), out_ref[...], NT)
         return carry
 
     lax.fori_loop(0, places // step, prepare, 0)
@@ -288,40 +318,41 @@
 
     lax.fori_loop(0, groups // together, some_groups, 0)
 
-    grad_qkv_ref[...] = jnp.zeros_like(grad_qkv_ref)
-    grad_out_ref[...] = jnp.zeros_like(grad_out_ref)
+    copies = [
+        pltpu.make_async_copy(mixture_ref, mixture_out, done.at[0]),
+        pltpu.make_async_copy(grad_packed_ref, grad_packed_out, done.at[1]),
+    ]
+    for copy in copies:
+        copy.start()
     half = bias_total.shape[1] // 2
     grad_bias_ref[:places, :] = bias_total[:, :half]
     grad_bias_ref[places:, :] = bias_total[:, half:]
 
     def finish(i, carry):
         here = pl.ds(pl.multiple_of(i * rows_in, rows_in), rows_in)
-        mixture = split(mixture_ref[here, :])
-        normed, spread_scale = normalize(chunk(i, 0))
-        grad = split(jnp.concatenate([grad_packed_ref[k, here, :] for k in range(3)], axis=1))
-        grad_normed = dot3(grad, qkv_ref[...], NT)
-        grad_in = normalize_back(grad_normed, normed, spread_scale)
-        attended = dot3(mixture, out_ref[...], NN)
-        leave_ref[pl.ds(i * step, step), :groups, :] = grad_in.reshape(step, groups, channels)
-        leave_ref[pl.ds(i * step, step), groups:, :] = attended.reshape(step, groups, channels)
-        grad_out_ref[...] += dot3(mixture, chunk(i, 1), TN)
-        grad_qkv_ref[...] += dot3(normed, grad, TN)
+        normed, spread_scale = normalize(chunk(i, mixed_ref))
+        grad = jnp.concatenate([grad_packed_ref[k, here, :] for k in range(3)], axis=1)
+        grad_in = normalize_back(dot3(grad, qkv_ref[...], NT), normed, spread_scale)
+        leave_ref[pl.ds(i * step, step)] = grad_in.reshape(step, groups, channels)
         return carry
 
     lax.fori_loop(0, places // step, finish, 0)
-
-
-def attend(came, qkv_weight, out_weight, bias):
-    places, both, channels = came.shape
-    tokens = places * both // 2
+    for copy in copies:
+        copy.wait()
+
+
+def attend(mixed, cot, qkv_weight, out_weight, bias):
+    places, groups, channels = mixed.shape
+    tokens = places * groups
+    vmem = pl.BlockSpec(memory_space=pltpu.VMEM)
     return call(
         attend_body,
         (),
-        [pl.BlockSpec(memory_space=pltpu.VMEM)] * 4,
-        [pl.BlockSpec(memory_space=pltpu.VMEM)] * 4,
+        [vmem] * 5,
+        [vmem, pl.BlockSpec(memory_space=pl.ANY), pl.BlockSpec(memory_space=pl.ANY), vmem],
         [
-            shape(places, both, channels), shape(channels, 3 * channels),
-            shape(channels, channels), shape(2 * places, bias.shape[1] // 2),
+            shape(places, groups, channels), pltpu.HBM((tokens, channels), F32), pltpu.HBM((3, tokens, channels), F32),
+            shape(2 * places, bias.shape[1] // 2),
         ],
         scratch=[
             pltpu.VMEM((3, tokens, channels), F32),
@@ -329,18 +360,99 @@
             pltpu.VMEM((tokens, channels), F32),
             pltpu.VMEM((3, tokens, channels), F32),
             pltpu.VMEM(bias.shape, F32),
+            pltpu.SemaphoreType.DMA((2,)),
         ],
         flops=6 * tokens * channels * (12 * channels + 6 * places),
         bytes_accessed=16 * tokens * channels,
-    )(came, qkv_weight, out_weight, bias)
+    )(mixed, cot, qkv_weight, out_weight, bias)
+
+
+def attend_late_body(
+    mixed_ref, cot_ref, mixture_ref, grad_packed_ref, out_ref, attended_ref, grad_qkv_ref, grad_out_ref
+):
+    @pl.when(pl.program_id(0) == 0)
+    def _():
+        grad_qkv_ref[...] = jnp.zeros_like(grad_qkv_ref)
+        grad_out_ref[...] = jnp.zeros_like(grad_out_ref)
+
+    step, groups, channels = mixed_ref.shape
+    mixture = split(mixture_ref[...])
+    attended_ref[...] = dot3(mixture, out_ref[...], NN).reshape(attended_ref.shape)
+    grad_out_ref[...] += dot3(mixture, cot_ref[...].reshape(step * groups, channels), TN)
+    normed, _ = normalize(mixed_ref[...].reshape(step * groups, channels))
+    grad = jnp.concatenate([grad_packed_ref[k] for k in range(3)], axis=1)
+    grad_qkv_ref[...] += dot3(normed, grad, TN)
+
+
+def attend_late(mixed, cot, mixture, grad_packed, out_weight, step=16):
+    places, groups, channels = mixed.shape
+    tile = rows(step, groups, channels)
+    return call(
+        attend_late_body,
+        (places // step,),
+        [
+            tile, tile, rows(step * groups, channels),
+            pl.BlockSpec((3, step * groups, channels), lambda i: (0, i, 0)), whole(channels, channels),
+        ],
+        [tile, whole(channels, 3 * channels), whole(channels, channels)],
+        [shape(places, groups, channels), shape(channels, 3 * channels), shape(channels, channels)],
+        flops=30 * places * groups * channels * channels,
+        bytes_accessed=28 * places * groups * channels,
+    )(mixed, cot, mixture, grad_packed, out_weight)
+
+
+def edges_body(
+    came_ref, cot_ref, top_ref, bottom_ref, left_ref, right_ref, weight_ref,
+    grad_top_ref, grad_bottom_ref, grad_left_ref, grad_right_ref, mixed,
+):
+    tile_rows, cols, _ = cot_ref.shape
+    span = tile_rows // GRID
+    piece = span * 8
+    sides = 2 * cols
+    for at, i in ((0, 0), (cols, tile_rows - 1)):
+        block, inner = divmod(i, span)
+        for k in range(8):
+            here = at + k * (cols // 8)
+            mixed[here : here + cols // 8] = (
+                came_ref[block, pl.ds(inner * 8 + k, cols // 8, stride=piece), :]
+                + cot_ref[i, pl.ds(k, cols // 8, stride=8), :]
+            )
+    for at, j in ((sides, 0), (sides + tile_rows, cols - 1)):
+        first = (j // 8) * piece + j % 8
+        for block in range(GRID):
+            mixed[at + block * span : at + (block + 1) * span] = came_ref[block, pl.ds(first, span, stride=8), :]
+        mixed[at : at + tile_rows] += cot_ref[:, j, :]
+    grad = dot3(mixed[...], weight_ref[...], NT)
+    at = 0
+    for depth_ref, grad_ref in (
+        (top_ref, grad_top_ref), (bottom_ref, grad_bottom_ref), (left_ref, grad_left_ref), (right_ref, grad_right_ref)
+    ):
+        depth_out = depth_ref[...]
+        grad_ref[...] = grad[at : at + depth_out.shape[0]] * gelu_slope(depth_out, gate(depth_out))
+        at += depth_out.shape[0]
+
+
+def edges(came, cot, depth_edges, weight):
+    tile_rows, tile_cols, channels = cot.shape
+    wide = weight.shape[0]
+    vmem = pl.BlockSpec(memory_space=pltpu.VMEM)
+    return call(
+        edges_body,
+        (),
+        [vmem] * 7,
+        [vmem] * 4,
+        [shape(*a.shape) for a in depth_edges],
+        scratch=[pltpu.VMEM((2 * tile_cols + 2 * tile_rows, channels), F32)],
+        flops=12 * (tile_cols + tile_rows) * channels * wide,
+        bytes_accessed=2**21,
+    )(came, cot, *depth_edges, weight)
 
 
 def project_back_body(
-    came_ref, sent_ref, depth_out_ref, weight_ref,
-    block_out_ref, grad_mixed_ref, grad_depth_ref, top_ref, bottom_ref, left_ref, right_ref, total_ref,
+    came_ref, cot_ref, depth_out_ref, weight_ref,
+    grad_mixed_ref, grad_depth_ref, total_ref,
 ):
     step = pl.program_id(0)
-    last = pl.num_programs(0) - 1
     count, cols, wide = depth_out_ref.shape
     span = count // came_ref.shape[0]
     piece = span * 8
@@ -352,17 +464,8 @@
     parts = []
     for i in range(count):
         block, inner = divmod(i, span)
-        for c in range(cols // 8):
-            at = 2 * c * piece + inner * 8
-            block_out_ref[i, 8 * c : 8 * c + 8, :] = (
-                sent_ref[block, at : at + 8, :] + came_ref[block, at + piece : at + piece + 8, :]
-            )
-        for k in range(8):
-            at = inner * 8 + k
-            parts.append(
-                came_ref[block, pl.ds(at, cols // 8, stride=2 * piece), :]
-                + sent_ref[block, pl.ds(at + piece, cols // 8, stride=2 * piece), :]
-            )
+        for k, cot in enumerate(load_row(cot_ref, (i,), cols)):
+            parts.append(came_ref[block, pl.ds(inner * 8 + k, cols // 8, stride=piece), :] + cot)
     grad_mixed = jnp.concatenate(parts, axis=0)
     grad_mixed_ref[...] = grad_mixed.reshape(grad_mixed_ref.shape)
     mixed_split = split(grad_mixed)
@@ -371,19 +474,9 @@
     grad = dot3(mixed_split, weight_ref[...], NT) * gelu_slope(depth_out, gated)
     grad_depth_ref[...] = grad.reshape(count, cols, wide)
     total_ref[...] += dot3(mixed_split, depth_out * gated, TN)
-    left_ref[...] = grad_depth_ref[:, 0, :]
-    right_ref[...] = grad_depth_ref[:, cols - 1, :]
-
-    @pl.when(step == 0)
-    def _():
-        top_ref[...] = grad_depth_ref[0]
-
-    @pl.when(step == last)
-    def _():
-        bottom_ref[...] = grad_depth_ref[count - 1]
-
-
-def project_back(came, sent, depth_out, weight, count=8):
+
+
+def project_back(came, cot, depth_out, weight, count=8):
     tile_rows, tile_cols, wide = depth_out.shape
     channels = weight.shape[1]
     span = tile_rows // GRID
@@ -391,25 +484,18 @@
     return call(
         project_back_body,
         (tile_rows // count,),
-        [rows(count // span, 2 * span * tile_cols, channels)] * 2
-        + [rows(count, tile_cols, wide), whole(wide, channels)],
-        [tile, tile, rows(count, tile_cols, wide)]
-        + [whole(tile_cols, wide)] * 2
-        + [rows(count, wide)] * 2
-        + [whole(channels, wide)],
-        [shape(tile_rows, tile_cols, channels)] * 2
-        + [shape(tile_rows, tile_cols, wide)]
-        + [shape(tile_cols, wide)] * 2
-        + [shape(tile_rows, wide)] * 2
-        + [shape(channels, wide)],
+        [rows(count // span, span * tile_cols, channels), tile, rows(count, tile_cols, wide), whole(wide, channels)],
+        [tile, rows(count, tile_cols, wide), whole(channels, wide)],
+        [shape(tile_rows, tile_cols, channels), shape(tile_rows, tile_cols, wide), shape(channels, wide)],
         flops=12 * tile_rows * tile_cols * channels * wide,
-        bytes_accessed=4 * tile_rows * tile_cols * (2 * wide + 6 * channels),
-    )(came, sent, depth_out, weight)
+        bytes_accessed=4 * tile_rows * tile_cols * (2 * wide + 3 * channels),
+        limit=56,
+    )(came, cot, depth_out, weight)
 
 
 def expand_back_body(
-    grad_ref, before_ref, after_ref, top, bottom, left, right, pre_ref, field_ref, grad_mixed_ref,
-    expand_ref, depth_ref, grad_field_ref, grad_expand_ref, grad_depth_ref, padded, grad_pre,
+    grad_ref, before_ref, after_ref, top, bottom, left, right, pre_ref, field_ref, depth_ref,
+    grad_pre_ref, grad_expand_ref, grad_depth_ref, padded,
 ):
     step = pl.program_id(0)
     last = pl.num_programs(0) - 1
@@ -443,21 +529,14 @@
                 total = term if total is None else total + term
                 part = jnp.sum((window * hidden).reshape(cols // 8, 8, 128), axis=0)
                 taps[tap] = part if taps[tap] is None else taps[tap] + part
-            grad_pre[i * cols : (i + 1) * cols, lanes] = total * gelu_slope(pre, gated)
+            grad_pre_ref[i, :, lanes] = total * gelu_slope(pre, gated)
         for tap in range(9):
             grad_depth_ref[tap : tap + 1, lanes] += jnp.sum(taps[tap], axis=0, keepdims=True)
-    normed, scale = normalize(load_rows(field_ref, cols))
-    grad = split(grad_pre[...])
-    grad_expand_ref[...] += dot3(normed, grad, TN)
-    grad_normed = dot3(grad, expand_ref[...], NT)
-    grad_field = normalize_back(grad_normed, normed, scale) + grad_mixed_ref[...].reshape(count * cols, -1)
-    for i in range(count):
-        for k in range(8):
-            here = i * cols + k * (cols // 8)
-            grad_field_ref[i, pl.ds(k, cols // 8, stride=8), :] = grad_field[here : here + cols // 8]
-
-
-def expand_back(grad_depth_out, halo, pre, field, grad_mixed, expand_weight, depth_weight, count=8):
+    normed, _ = normalize(load_rows(field_ref, cols))
+    grad_expand_ref[...] += dot3(normed, grad_pre_ref[...].reshape(count * cols, wide), TN)
+
+
+def expand_back(grad_depth_out, halo, pre, field, depth_weight, count=8):
     tile_rows, tile_cols, channels = field.shape
     wide = pre.shape[2]
     edge = tile_rows + 2
@@ -471,19 +550,51 @@
         ]
         + [whole(tile_cols, wide)] * 2
         + [whole(edge, wide)] * 2
-        + [
-            rows(count, tile_cols, wide), rows(count, tile_cols, channels), rows(count, tile_cols, channels),
-            whole(channels, wide), whole(9, wide),
-        ],
-        [rows(count, tile_cols, channels), whole(channels, wide), whole(16, wide)],
-        [shape(tile_rows, tile_cols, channels), shape(channels, wide), shape(16, wide)],
-        scratch=[
-            pltpu.VMEM((count + 2, tile_cols + 16, wide), F32),
-            pltpu.VMEM((count * tile_cols, wide), F32),
-        ],
-        flops=12 * tile_rows * tile_cols * channels * wide,
-        bytes_accessed=4 * tile_rows * tile_cols * (2 * wide + 3 * channels),
-    )(grad_depth_out, grad_depth_out, grad_depth_out, *halo, pre, field, grad_mixed, expand_weight, depth_weight)
+        + [rows(count, tile_cols, wide), rows(count, tile_cols, channels), whole(9, wide)],
+        [rows(count, tile_cols, wide), whole(channels, wide), whole(16, wide)],
+        [shape(tile_rows, tile_cols, wide), shape(channels, wide), shape(16, wide)],
+        scratch=[pltpu.VMEM((count + 2, tile_cols + 16, wide), F32)],
+        flops=6 * tile_rows * tile_cols * channels * wide,
+        bytes_accessed=4 * tile_rows * tile_cols * (3 * wide + channels),
+        limit=56,
+    )(grad_depth_out, grad_depth_out, grad_depth_out, *halo, pre, field, depth_weight)
+
+
+def finish_body(
+    grad_pre_ref, field_ref, grad_mixed_ref, sent_ref, placed_ref, expand_ref, block_out_ref, grad_field_ref
+):
+    count, cols, wide = grad_pre_ref.shape
+    span = count // sent_ref.shape[0]
+    for i in range(count):
+        block, inner = divmod(i, span)
+        for c in range(cols // 8):
+            there = slice(c * span * 8 + inner * 8, c * span * 8 + inner * 8 + 8)
+            block_out_ref[i, 8 * c : 8 * c + 8, :] = sent_ref[block, there, :] + placed_ref[block, there, :]
+    normed, scale = normalize(load_rows(field_ref, cols))
+    grad_normed = dot3(grad_pre_ref[...].reshape(count * cols, wide), expand_ref[...], NT)
+    grad_field = normalize_back(grad_normed, normed, scale) + grad_mixed_ref[...].reshape(count * cols, -1)
+    for i in range(count):
+        for k in range(8):
+            here = i * cols + k * (cols // 8)
+            grad_field_ref[i, pl.ds(k, cols // 8, stride=8), :] = grad_field[here : here + cols // 8]
+
+
+def finish(grad_pre, field, grad_mixed, sent, placed, expand_weight, count=8):
+    tile_rows, tile_cols, channels = field.shape
+    wide = grad_pre.shape[2]
+    span = tile_rows // GRID
+    tile = rows(count, tile_cols, channels)
+    blocks = rows(count // span, span * tile_cols, channels)
+    return call(
+        finish_body,
+        (tile_rows // count,),
+        [rows(count, tile_cols, wide), tile, tile, blocks, blocks, whole(channels, wide)],
+        [tile, tile],
+        [shape(*field.shape)] * 2,
+        flops=6 * tile_rows * tile_cols * channels * wide,
+        bytes_accessed=4 * tile_rows * tile_cols * (wide + 6 * channels),
+        limit=56,
+    )(grad_pre, field, grad_mixed, sent, placed, expand_weight)
 
 
 SLOTS = 16
@@ -537,16 +648,18 @@
         depth_ref[:, k * size : (k + 1) * size] = matrix(slot + 2, taps, taps * k)[: depth_ref.shape[0]]
 
 
-def reduce_all(grads, like):
+def reduce_all(grads, like, after):
     size = grads[3].shape[0]
     vmem = pl.BlockSpec(memory_space=pltpu.VMEM)
     packed = call(pack_body, (), [vmem] * 6, vmem, shape(size * SLOTS, size))(*grads)
+    packed, after = lax.optimization_barrier((packed, after))
     came = lax.all_to_all(packed.reshape(size, SLOTS, size), ALL, 0, 0, tiled=True)
     total = call(total_body, (), [vmem], vmem, shape(size, SLOTS, size))(came)
     came = lax.all_to_all(total, ALL, 0, 0, tiled=True)
-    return call(unpack_body, (), [vmem], [vmem] * 6, [shape(*a.shape) for a in like])(
+    totals = call(unpack_body, (), [vmem], [vmem] * 6, [shape(*a.shape) for a in like])(
         came.reshape(size * SLOTS, size)
     )
+    return totals, after
 
 
 def shift(values, axes, count, by):
@@ -554,20 +667,16 @@
     return lax.ppermute(values, axes, ends if by > 0 else [(j, i) for i, j in ends])
 
 
-def surround(first, last, left, right, row_count, col_count):
-    top = shift(last, "row", row_count, 1)
-    bottom = shift(first, "row", row_count, -1)
-
+def beyond_rows(first, last, row_count):
+    return shift(last, "row", row_count, 1), shift(first, "row", row_count, -1)
+
+
+def beyond_columns(top, bottom, left, right, col_count):
     def column(edge, j):
         return jnp.concatenate([top[j : j + 1], edge, bottom[j : j + 1]], axis=0)
 
-    end = first.shape[0] - 1
-    return (
-        top,
-        bottom,
-        shift(column(right, end), COLS, col_count, 1),
-        shift(column(left, 0), COLS, col_count, -1),
-    )
+    end = top.shape[0] - 1
+    return shift(column(right, end), COLS, col_count, 1), shift(column(left, 0), COLS, col_count, -1)
 
 
 def swap(blocks):
@@ -580,22 +689,33 @@
     sizes, field, expand_weight, depth_weight, project_weight, qkv_weight, out_weight, pos_bias, cotangent
 ):
     places = GRID * GRID
-    halo = surround(field[0], field[-1], field[:, 0], field[:, -1], *sizes)
-    sent, pre, depth_out = forward(field, cotangent, halo, expand_weight, depth_weight, project_weight)
+    row_count, col_count = sizes
+    halo = beyond_rows(field[0], field[-1], row_count)
+    halo += beyond_columns(*halo, field[:, 0], field[:, -1], col_count)
+    arranged, halo = lax.optimization_barrier((arrange(cotangent), halo))
+    cot_grid = swap(arranged)
+    sent, pre, depth_out, *depth_edges = forward(field, halo, expand_weight, depth_weight, project_weight)
+    mixed_grid = swap(sent)
     bias = pos_bias.transpose(2, 0, 1).reshape(places, HEADS * places)
-    leave, grad_qkv, grad_out, grad_bias = attend(swap(sent), qkv_weight, out_weight, bias)
-    came = swap(leave).reshape(sent.shape)
-    block_out, grad_mixed, grad_depth_out, *edges, grad_project = project_back(
-        came, sent, depth_out, project_weight
-    )
-    halo = surround(*edges, *sizes)
-    grad_field, grad_expand, grad_depth = expand_back(
-        grad_depth_out, halo, pre, field, grad_mixed, expand_weight, depth_weight
-    )
-    grad_expand, grad_project, grad_qkv, grad_out, grad_bias, grad_depth = reduce_all(
+    leave, mixture, grad_packed, grad_bias = attend(mixed_grid, cot_grid, qkv_weight, out_weight, bias)
+    came = swap(leave)
+    attended, grad_qkv, grad_out = attend_late(mixed_grid, cot_grid, mixture, grad_packed, out_weight)
+    came, attended = lax.optimization_barrier((came, attended))
+    came = came.reshape(sent.shape)
+    placed = swap(attended).reshape(sent.shape)
+    first, last, left, right = edges(came, cotangent, depth_edges, project_weight)
+    halo = beyond_rows(first, last, row_count)
+    grad_mixed, grad_depth_out, grad_project = project_back(came, cotangent, depth_out, project_weight)
+    halo, grad_depth_out = lax.optimization_barrier((halo, grad_depth_out))
+    halo += beyond_columns(*halo, left, right, col_count)
+    grad_pre, grad_expand, grad_depth = expand_back(grad_depth_out, halo, pre, field, depth_weight)
+    totals, placed = reduce_all(
         (grad_expand, grad_project, grad_qkv, grad_out, grad_bias, grad_depth),
         (expand_weight, project_weight, qkv_weight, out_weight, pos_bias, depth_weight),
+        placed,
     )
+    grad_expand, grad_project, grad_qkv, grad_out, grad_bias, grad_depth = totals
+    block_out, grad_field = finish(grad_pre, field, grad_mixed, sent, placed, expand_weight)
     return (
         block_out,
         grad_field,

time: 247 us -> 223 us (0.903)
  blocking collectives: 89.2 us -> 30.8 us
  starting transfers between devices: 39.3 us -> 61.1 us
  local copies, waits for them, and re-layouts: 5.12 us -> 17.1 us
  waiting for transfers between devices: 41.2 us -> 47.8 us
  Pallas kernels: 68.7 us -> 63.7 us
    all_to_all x2 -> x0, blocking collectives: 58.5 us -> none  [the longest x1 33.6 us: swap(): return lax.all_to_all(flat, PAIRS, 0, 0, tiled=True)]
    all_to_all x1 -> x4, starting transfers between devices: 12.9 us -> 29.6 us  [swap(): return lax.all_to_all(flat, PAIRS, 0, 0, tiled=True)]
    all_to_all x0 -> x1, waiting for transfers between devices: none -> 12.9 us  [reduce_all(): came = lax.all_to_all(total, ALL, 0, 0, tiled=True)]
    unnamed x20 -> x66, local copies, waits for them, and re-layouts: 2.61 us -> 15.2 us
    ppermute x8, waiting for transfers between devices: 12.9 us -> 6.13 us  [shift(): lax.ppermute(values, axes, ends if by > 0 else [(j, i) for i, j in ends])]
    all_to_all x0 -> x1, starting transfers between devices: none -> 4.59 us  [reduce_all(): came = lax.all_to_all(total, ALL, 0, 0, tiled=True)]
    pallas_call x2 -> x6, Pallas kernels: 32.9 us -> 35.9 us  [the longest x1 17.3 us: attend(): call(attend_body, (), [vmem] * 5, [vmem, pl.BlockSpec(memory_space=pl.ANY...]
    all_to_all x1 -> x4, waiting for transfers between devices: 28.3 us -> 28.7 us  [swap(): return lax.all_to_all(flat, PAIRS, 0, 0, tiled=True)]
  transfers between devices with their start and end apart: 9 -> 13, of which waited for: 5 -> 7; matrix products, arithmetic and copies ran while one was open for 1% -> 1% of each run, Pallas kernels for 0% -> 20%
where the time goes in v3:
time: 223 us; the launch traced here: 222 us
  Pallas kernels  63.7 us (29%)
  starting transfers between devices  61.1 us (27%)
  waiting for transfers between devices  47.8 us (21%)
  blocking collectives  30.8 us (14%)
  local copies, waits for them, and re-layouts  17.1 us (8%)
    all_to_all x1, blocking collectives, reduce_all(): lax.all_to_all(packed.reshape(size, SLOTS, size), ALL, 0, 0, tiled=True)  30.8 us
    all_to_all x4, starting transfers between devices, swap(): return lax.all_to_all(flat, PAIRS, 0, 0, tiled=True)  29.6 us
    all_to_all x4, waiting for transfers between devices, swap(): return lax.all_to_all(flat, PAIRS, 0, 0, tiled=True)  28.7 us
    ppermute x8, starting transfers between devices, shift(): lax.ppermute(values, axes, ends if by > 0 else [(j, i) for i, j in ends])  26.9 us
    pallas_call x1, Pallas kernels, attend(): call(attend_body, (), [vmem] * 5, [vmem, pl.BlockSpec(memory_space=pl.ANY...  17.3 us
    unnamed x66, local copies, waits for them, and re-layouts  15.2 us
    pallas_call x1, Pallas kernels, expand_back(): call(expand_back_body, (tile_rows // count,), [rows(count, tile_cols, wid...  13.2 us
    all_to_all x1, waiting for transfers between devices, reduce_all(): came = lax.all_to_all(total, ALL, 0, 0, tiled=True)  12.9 us
  transfers between devices with their start and end apart: 13, of which 7 were waited for; matrix products, arithmetic and copies ran while one was open for 1% of the time, Pallas kernels for 20%

profile of v3, /device:TPU:1, one launch (start us, length us, event | category | flops | bytes accessed | tf_op | source)
XLA Modules:
  0.0 221.5 jit_solution(1396546478831287191)
XLA Ops:
  2.8 6.3 %collective-permute-start = (f32[64,128]{1,0:T(8,128)S(1)}, f32[64,128]{1,0:T(8,128)S(1)}, u32[]{:S(2)}, u32[]{:S(2)}) collective-permute-start(f32[64,128]{1,0:T(8,128)S(1)} %get-tuple-element.99), channel_id=1, source_target_pairs={{0,16},{16,32},{32,48},{48,64},{64,80},{80,96},{96,112},{1,17},{17... | collective-permute-start | bytes 98312 | tf_op jit(solution)/shard_map/ppermute | solution.py:667
  10.1 5.2 %collective-permute-start.2 = (f32[34,128]{1,0:T(8,128)S(1)}, f32[34,128]{1,0:T(8,128)S(1)}, u32[]{:S(2)}, u32[]{:S(2)}) collective-permute-start(f32[34,128]{1,0:T(8,128)S(1)} %pad_maximum_fusion.2), channel_id=1, source_target_pairs={{0,1},{1,2},{2,3},{3,4},{4,5},{5,6},{6,7},{7,8},{8,9},{9,10},{10,1... | collective-permute-start | bytes 52232 | tf_op jit(solution)/shard_map/ppermute | solution.py:667
  15.4 1.9 collective-permute-start.3
  20.5 12.8 %all-to-all-start.1 = ((f32[64,32,128]{2,1,0:T(8,128)}), f32[64,32,128]{2,1,0:T(8,128)S(1)}, u32[]{:S(2)}, u32[]{:S(2)}) async-start(f32[64,32,128]{2,1,0:T(8,128)} %bitcast.5), calls=%async_computation.1 | async-start | bytes 2097152 | tf_op jit(solution)/shard_map/all_to_all | solution.py:685
  33.3 11.8 %shard_map.144 = (f32[8,256,128]{2,1,0:T(8,128)}, f32[32,64,512]{2,1,0:T(8,128)}, f32[32,64,512]{2,1,0:T(8,128)}, f32[64,512]{1,0:T(8,128)}, f32[64,512]{1,0:T(8...) custom-call(f32[32,64,128]{2,1,0:T(8,128)S(1)} %copy-done.3, f32[32,64,128]{2,1,0:T(8,128)S(1)} %copy-done.3, ...), custom_call_target="tpu_custom_call" | custom-call | flops 1610612736 | bytes 11534336 | tf_op jit(solution)/shard_map/pallas_call | solution.py:197
  45.1 6.6 %all-to-all-done.1.cot_ref = f32[64,32,128]{2,1,0:T(8,128)S(1)} async-done(((f32[64,32,128]{2,1,0:T(8,128)}), f32[64,32,128]{2,1,0:T(8,128)S(1)}, u32[]{:S(2)}, u32[]{:S(2)}) %all-to-all-start.1) | async-done | bytes 1048608 | tf_op jit(solution)/shard_map/all_to_all | solution.py:685
  51.7 4.7 %all-to-all-start = ((f32[64,32,128]{2,1,0:T(8,128)}), f32[64,32,128]{2,1,0:T(8,128)S(1)}, u32[]{:S(2)}, u32[]{:S(2)}) async-start(f32[64,32,128]{2,1,0:T(8,128)} %bitcast.4), calls=%async_computation | async-start | bytes 2097152 | tf_op jit(solution)/shard_map/all_to_all | solution.py:685
  56.5 16.5 %all-to-all-done.mixed_ref = f32[64,32,128]{2,1,0:T(8,128)S(1)} async-done(((f32[64,32,128]{2,1,0:T(8,128)}), f32[64,32,128]{2,1,0:T(8,128)S(1)}, u32[]{:S(2)}, u32[]{:S(2)}) %all-to-all-start) | async-done | bytes 1048608 | tf_op jit(solution)/shard_map/all_to_all | solution.py:685
  74.0 17.3 %shard_map.145 = (f32[64,32,128]{2,1,0:T(8,128)}, f32[2048,128]{1,0:T(8,128)}, f32[3,2048,128]{2,1,0:T(8,128)}, f32[128,128]{1,0:T(8,128)S(1)}) custom-call(f32[64,32,128]{2,1,0:T(8,128)S(1)} %all-to-all-done.mixed_ref, f32[64,32,128]{2,1,0:T(8,128)S(1)} %all-to-all-done.1.cot_ref, f32[128,384]{1,0:T(8,128)S(1)} %copy-done.27, f32[128,128]{1,0:T(8,128)S(1)} %copy-done.17, ...), custom_call_target="tpu_custom_call" | custom-call | flops 3019898880 | bytes 4194304 | tf_op jit(solution)/shard_map/pallas_call | solution.py:348
  91.9 5.7 %all-to-all-start.2 = ((f32[64,32,128]{2,1,0:T(8,128)}), f32[64,32,128]{2,1,0:T(8,128)S(1)}, u32[]{:S(2)}, u32[]{:S(2)}) async-start(f32[64,32,128]{2,1,0:T(8,128)} %get-tuple-element.58), calls=%async_computation.2 | async-start | bytes 2097152 | tf_op jit(solution)/shard_map/all_to_all | solution.py:685
  98.9 1.9 copy-done.6
  102.8 3.2 %shard_map.146 = (f32[64,32,128]{2,1,0:T(8,128)S(1)}, f32[128,384]{1,0:T(8,128)S(1)}, f32[128,128]{1,0:T(8,128)S(1)}) custom-call(f32[64,32,128]{2,1,0:T(8,128)S(1)} %all-to-all-done.mixed_ref, f32[64,32,128]{2,1,0:T(8,128)S(1)} %copy-done.5, f32[2048,128]{1,0:T(8,128)S(1)} %copy-done.7, f32[3,2048,128]{2,1,0:T(8,128)S(1)} %copy-done.6, ...), custom_call_target="tpu_custom_call" | custom-call | flops 1006632960 | bytes 7340032 | tf_op jit(solution)/shard_map/pallas_call | solution.py:390
  108.3 5.6 %all-to-all-done.2 = f32[64,32,128]{2,1,0:T(8,128)S(1)} async-done(((f32[64,32,128]{2,1,0:T(8,128)}), f32[64,32,128]{2,1,0:T(8,128)S(1)}, u32[]{:S(2)}, u32[]{:S(2)}) %all-to-all-start.2) | async-done | bytes 1048608 | tf_op jit(solution)/shard_map/all_to_all | solution.py:685
  113.9 6.5 %all-to-all-start.3 = ((f32[64,32,128]{2,1,0:T(8,128)}), f32[64,32,128]{2,1,0:T(8,128)}, u32[]{:S(2)}, u32[]{:S(2)}) async-start(f32[64,32,128]{2,1,0:T(8,128)} %copy-done.8), calls=%async_computation.3 | async-start | bytes 2097152 | tf_op jit(solution)/shard_map/all_to_all | solution.py:685
  123.4 4.4 %collective-permute-start.4 = (f32[64,512]{1,0:T(8,128)S(1)}, f32[64,512]{1,0:T(8,128)S(1)}, u32[]{:S(2)}, u32[]{:S(2)}) collective-permute-start(f32[64,512]{1,0:T(8,128)S(1)} %get-tuple-element.67), channel_id=1, source_target_pairs={{0,16},{16,32},{32,48},{48,64},{64,80},{80,96},{96,112},{1,17},{17... | collective-permute-start | bytes 393224 | tf_op jit(solution)/shard_map/ppermute | solution.py:667
  129.2 7.4 %shard_map.148 = (f32[32,64,128]{2,1,0:T(8,128)}, f32[32,64,512]{2,1,0:T(8,128)}, f32[128,512]{1,0:T(8,128)}) custom-call(f32[8,256,128]{2,1,0:T(8,128)} %bitcast.20, f32[32,64,128]{2,1,0:T(8,128)} %cot_ref.3, f32[32,64,512]{2,1,0:T(8,128)} %get-tuple-element.69.depth_out_ref, f32[512,128]{1,0:T(8,128)} %weight_ref.5), custom_call_target="tpu_custom_call" | custom-call | flops 1610612736 | bytes 11534336 | tf_op jit(solution)/shard_map/pallas_call | solution.py:484
  138.1 4.4 %collective-permute-start.6 = (f32[34,512]{1,0:T(8,128)S(1)}, f32[34,512]{1,0:T(8,128)S(1)}, u32[]{:S(2)}, u32[]{:S(2)}) collective-permute-start(f32[34,512]{1,0:T(8,128)S(1)} %pad_maximum_fusion), channel_id=1, source_target_pairs={{0,1},{1,2},{2,3},{3,4},{4,5},{5,6},{6,7},{7,8},{8,9},{9,10},{10,1... | collective-permute-start | bytes 208904 | tf_op jit(solution)/shard_map/ppermute | solution.py:667
  142.5 1.9 collective-permute-start.7
  144.5 3.8 %collective-permute-done.7.right = f32[34,512]{1,0:T(8,128)S(1)} collective-permute-done((f32[34,512]{1,0:T(8,128)S(1)}, f32[34,512]{1,0:T(8,128)S(1)}, u32[]{:S(2)}, u32[]{:S(2)}) %collective-permute-start.7) | collective-permute-done | bytes 69664 | tf_op jit(solution)/shard_map/ppermute | solution.py:667
  148.9 13.2 %shard_map.149 = (f32[32,64,512]{2,1,0:T(8,128)}, f32[128,512]{1,0:T(8,128)}, f32[16,512]{1,0:T(8,128)}) custom-call(f32[32,64,512]{2,1,0:T(8,128)} %get-tuple-element.71.grad_ref.before_ref.after_ref, f32[32,64,512]{2,1,0:T(8,128)} %get-tuple-element.71.grad_ref.before_ref.after_ref, f32[32,64,512]{2,1,0:T(8,128)} %get-tuple-element.71.grad_ref.before_ref.after_ref, ...), custom_call_target="tpu_custom_call" | custom-call | flops 805306368 | bytes 13631488 | tf_op jit(solution)/shard_map/pallas_call | solution.py:543
  164.4 30.8 %all_to_all.30.came_ref = f32[128,16,128]{2,1,0:T(8,128)S(1)} all-to-all(f32[128,16,128]{2,1,0:T(8,128)S(1)} %bitcast.22), channel_id=1, replica_groups=mesh['row'=8,'ch'=8,'core'=2] {'row','ch','core'}, dimensions={0} | all-to-all | bytes 2097152 | tf_op jit(solution)/shard_map/all_to_all | solution.py:656
  196.4 4.6 %all-to-all-start.5 = ((f32[128,16,128]{2,1,0:T(8,128)}), f32[128,16,128]{2,1,0:T(8,128)S(1)}, u32[]{:S(2)}, u32[]{:S(2)}) async-start(f32[128,16,128]{2,1,0:T(8,128)} %shard_map.152), calls=%async_computation.5 | async-start | bytes 2097152 | tf_op jit(solution)/shard_map/all_to_all | solution.py:658
  201.0 6.5 %shard_map.151 = (f32[32,64,128]{2,1,0:T(8,128)}, f32[32,64,128]{2,1,0:T(8,128)}) custom-call(f32[32,64,512]{2,1,0:T(8,128)} %get-tuple-element.77.grad_pre_ref, f32[32,64,128]{2,1,0:T(8,128)} %field_ref.5, f32[32,64,128]{2,1,0:T(8,128)} %get-tuple-element.78.grad_mixed_ref, f32[8,256,128]{2,1,0:T(8,128)} %get-tuple-element.56.sent_ref, ...), custom_call_target="tpu_custom_call" | custom-call | flops 805306368 | bytes 10485760 | tf_op jit(solution)/shard_map/pallas_call | solution.py:588
  207.5 12.9 %all-to-all-done.5 = f32[128,16,128]{2,1,0:T(8,128)S(1)} async-done(((f32[128,16,128]{2,1,0:T(8,128)}), f32[128,16,128]{2,1,0:T(8,128)S(1)}, u32[]{:S(2)}, u32[]{:S(2)}) %all-to-all-start.5) | async-done | bytes 1048608 | tf_op jit(solution)/shard_map/all_to_all | solution.py:658
  (90 shorter events, 24.6 us)
Async XLA Ops:
  0.6 32.6 %copy-start.9 = (f32[512,128]{1,0:T(8,128)S(1)}, f32[512,128]{1,0:T(8,128)}, u32[]{:S(2)}) copy-start(f32[512,128]{1,0:T(8,128)} %weight_ref.5) | copy-start | bytes 786436
  0.6 32.6 %copy-start.25 = (f32[9,512]{1,0:T(8,128)S(1)}, f32[9,512]{1,0:T(8,128)}, u32[]{:S(2)}) copy-start(f32[9,512]{1,0:T(8,128)} %depth_ref.3) | copy-start | bytes 55300
  1.5 8.6 %collective-permute-start.1 = (f32[64,128]{1,0:T(8,128)S(1)}, f32[64,128]{1,0:T(8,128)S(1)}, u32[]{:S(2)}, u32[]{:S(2)}) collective-permute-start(f32[64,128]{1,0:T(8,128)S(1)} %get-tuple-element.98), channel_id=1, source_target_pairs={{16,0},{32,16},{48,32},{64,48},{80,64},{96,80},{112,96},{17,1},{33... | collective-permute-start | bytes 98312 | tf_op jit(solution)/shard_map/ppermute | solution.py:667
  2.8 7.3 %collective-permute-start = (f32[64,128]{1,0:T(8,128)S(1)}, f32[64,128]{1,0:T(8,128)S(1)}, u32[]{:S(2)}, u32[]{:S(2)}) collective-permute-start(f32[64,128]{1,0:T(8,128)S(1)} %get-tuple-element.99), channel_id=1, source_target_pairs={{0,16},{16,32},{32,48},{48,64},{64,80},{80,96},{96,112},{1,17},{17... | collective-permute-start | bytes 98312 | tf_op jit(solution)/shard_map/ppermute | solution.py:667
  10.1 9.5 %collective-permute-start.2 = (f32[34,128]{1,0:T(8,128)S(1)}, f32[34,128]{1,0:T(8,128)S(1)}, u32[]{:S(2)}, u32[]{:S(2)}) collective-permute-start(f32[34,128]{1,0:T(8,128)S(1)} %pad_maximum_fusion.2), channel_id=1, source_target_pairs={{0,1},{1,2},{2,3},{3,4},{4,5},{5,6},{6,7},{7,8},{8,9},{9,10},{10,1... | collective-permute-start | bytes 52232 | tf_op jit(solution)/shard_map/ppermute | solution.py:667
  15.4 5.1 %collective-permute-start.3 = (f32[34,128]{1,0:T(8,128)S(1)}, f32[34,128]{1,0:T(8,128)S(1)}, u32[]{:S(2)}, u32[]{:S(2)}) collective-permute-start(f32[34,128]{1,0:T(8,128)S(1)} %pad_maximum_fusion.3), channel_id=1, source_target_pairs={{1,0},{2,1},{3,2},{4,3},{5,4},{6,5},{7,6},{8,7},{9,8},{10,9},{11,1... | collective-permute-start | bytes 52232 | tf_op jit(solution)/shard_map/ppermute | solution.py:667
  18.5 14.7 %copy-start.3 = (f32[32,64,128]{2,1,0:T(8,128)S(1)}, f32[32,64,128]{2,1,0:T(8,128)}, u32[]{:S(2)}) copy-start(f32[32,64,128]{2,1,0:T(8,128)} %field_ref.5) | copy-start | bytes 3145732
  18.5 14.8 %copy-start.10 = (f32[128,512]{1,0:T(8,128)S(1)}, f32[128,512]{1,0:T(8,128)}, u32[]{:S(2)}) copy-start(f32[128,512]{1,0:T(8,128)} %expand_ref.3) | copy-start | bytes 786436
  20.5 31.2 %all-to-all-start.1 = ((f32[64,32,128]{2,1,0:T(8,128)}), f32[64,32,128]{2,1,0:T(8,128)S(1)}, u32[]{:S(2)}, u32[]{:S(2)}) async-start(f32[64,32,128]{2,1,0:T(8,128)} %bitcast.5), calls=%async_computation.1 | async-start | bytes 2097152 | tf_op jit(solution)/shard_map/all_to_all | solution.py:685
  33.3 23.1 %copy-start.30 = (f32[4,64,64]{2,1,0:T(8,128)S(1)}, f32[4,64,64]{2,1,0:T(8,128)}, u32[]{:S(2)}) copy-start(f32[4,64,64]{2,1,0:T(8,128)} %param.14) | copy-start | bytes 196612
  33.3 39.8 %copy-start.17 = (f32[128,128]{1,0:T(8,128)S(1)}, f32[128,128]{1,0:T(8,128)}, u32[]{:S(2)}) copy-start(f32[128,128]{1,0:T(8,128)} %out_ref.3) | copy-start | bytes 196612
  51.7 39.6 %copy-start.4 = (f32[64,32,128]{2,1,0:T(8,128)}, f32[64,32,128]{2,1,0:T(8,128)S(1)}, u32[]{:S(2)}) copy-start(f32[64,32,128]{2,1,0:T(8,128)S(1)} %all-to-all-done.1.cot_ref) | copy-start | bytes 3145732
  51.7 21.4 %all-to-all-start = ((f32[64,32,128]{2,1,0:T(8,128)}), f32[64,32,128]{2,1,0:T(8,128)S(1)}, u32[]{:S(2)}, u32[]{:S(2)}) async-start(f32[64,32,128]{2,1,0:T(8,128)} %bitcast.4), calls=%async_computation | async-start | bytes 2097152 | tf_op jit(solution)/shard_map/all_to_all | solution.py:685
  91.9 21.9 %all-to-all-start.2 = ((f32[64,32,128]{2,1,0:T(8,128)}), f32[64,32,128]{2,1,0:T(8,128)S(1)}, u32[]{:S(2)}, u32[]{:S(2)}) async-start(f32[64,32,128]{2,1,0:T(8,128)} %get-tuple-element.58), calls=%async_computation.2 | async-start | bytes 2097152 | tf_op jit(solution)/shard_map/all_to_all | solution.py:685
  102.8 17.5 %copy-start.1 = (f32[32,64,128]{2,1,0:T(8,128)S(1)}, f32[32,64,128]{2,1,0:T(8,128)}, u32[]{:S(2)}) copy-start(f32[32,64,128]{2,1,0:T(8,128)} %cot_ref.3) | copy-start | bytes 3145732
  102.8 17.6 %copy-start.15 = (f32[64,512]{1,0:T(8,128)S(1)}, f32[64,512]{1,0:T(8,128)}, u32[]{:S(2)}) copy-start(f32[64,512]{1,0:T(8,128)} %get-tuple-element.63.top_ref) | copy-start | bytes 393220
  113.9 15.3 %copy-start.2 = (f32[64,32,128]{2,1,0:T(8,128)}, f32[64,32,128]{2,1,0:T(8,128)S(1)}, u32[]{:S(2)}) copy-start(f32[64,32,128]{2,1,0:T(8,128)S(1)} %all-to-all-done.2) | copy-start | bytes 3145732
  113.9 50.5 %all-to-all-start.3 = ((f32[64,32,128]{2,1,0:T(8,128)}), f32[64,32,128]{2,1,0:T(8,128)}, u32[]{:S(2)}, u32[]{:S(2)}) async-start(f32[64,32,128]{2,1,0:T(8,128)} %copy-done.8), calls=%async_computation.3 | async-start | bytes 2097152 | tf_op jit(solution)/shard_map/all_to_all | solution.py:685
  123.4 13.3 %collective-permute-start.4 = (f32[64,512]{1,0:T(8,128)S(1)}, f32[64,512]{1,0:T(8,128)S(1)}, u32[]{:S(2)}, u32[]{:S(2)}) collective-permute-start(f32[64,512]{1,0:T(8,128)S(1)} %get-tuple-element.67), channel_id=1, source_target_pairs={{0,16},{16,32},{32,48},{48,64},{64,80},{80,96},{96,112},{1,17},{17... | collective-permute-start | bytes 393224 | tf_op jit(solution)/shard_map/ppermute | solution.py:667
  127.7 10.3 %collective-permute-start.5 = (f32[64,512]{1,0:T(8,128)S(1)}, f32[64,512]{1,0:T(8,128)S(1)}, u32[]{:S(2)}, u32[]{:S(2)}) collective-permute-start(f32[64,512]{1,0:T(8,128)S(1)} %get-tuple-element.68), channel_id=1, source_target_pairs={{16,0},{32,16},{48,32},{64,48},{80,64},{96,80},{112,96},{17,1},{33... | collective-permute-start | bytes 393224 | tf_op jit(solution)/shard_map/ppermute | solution.py:667
  138.1 6.4 %collective-permute-start.6 = (f32[34,512]{1,0:T(8,128)S(1)}, f32[34,512]{1,0:T(8,128)S(1)}, u32[]{:S(2)}, u32[]{:S(2)}) collective-permute-start(f32[34,512]{1,0:T(8,128)S(1)} %pad_maximum_fusion), channel_id=1, source_target_pairs={{0,1},{1,2},{2,3},{3,4},{4,5},{5,6},{6,7},{7,8},{8,9},{9,10},{10,1... | collective-permute-start | bytes 208904 | tf_op jit(solution)/shard_map/ppermute | solution.py:667
  142.5 5.8 %collective-permute-start.7 = (f32[34,512]{1,0:T(8,128)S(1)}, f32[34,512]{1,0:T(8,128)S(1)}, u32[]{:S(2)}, u32[]{:S(2)}) collective-permute-start(f32[34,512]{1,0:T(8,128)S(1)} %pad_maximum_fusion.1), channel_id=1, source_target_pairs={{1,0},{2,1},{3,2},{4,3},{5,4},{6,5},{7,6},{8,7},{9,8},{10,9},{11,1... | collective-permute-start | bytes 208904 | tf_op jit(solution)/shard_map/ppermute | solution.py:667
  148.9 13.2 %copy-start.24 = (f32[128,128]{1,0:T(8,128)S(1)}, f32[128,128]{1,0:T(8,128)}, u32[]{:S(2)}) copy-start(f32[128,128]{1,0:T(8,128)} %copy-done.23) | copy-start | bytes 196612
  196.4 24.0 %all-to-all-start.5 = ((f32[128,16,128]{2,1,0:T(8,128)}), f32[128,16,128]{2,1,0:T(8,128)S(1)}, u32[]{:S(2)}, u32[]{:S(2)}) async-start(f32[128,16,128]{2,1,0:T(8,128)} %shard_map.152), calls=%async_computation.5 | async-start | bytes 2097152 | tf_op jit(solution)/shard_map/all_to_all | solution.py:658
  (22 other events, 80.5 us)

commit v4 on v3

--- a/solution.py
+++ b/solution.py
@@ -112,8 +112,18 @@
     padded[at, 15 + cols : 16 + cols, :] = right
 
 
+def keep_row(values, flag):
+    return jnp.where(flag > 0, values, 0.0)
+
+
+def keep_column(values, flag, above, below):
+    at = lax.broadcasted_iota(jnp.int32, values.shape, 0)
+    kept = jnp.where(at == 0, above, jnp.where(at == values.shape[0] - 1, below, 1)) * flag
+    return jnp.where(kept > 0, values, 0.0)
+
+
 def forward_body(
-    field_ref, late_ref, top_ref, bottom_ref, left_ref, right_ref, expand_ref, depth_ref, weight_ref,
+    inside_ref, field_ref, late_ref, top_ref, bottom_ref, left_ref, right_ref, expand_ref, depth_ref, weight_ref,
     sent_ref, pre_ref, depth_out_ref, depth_top_ref, depth_bottom_ref, depth_left_ref, depth_right_ref,
     padded, left, right,
 ):
@@ -130,10 +140,11 @@
         def hidden(values):
             return gelu(dot3(normalize(values)[0], weight, NN))
 
-        left[...] = hidden(left_ref[...])
-        right[...] = hidden(right_ref[...])
-        for at, ref in ((0, top_ref), (total_rows + 1, bottom_ref)):
-            row = hidden(jnp.concatenate(load_row(ref, (), cols), axis=0))
+        above, below = inside_ref[0], inside_ref[1]
+        left[...] = hidden(keep_column(left_ref[...], inside_ref[2], above, below))
+        right[...] = hidden(keep_column(right_ref[...], inside_ref[3], above, below))
+        for at, ref, flag in ((0, top_ref, above), (total_rows + 1, bottom_ref, below)):
+            row = hidden(keep_row(jnp.concatenate(load_row(ref, (), cols), axis=0), flag))
             fill_row(padded, at, row, left[at : at + 1, :], right[at : at + 1, :])
 
     @pl.when(step < last)
@@ -181,7 +192,7 @@
         depth_bottom_ref[...] = depth_out_ref[count - 1]
 
 
-def forward(field, halo, expand_weight, depth_weight, weight, count=8):
+def forward(flags, field, halo, expand_weight, depth_weight, weight, count=8):
     tile_rows, tile_cols, channels = field.shape
     wide = expand_weight.shape[1]
     span = tile_rows // GRID
@@ -197,7 +208,7 @@
     return call(
         forward_body,
         (steps + 1,),
-        [early(count, tile_cols, channels), late(count, tile_cols, channels)]
+        [pl.BlockSpec(memory_space=pltpu.SMEM), early(count, tile_cols, channels), late(count, tile_cols, channels)]
         + [whole(tile_cols, channels)] * 2
         + [whole(edge, channels)] * 2
         + [whole(channels, wide), whole(9, wide), whole(wide, channels)],
@@ -226,7 +237,7 @@
         ],
         flops=12 * tile_rows * tile_cols * channels * wide,
         bytes_accessed=4 * tile_rows * tile_cols * (2 * wide + 3 * channels),
-    )(field, field, *halo, expand_weight, depth_weight, weight)
+    )(flags, field, field, *halo, expand_weight, depth_weight, weight)
 
 
 def arrange_body(tile_ref, sent_ref):
@@ -245,14 +256,24 @@
     return call(arrange_body, (), [vmem], vmem, shape(GRID, tile_rows * tile_cols // GRID, channels))(tile)
 
 
+SPARE = 8
+
+
+def pitched(ref, lead, first, count, pitch, groups):
+    return jnp.concatenate(
+        [ref[lead + (pl.ds(pl.multiple_of((first + j) * pitch, 8), groups),)] for j in range(count)], axis=0
+    )
+
+
 def attend_body(
     mixed_ref, cot_ref, qkv_ref, out_ref, bias_ref,
-    leave_ref, mixture_out, grad_packed_out, grad_bias_ref,
-    packed_ref, delta_ref, mixture_ref, grad_packed_ref, bias_total, done,
+    leave_ref, mixture_out, grad_packed_out, grad_bias_out,
+    packed_ref, delta_ref, mixture_ref, grad_packed_ref, bias_total, grad_bias_ref, done,
 ):
     places, groups, channels = mixed_ref.shape
     head = channels // HEADS
     scale = head ** (-0.5)
+    pitch = groups + SPARE
     step = 32
     rows_in = step * groups
     together = 4
@@ -261,13 +282,16 @@
         return ref[pl.ds(i * step, step)].reshape(rows_in, channels)
 
     def prepare(i, carry):
-        here = pl.ds(pl.multiple_of(i * rows_in, rows_in), rows_in)
         normed, _ = normalize(chunk(i, mixed_ref))
         packed = dot3(normed, qkv_ref[...], NN)
-        packed_ref[0, here, :] = packed[:, :channels] * scale
-        packed_ref[1, here, :] = packed[:, channels : 2 * channels]
-        packed_ref[2, here, :] = packed[:, 2 * channels :]
-        delta_ref[here, :] = dot3(chunk(i, cot_ref), out_ref[...], NT)
+        delta = dot3(chunk(i, cot_ref), out_ref[...], NT)
+        for j in range(step):
+            here = pl.ds(pl.multiple_of((i * step + j) * pitch, 8), groups)
+            part = slice(j * groups, (j + 1) * groups)
+            packed_ref[0, here, :] = packed[part, :channels] * scale
+            packed_ref[1, here, :] = packed[part, channels : 2 * channels]
+            packed_ref[2, here, :] = packed[part, 2 * channels :]
+            delta_ref[here, :] = delta[part]
         return carry
 
     lax.fori_loop(0, places // step, prepare, 0)
@@ -291,7 +315,7 @@
         return total
 
     def some_groups(i, carry):
-        here = [pl.ds(i * together + k, places, stride=groups) for k in range(together)]
+        here = [pl.ds(i * together + k, places, stride=pitch) for k in range(together)]
         query = [spread_split(packed_ref[0, h, :]) for h in here]
         delta = [spread_split(delta_ref[h, :]) for h in here]
         key = [split(packed_ref[1, h, :]) for h in here]
@@ -318,20 +342,22 @@
 
     lax.fori_loop(0, groups // together, some_groups, 0)
 
+    half = bias_total.shape[1] // 2
+    grad_bias_ref[:places, :] = bias_total[:, :half]
+    grad_bias_ref[places:, :] = bias_total[:, half:]
     copies = [
         pltpu.make_async_copy(mixture_ref, mixture_out, done.at[0]),
         pltpu.make_async_copy(grad_packed_ref, grad_packed_out, done.at[1]),
+        pltpu.make_async_copy(grad_bias_ref, grad_bias_out, done.at[2]),
     ]
     for copy in copies:
         copy.start()
-    half = bias_total.shape[1] // 2
-    grad_bias_ref[:places, :] = bias_total[:, :half]
-    grad_bias_ref[places:, :] = bias_total[:, half:]
 
     def finish(i, carry):
-        here = pl.ds(pl.multiple_of(i * rows_in, rows_in), rows_in)
         normed, spread_scale = normalize(chunk(i, mixed_ref))
-        grad = jnp.concatenate([grad_packed_ref[k, here, :] for k in range(3)], axis=1)
+        grad = jnp.concatenate(
+            [pitched(grad_packed_ref, (k,), i * step, step, pitch, groups) for k in range(3)], axis=1
+        )
         grad_in = normalize_back(dot3(grad, qkv_ref[...], NT), normed, spread_scale)
         leave_ref[pl.ds(i * step, step)] = grad_in.reshape(step, groups, channels)
         return carry
@@ -344,23 +370,25 @@
 def attend(mixed, cot, qkv_weight, out_weight, bias):
     places, groups, channels = mixed.shape
     tokens = places * groups
+    padded = places * (groups + SPARE)
     vmem = pl.BlockSpec(memory_space=pltpu.VMEM)
     return call(
         attend_body,
         (),
         [vmem] * 5,
-        [vmem, pl.BlockSpec(memory_space=pl.ANY), pl.BlockSpec(memory_space=pl.ANY), vmem],
+        [vmem] + [pl.BlockSpec(memory_space=pl.ANY)] * 3,
         [
-            shape(places, groups, channels), pltpu.HBM((tokens, channels), F32), pltpu.HBM((3, tokens, channels), F32),
-            shape(2 * places, bias.shape[1] // 2),
+            shape(places, groups, channels), pltpu.HBM((padded, channels), F32), pltpu.HBM((3, padded, channels), F32),
+            pltpu.HBM((2 * places, bias.shape[1] // 2), F32),
         ],
         scratch=[
-            pltpu.VMEM((3, tokens, channels), F32),
-            pltpu.VMEM((tokens, channels), F32),
-            pltpu.VMEM((tokens, channels), F32),
-            pltpu.VMEM((3, tokens, channels), F32),
+            pltpu.VMEM((3, padded, channels), F32),
+            pltpu.VMEM((padded, channels), F32),
+            pltpu.VMEM((padded, channels), F32),
+            pltpu.VMEM((3, padded, channels), F32),
             pltpu.VMEM(bias.shape, F32),
-            pltpu.SemaphoreType.DMA((2,)),
+            pltpu.VMEM((2 * places, bias.shape[1] // 2), F32),
+            pltpu.SemaphoreType.DMA((3,)),
         ],
         flops=6 * tokens * channels * (12 * channels + 6 * places),
         bytes_accessed=16 * tokens * channels,
@@ -376,11 +404,14 @@
         grad_out_ref[...] = jnp.zeros_like(grad_out_ref)
 
     step, groups, channels = mixed_ref.shape
-    mixture = split(mixture_ref[...])
+    pitch = groups + SPARE
+    mixture = split(pitched(mixture_ref, (), 0, step, pitch, groups))
     attended_ref[...] = dot3(mixture, out_ref[...], NN).reshape(attended_ref.shape)
     grad_out_ref[...] += dot3(mixture, cot_ref[...].reshape(step * groups, channels), TN)
     normed, _ = normalize(mixed_ref[...].reshape(step * groups, channels))
-    grad = jnp.concatenate([grad_packed_ref[k] for k in range(3)], axis=1)
+    grad = jnp.concatenate(
+        [pitched(grad_packed_ref, (k,), 0, step, pitch, groups) for k in range(3)], axis=1
+    )
     grad_qkv_ref[...] += dot3(normed, grad, TN)
 
 
@@ -391,8 +422,8 @@
         attend_late_body,
         (places // step,),
         [
-            tile, tile, rows(step * groups, channels),
-            pl.BlockSpec((3, step * groups, channels), lambda i: (0, i, 0)), whole(channels, channels),
+            tile, tile, rows(step * (groups + SPARE), channels),
+            pl.BlockSpec((3, step * (groups + SPARE), channels), lambda i: (0, i, 0)), whole(channels, channels),
         ],
         [tile, whole(channels, 3 * channels), whole(channels, channels)],
         [shape(places, groups, channels), shape(channels, 3 * channels), shape(channels, channels)],
@@ -445,6 +476,7 @@
         scratch=[pltpu.VMEM((2 * tile_cols + 2 * tile_rows, channels), F32)],
         flops=12 * (tile_cols + tile_rows) * channels * wide,
         bytes_accessed=2**21,
+        limit=56,
     )(came, cot, *depth_edges, weight)
 
 
@@ -493,9 +525,29 @@
     )(came, cot, depth_out, weight)
 
 
+SLOTS = 16
+
+
+def pack(refs, taps_ref, packed_ref):
+    size = refs[0].shape[0]
+    slot = 0
+    for ref in refs:
+        for lane in range(0, ref.shape[1], size):
+            packed_ref[pl.ds(slot, size, stride=SLOTS), :] = ref[:, lane : lane + size]
+            slot += 1
+    taps = taps_ref.shape[0]
+    empty = jnp.zeros((size, size), F32)
+    packed_ref[pl.ds(slot, size, stride=SLOTS), :] = empty
+    for k in range(taps_ref.shape[1] // size):
+        packed_ref[pl.ds(slot + SLOTS * taps * k, taps, stride=SLOTS), :] = taps_ref[:, k * size : (k + 1) * size]
+    for spare in range(slot + 1, SLOTS):
+        packed_ref[pl.ds(spare, size, stride=SLOTS), :] = empty
+
+
 def expand_back_body(
-    grad_ref, before_ref, after_ref, top, bottom, left, right, pre_ref, field_ref, depth_ref,
-    grad_pre_ref, grad_expand_ref, grad_depth_ref, padded,
+    inside_ref, grad_ref, before_ref, after_ref, top, bottom, left_ref, right_ref, pre_ref, field_ref, depth_ref,
+    project_ref, qkv_ref, out_ref, bias_ref,
+    grad_pre_ref, packed_ref, padded, left, right, grad_expand_ref, grad_depth_ref,
 ):
     step = pl.program_id(0)
     last = pl.num_programs(0) - 1
@@ -505,13 +557,15 @@
     def _():
         grad_expand_ref[...] = jnp.zeros_like(grad_expand_ref)
         grad_depth_ref[...] = jnp.zeros_like(grad_depth_ref)
+        left[...] = keep_column(left_ref[...], inside_ref[2], inside_ref[0], inside_ref[1])
+        right[...] = keep_column(right_ref[...], inside_ref[3], inside_ref[0], inside_ref[1])
 
     def fill(at, row):
         edge = pl.ds(step * count + at, 1)
         fill_row(padded, at, row, left[edge, :], right[edge, :])
 
-    fill(0, jnp.where(step == 0, top[...], before_ref[0]))
-    fill(count + 1, jnp.where(step == last, bottom[...], after_ref[0]))
+    fill(0, jnp.where(step == 0, keep_row(top[...], inside_ref[0]), before_ref[0]))
+    fill(count + 1, jnp.where(step == last, keep_row(bottom[...], inside_ref[1]), after_ref[0]))
     for i in range(count):
         fill(i + 1, grad_ref[i])
     for lane in range(0, wide, 128):
@@ -535,8 +589,12 @@
     normed, _ = normalize(load_rows(field_ref, cols))
     grad_expand_ref[...] += dot3(normed, grad_pre_ref[...].reshape(count * cols, wide), TN)
 
-
-def expand_back(grad_depth_out, halo, pre, field, depth_weight, count=8):
+    @pl.when(step == last)
+    def _():
+        pack((grad_expand_ref, project_ref, qkv_ref, out_ref, bias_ref), grad_depth_ref, packed_ref)
+
+
+def expand_back(flags, grad_depth_out, halo, pre, field, depth_weight, grads, count=8):
     tile_rows, tile_cols, channels = field.shape
     wide = pre.shape[2]
     edge = tile_rows + 2
@@ -544,20 +602,28 @@
         expand_back_body,
         (tile_rows // count,),
         [
+            pl.BlockSpec(memory_space=pltpu.SMEM),
             rows(count, tile_cols, wide),
             pl.BlockSpec((1, tile_cols, wide), lambda i: (jnp.maximum(count * i - 1, 0), 0, 0)),
             pl.BlockSpec((1, tile_cols, wide), lambda i: (jnp.minimum(count * i + count, tile_rows - 1), 0, 0)),
         ]
         + [whole(tile_cols, wide)] * 2
         + [whole(edge, wide)] * 2
-        + [rows(count, tile_cols, wide), rows(count, tile_cols, channels), whole(9, wide)],
-        [rows(count, tile_cols, wide), whole(channels, wide), whole(16, wide)],
-        [shape(tile_rows, tile_cols, wide), shape(channels, wide), shape(16, wide)],
-        scratch=[pltpu.VMEM((count + 2, tile_cols + 16, wide), F32)],
+        + [rows(count, tile_cols, wide), rows(count, tile_cols, channels), whole(9, wide)]
+        + [whole(*a.shape) for a in grads],
+        [rows(count, tile_cols, wide), whole(channels * SLOTS, channels)],
+        [pltpu.HBM((tile_rows, tile_cols, wide), F32), shape(channels * SLOTS, channels)],
+        scratch=[
+            pltpu.VMEM((count + 2, tile_cols + 16, wide), F32),
+            pltpu.VMEM((edge, wide), F32),
+            pltpu.VMEM((edge, wide), F32),
+            pltpu.VMEM((channels, wide), F32),
+            pltpu.VMEM((16, wide), F32),
+        ],
         flops=6 * tile_rows * tile_cols * channels * wide,
         bytes_accessed=4 * tile_rows * tile_cols * (3 * wide + channels),
         limit=56,
-    )(grad_depth_out, grad_depth_out, grad_depth_out, *halo, pre, field, depth_weight)
+    )(flags, grad_depth_out, grad_depth_out, grad_depth_out, *halo, pre, field, depth_weight, *grads)
 
 
 def finish_body(
@@ -595,25 +661,6 @@
         bytes_accessed=4 * tile_rows * tile_cols * (wide + 6 * channels),
         limit=56,
     )(grad_pre, field, grad_mixed, sent, placed, expand_weight)
-
-
-SLOTS = 16
-
-
-def pack_body(expand_ref, project_ref, qkv_ref, out_ref, bias_ref, depth_ref, packed_ref):
-    size = out_ref.shape[0]
-    slot = 0
-    for ref in (expand_ref, project_ref, qkv_ref, out_ref, bias_ref):
-        for lane in range(0, ref.shape[1], size):
-            packed_ref[pl.ds(slot, size, stride=SLOTS), :] = ref[:, lane : lane + size]
-            slot += 1
-    taps = depth_ref.shape[0]
-    empty = jnp.zeros((size, size), F32)
-    packed_ref[pl.ds(slot, size, stride=SLOTS), :] = empty
-    for k in range(depth_ref.shape[1] // size):
-        packed_ref[pl.ds(slot + SLOTS * taps * k, taps, stride=SLOTS), :] = depth_ref[:, k * size : (k + 1) * size]
-    for spare in range(slot + 1, SLOTS):
-        packed_ref[pl.ds(spare, size, stride=SLOTS), :] = empty
 
 
 def total_body(came_ref, total_ref):
@@ -648,10 +695,9 @@
         depth_ref[:, k * size : (k + 1) * size] = matrix(slot + 2, taps, taps * k)[: depth_ref.shape[0]]
 
 
-def reduce_all(grads, like, after):
-    size = grads[3].shape[0]
+def reduce_all(packed, like, after):
+    size = packed.shape[1]
     vmem = pl.BlockSpec(memory_space=pltpu.VMEM)
-    packed = call(pack_body, (), [vmem] * 6, vmem, shape(size * SLOTS, size))(*grads)
     packed, after = lax.optimization_barrier((packed, after))
     came = lax.all_to_all(packed.reshape(size, SLOTS, size), ALL, 0, 0, tiled=True)
     total = call(total_body, (), [vmem], vmem, shape(size, SLOTS, size))(came)
@@ -663,8 +709,12 @@
 
 
 def shift(values, axes, count, by):
-    ends = [(i, i + 1) for i in range(count - 1)]
-    return lax.ppermute(values, axes, ends if by > 0 else [(j, i) for i, j in ends])
+    return lax.ppermute(values, axes, [(i, (i + by) % count) for i in range(count)])
+
+
+def inside(row_count, col_count):
+    row, col = lax.axis_index("row"), lax.axis_index(COLS)
+    return jnp.stack([row > 0, row < row_count - 1, col > 0, col < col_count - 1]).astype(jnp.int32)
 
 
 def beyond_rows(first, last, row_count):
@@ -690,11 +740,12 @@
 ):
     places = GRID * GRID
     row_count, col_count = sizes
+    flags = inside(row_count, col_count)
     halo = beyond_rows(field[0], field[-1], row_count)
     halo += beyond_columns(*halo, field[:, 0], field[:, -1], col_count)
     arranged, halo = lax.optimization_barrier((arrange(cotangent), halo))
     cot_grid = swap(arranged)
-    sent, pre, depth_out, *depth_edges = forward(field, halo, expand_weight, depth_weight, project_weight)
+    sent, pre, depth_out, *depth_edges = forward(flags, field, halo, expand_weight, depth_weight, project_weight)
     mixed_grid = swap(sent)
     bias = pos_bias.transpose(2, 0, 1).reshape(places, HEADS * places)
     leave, mixture, grad_packed, grad_bias = attend(mixed_grid, cot_grid, qkv_weight, out_weight, bias)
@@ -702,15 +753,18 @@
     attended, grad_qkv, grad_out = attend_late(mixed_grid, cot_grid, mixture, grad_packed, out_weight)
     came, attended = lax.optimization_barrier((came, attended))
     came = came.reshape(sent.shape)
-    placed = swap(attended).reshape(sent.shape)
     first, last, left, right = edges(came, cotangent, depth_edges, project_weight)
     halo = beyond_rows(first, last, row_count)
     grad_mixed, grad_depth_out, grad_project = project_back(came, cotangent, depth_out, project_weight)
     halo, grad_depth_out = lax.optimization_barrier((halo, grad_depth_out))
     halo += beyond_columns(*halo, left, right, col_count)
-    grad_pre, grad_expand, grad_depth = expand_back(grad_depth_out, halo, pre, field, depth_weight)
+    halo, attended = lax.optimization_barrier((halo, attended))
+    placed = swap(attended).reshape(sent.shape)
+    grad_pre, packed = expand_back(
+        flags, grad_depth_out, halo, pre, field, depth_weight, (grad_project, grad_qkv, grad_out, grad_bias)
+    )
     totals, placed = reduce_all(
-        (grad_expand, grad_project, grad_qkv, grad_out, grad_bias, grad_depth),
+        packed,
         (expand_weight, project_weight, qkv_weight, out_weight, pos_bias, depth_weight),
         placed,
     )

time: 223 us -> 206 us (0.924)
  starting transfers between devices: 61.1 us -> 49 us
  local copies, waits for them, and re-layouts: 17.1 us -> 7.31 us
  waiting for transfers between devices: 47.8 us -> 56.4 us
  blocking collectives: 30.8 us -> 25.1 us
    unnamed x66 -> x40, local copies, waits for them, and re-layouts: 15.2 us -> 5.4 us
    ppermute x8, starting transfers between devices: 26.9 us -> 19.4 us  [shift(): lax.ppermute(values, axes, [(i, (i + by) % count) for i in range(count)])]
    all_to_all x1, blocking collectives: 30.8 us -> 25.1 us  [reduce_all(): lax.all_to_all(packed.reshape(size, SLOTS, size), ALL, 0, 0, tiled=True)]
    all_to_all x4, starting transfers between devices: 29.6 us -> 25 us  [swap(): return lax.all_to_all(flat, PAIRS, 0, 0, tiled=True)]
    all_to_all x4, waiting for transfers between devices: 28.7 us -> 33.3 us  [swap(): return lax.all_to_all(flat, PAIRS, 0, 0, tiled=True)]
    ppermute x8, waiting for transfers between devices: 6.13 us -> 10.3 us  [shift(): lax.ppermute(values, axes, [(i, (i + by) % count) for i in range(count)])]
    pallas_call x1, Pallas kernels: 0.41 us -> 2.72 us  [edges(): call(edges_body, (), [vmem] * 7, [vmem] * 4, [shape(*a.shape) for a in de...]
    pallas_call x5 -> x4, Pallas kernels: 46 us -> 45.8 us  [the longest x1 15 us: attend(): call(attend_body, (), [vmem] * 5, [vmem] + [pl.BlockSpec(memory_space=pl....]
  transfers between devices with their start and end apart: 13 -> 13, of which waited for: 7 -> 9; matrix products, arithmetic and copies ran while one was open for 1% -> 1% of each run, Pallas kernels for 20% -> 22%
where the time goes in v4:
time: 206 us; the launch traced here: 205 us
  Pallas kernels  65.8 us (32%)
  waiting for transfers between devices  56.4 us (27%)
  starting transfers between devices  49 us (24%)
  blocking collectives  25.1 us (12%)
  local copies, waits for them, and re-layouts  7.31 us (4%)
    all_to_all x4, waiting for transfers between devices, swap(): return lax.all_to_all(flat, PAIRS, 0, 0, tiled=True)  33.3 us
    all_to_all x1, blocking collectives, reduce_all(): lax.all_to_all(packed.reshape(size, SLOTS, size), ALL, 0, 0, tiled=True)  25.1 us
    all_to_all x4, starting transfers between devices, swap(): return lax.all_to_all(flat, PAIRS, 0, 0, tiled=True)  25 us
    ppermute x8, starting transfers between devices, shift(): lax.ppermute(values, axes, [(i, (i + by) % count) for i in range(count)])  19.4 us
    pallas_call x1, Pallas kernels, attend(): call(attend_body, (), [vmem] * 5, [vmem] + [pl.BlockSpec(memory_space=pl....  15 us
    pallas_call x1, Pallas kernels, expand_back(): call(expand_back_body, (tile_rows // count,), [pl.BlockSpec(memory_space=...  14.7 us
    all_to_all x1, waiting for transfers between devices, reduce_all(): came = lax.all_to_all(total, ALL, 0, 0, tiled=True)  12.9 us
    pallas_call x1, Pallas kernels, forward(): call(forward_body, (steps + 1,), [pl.BlockSpec(memory_space=pltpu.SMEM),...  12.3 us
  transfers between devices with their start and end apart: 13, of which 9 were waited for; matrix products, arithmetic and copies ran while one was open for 1% of the time, Pallas kernels for 22%

profile of v4, /device:TPU:1, one launch (start us, length us, event | category | flops | bytes accessed | tf_op | source)
XLA Modules:
  0.0 204.7 jit_solution(1027508817352913012)
XLA Ops:
  1.5 5.9 %collective-permute-start.1 = (f32[64,128]{1,0:T(8,128)S(1)}, f32[64,128]{1,0:T(8,128)S(1)}, u32[]{:S(2)}, u32[]{:S(2)}) collective-permute-start(f32[64,128]{1,0:T(8,128)S(1)} %get-tuple-element.106), channel_id=1, source_target_pairs={{0,112},{16,0},{32,16},{48,32},{64,48},{80,64},{96,80},{112,96},{1... | collective-permute-start | bytes 98312 | tf_op jit(solution)/shard_map/ppermute | solution.py:712
  8.4 5.3 %collective-permute-done.top_ref = f32[64,128]{1,0:T(8,128)S(1)} collective-permute-done((f32[64,128]{1,0:T(8,128)S(1)}, f32[64,128]{1,0:T(8,128)S(1)}, u32[]{:S(2)}, u32[]{:S(2)}) %collective-permute-start) | collective-permute-done | bytes 32800 | tf_op jit(solution)/shard_map/ppermute | solution.py:712
  13.8 3.7 %collective-permute-start.2 = (f32[34,128]{1,0:T(8,128)S(1)}, f32[34,128]{1,0:T(8,128)S(1)}, u32[]{:S(2)}, u32[]{:S(2)}) collective-permute-start(f32[34,128]{1,0:T(8,128)S(1)} %pad_maximum_fusion.2), channel_id=1, source_target_pairs={{0,1},{1,2},{2,3},{3,4},{4,5},{5,6},{6,7},{7,8},{8,9},{9,10},{10,1... | collective-permute-start | bytes 52232 | tf_op jit(solution)/shard_map/ppermute | solution.py:712
  20.9 6.2 %all-to-all-start.1 = ((f32[64,32,128]{2,1,0:T(8,128)}), f32[64,32,128]{2,1,0:T(8,128)S(1)}, u32[]{:S(2)}, u32[]{:S(2)}) async-start(f32[64,32,128]{2,1,0:T(8,128)} %bitcast.9), calls=%async_computation.1 | async-start | bytes 2097152 | tf_op jit(solution)/shard_map/all_to_all | solution.py:735
  27.3 12.3 %shard_map.144 = (f32[8,256,128]{2,1,0:T(8,128)}, f32[32,64,512]{2,1,0:T(8,128)}, f32[32,64,512]{2,1,0:T(8,128)}, f32[64,512]{1,0:T(8,128)}, f32[64,512]{1,0:T(8...) custom-call(s32[4]{0:T(128)S(1)} %add_convert_fusion.inside_ref, f32[32,64,128]{2,1,0:T(8,128)S(1)} %copy-done.1, ...), custom_call_target="tpu_custom_call" | custom-call | flops 1610612736 | bytes 11534336 | tf_op jit(solution)/shard_map/pallas_call | solution.py:208
  39.6 5.8 %all-to-all-done.1.cot_ref = f32[64,32,128]{2,1,0:T(8,128)S(1)} async-done(((f32[64,32,128]{2,1,0:T(8,128)}), f32[64,32,128]{2,1,0:T(8,128)S(1)}, u32[]{:S(2)}, u32[]{:S(2)}) %all-to-all-start.1) | async-done | bytes 1048608 | tf_op jit(solution)/shard_map/all_to_all | solution.py:735
  45.5 4.8 %all-to-all-start = ((f32[64,32,128]{2,1,0:T(8,128)}), f32[64,32,128]{2,1,0:T(8,128)S(1)}, u32[]{:S(2)}, u32[]{:S(2)}) async-start(f32[64,32,128]{2,1,0:T(8,128)} %bitcast.8), calls=%async_computation | async-start | bytes 2097152 | tf_op jit(solution)/shard_map/all_to_all | solution.py:735
  50.3 16.5 %all-to-all-done.mixed_ref = f32[64,32,128]{2,1,0:T(8,128)S(1)} async-done(((f32[64,32,128]{2,1,0:T(8,128)}), f32[64,32,128]{2,1,0:T(8,128)S(1)}, u32[]{:S(2)}, u32[]{:S(2)}) %all-to-all-start) | async-done | bytes 1048608 | tf_op jit(solution)/shard_map/all_to_all | solution.py:735
  66.9 15.0 %shard_map.145 = (f32[64,32,128]{2,1,0:T(8,128)}, f32[2560,128]{1,0:T(8,128)}, f32[3,2560,128]{2,1,0:T(8,128)}, f32[128,128]{1,0:T(8,128)}) custom-call(f32[64,32,128]{2,1,0:T(8,128)S(1)} %all-to-all-done.mixed_ref, f32[64,32,128]{2,1,0:T(8,128)S(1)} %all-to-all-done.1.cot_ref, f32[128,384]{1,0:T(8,128)S(1)} %copy-done.11, f32[128,128]{1,0:T(8,128)S(1)} %copy-done.7, ...), custom_call_target="tpu_custom_call" | custom-call | flops 3019898880 | bytes 4194304 | tf_op jit(solution)/shard_map/pallas_call | solution.py:375
  81.9 6.0 %all-to-all-start.2 = ((f32[64,32,128]{2,1,0:T(8,128)}), f32[64,32,128]{2,1,0:T(8,128)}, u32[]{:S(2)}, u32[]{:S(2)}) async-start(f32[64,32,128]{2,1,0:T(8,128)} %get-tuple-element.62), calls=%async_computation.2 | async-start | bytes 2097152 | tf_op jit(solution)/shard_map/all_to_all | solution.py:735
  91.3 3.8 %shard_map.146 = (f32[64,32,128]{2,1,0:T(8,128)}, f32[128,384]{1,0:T(8,128)S(1)}, f32[128,128]{1,0:T(8,128)S(1)}) custom-call(f32[64,32,128]{2,1,0:T(8,128)S(1)} %all-to-all-done.mixed_ref, f32[64,32,128]{2,1,0:T(8,128)S(1)} %all-to-all-done.1.cot_ref, f32[2560,128]{1,0:T(8,128)S(1)} %copy-done.3, f32[3,2560,128]{2,1,0:T(8,128)S(1)} %copy-done.2, ...), custom_call_target="tpu_custom_call" | custom-call | flops 1006632960 | bytes 7340032 | tf_op jit(solution)/shard_map/pallas_call | solution.py:421
  95.7 7.9 %all-to-all-done.2 = f32[64,32,128]{2,1,0:T(8,128)} async-done(((f32[64,32,128]{2,1,0:T(8,128)}), f32[64,32,128]{2,1,0:T(8,128)}, u32[]{:S(2)}, u32[]{:S(2)}) %all-to-all-start.2) | async-done | bytes 1048608 | tf_op jit(solution)/shard_map/all_to_all | solution.py:735
  103.7 2.7 %shard_map.147 = (f32[64,512]{1,0:T(8,128)}, f32[64,512]{1,0:T(8,128)}, f32[32,512]{1,0:T(8,128)}, f32[32,512]{1,0:T(8,128)}) custom-call(f32[8,256,128]{2,1,0:T(8,128)} %bitcast.12.came_ref, f32[32,64,128]{2,1,0:T(8,128)} %cot_ref.3, f32[64,512]{1,0:T(8,128)} %get-tuple-element.67.top_ref, f32[64,512]{1,0:T(8,128)} %get-tuple-element.68.bottom_ref, ...), custom_call_target="tpu_custom_call" | custom-call | flops 75497472 | bytes 2097152 | tf_op jit(solution)/shard_map/pallas_call | solution.py:470
  106.7 5.1 %collective-permute-start.5 = (f32[64,512]{1,0:T(8,128)}, f32[64,512]{1,0:T(8,128)S(1)}, u32[]{:S(2)}, u32[]{:S(2)}) collective-permute-start(f32[64,512]{1,0:T(8,128)} %get-tuple-element.72), channel_id=1, source_target_pairs={{0,112},{16,0},{32,16},{48,32},{64,48},{80,64},{96,80},{112,96},{1... | collective-permute-start | bytes 393224 | tf_op jit(solution)/shard_map/ppermute | solution.py:712
  111.7 7.4 %shard_map.148 = (f32[32,64,128]{2,1,0:T(8,128)}, f32[32,64,512]{2,1,0:T(8,128)}, f32[128,512]{1,0:T(8,128)}) custom-call(f32[8,256,128]{2,1,0:T(8,128)} %bitcast.12.came_ref, f32[32,64,128]{2,1,0:T(8,128)} %cot_ref.3, f32[32,64,512]{2,1,0:T(8,128)} %get-tuple-element.73.depth_out_ref, f32[512,128]{1,0:T(8,128)} %weight_ref.5), custom_call_target="tpu_custom_call" | custom-call | flops 1610612736 | bytes 11534336 | tf_op jit(solution)/shard_map/pallas_call | solution.py:516
  119.2 4.3 %collective-permute-start.6 = (f32[34,512]{1,0:T(8,128)S(1)}, f32[34,512]{1,0:T(8,128)S(1)}, u32[]{:S(2)}, u32[]{:S(2)}) collective-permute-start(f32[34,512]{1,0:T(8,128)S(1)} %pad_maximum_fusion), channel_id=1, source_target_pairs={{0,1},{1,2},{2,3},{3,4},{4,5},{5,6},{6,7},{7,8},{8,9},{9,10},{10,1... | collective-permute-start | bytes 208904 | tf_op jit(solution)/shard_map/ppermute | solution.py:712
  125.0 2.5 %collective-permute-done.7.right_ref = f32[34,512]{1,0:T(8,128)S(1)} collective-permute-done((f32[34,512]{1,0:T(8,128)S(1)}, f32[34,512]{1,0:T(8,128)S(1)}, u32[]{:S(2)}, u32[]{:S(2)}) %collective-permute-start.7) | collective-permute-done | bytes 69664 | tf_op jit(solution)/shard_map/ppermute | solution.py:712
  127.5 8.0 %all-to-all-start.3 = ((f32[64,32,128]{2,1,0:T(8,128)}), f32[64,32,128]{2,1,0:T(8,128)S(1)}, u32[]{:S(2)}, u32[]{:S(2)}) async-start(f32[64,32,128]{2,1,0:T(8,128)} %get-tuple-element.93), calls=%async_computation.3 | async-start | bytes 2097152 | tf_op jit(solution)/shard_map/all_to_all | solution.py:735
  135.5 14.7 %shard_map.149 = (f32[32,64,512]{2,1,0:T(8,128)}, f32[2048,128]{1,0:T(8,128)}) custom-call(s32[4]{0:T(128)} %copy-done.10, f32[32,64,512]{2,1,0:T(8,128)} %get-tuple-element.75.grad_ref.before_ref.after_ref, f32[32,64,512]{2,1,0:T(8,128)} %get-tuple-element.75.grad_ref.before_ref.after_ref, f32[32,64,512]{2,1,0:T(8,128)} %get-tuple-element.75.grad_ref.before_ref.after_ref, ...), custom_call_target="tpu_custom_call" | custom-call | flops 805306368 | bytes 13631488 | tf_op jit(solution)/shard_map/pallas_call | solution.py:601
  150.3 3.0 %all-to-all-done.3 = f32[64,32,128]{2,1,0:T(8,128)S(1)} async-done(((f32[64,32,128]{2,1,0:T(8,128)}), f32[64,32,128]{2,1,0:T(8,128)S(1)}, u32[]{:S(2)}, u32[]{:S(2)}) %all-to-all-start.3) | async-done | bytes 1048608 | tf_op jit(solution)/shard_map/all_to_all | solution.py:735
  153.3 25.1 %all_to_all.30.came_ref = f32[128,16,128]{2,1,0:T(8,128)S(1)} all-to-all(f32[128,16,128]{2,1,0:T(8,128)} %bitcast.25), channel_id=1, replica_groups=mesh['row'=8,'ch'=8,'core'=2] {'row','ch','core'}, dimensions={0} | all-to-all | bytes 2097152 | tf_op jit(solution)/shard_map/all_to_all | solution.py:702
  179.5 4.6 %all-to-all-start.5 = ((f32[128,16,128]{2,1,0:T(8,128)}), f32[128,16,128]{2,1,0:T(8,128)S(1)}, u32[]{:S(2)}, u32[]{:S(2)}) async-start(f32[128,16,128]{2,1,0:T(8,128)} %shard_map.151), calls=%async_computation.5 | async-start | bytes 2097152 | tf_op jit(solution)/shard_map/all_to_all | solution.py:704
  184.2 6.5 %shard_map.150 = (f32[32,64,128]{2,1,0:T(8,128)}, f32[32,64,128]{2,1,0:T(8,128)}) custom-call(f32[32,64,512]{2,1,0:T(8,128)} %get-tuple-element.90.grad_pre_ref, f32[32,64,128]{2,1,0:T(8,128)} %field_ref.5, f32[32,64,128]{2,1,0:T(8,128)} %get-tuple-element.91.grad_mixed_ref, f32[8,256,128]{2,1,0:T(8,128)} %get-tuple-element.60.sent_ref, ...), custom_call_target="tpu_custom_call" | custom-call | flops 805306368 | bytes 10485760 | tf_op jit(solution)/shard_map/pallas_call | solution.py:654
  190.6 12.9 %all-to-all-done.5 = f32[128,16,128]{2,1,0:T(8,128)S(1)} async-done(((f32[128,16,128]{2,1,0:T(8,128)}), f32[128,16,128]{2,1,0:T(8,128)S(1)}, u32[]{:S(2)}, u32[]{:S(2)}) %all-to-all-start.5) | async-done | bytes 1048608 | tf_op jit(solution)/shard_map/all_to_all | solution.py:704
  (64 shorter events, 13.6 us)
Async XLA Ops:
  0.6 26.6 %copy-start.4 = (f32[512,128]{1,0:T(8,128)S(1)}, f32[512,128]{1,0:T(8,128)}, u32[]{:S(2)}) copy-start(f32[512,128]{1,0:T(8,128)} %weight_ref.5) | copy-start | bytes 786436
  0.6 26.6 %copy-start.9 = (f32[9,512]{1,0:T(8,128)S(1)}, f32[9,512]{1,0:T(8,128)}, u32[]{:S(2)}) copy-start(f32[9,512]{1,0:T(8,128)} %depth_ref.3) | copy-start | bytes 55300
  1.5 7.0 %collective-permute-start.1 = (f32[64,128]{1,0:T(8,128)S(1)}, f32[64,128]{1,0:T(8,128)S(1)}, u32[]{:S(2)}, u32[]{:S(2)}) collective-permute-start(f32[64,128]{1,0:T(8,128)S(1)} %get-tuple-element.106), channel_id=1, source_target_pairs={{0,112},{16,0},{32,16},{48,32},{64,48},{80,64},{96,80},{112,96},{1... | collective-permute-start | bytes 98312 | tf_op jit(solution)/shard_map/ppermute | solution.py:712
  7.4 6.4 %collective-permute-start = (f32[64,128]{1,0:T(8,128)S(1)}, f32[64,128]{1,0:T(8,128)S(1)}, u32[]{:S(2)}, u32[]{:S(2)}) collective-permute-start(f32[64,128]{1,0:T(8,128)S(1)} %get-tuple-element.107), channel_id=1, source_target_pairs={{0,16},{16,32},{32,48},{48,64},{64,80},{80,96},{96,112},{112,0},{1... | collective-permute-start | bytes 98312 | tf_op jit(solution)/shard_map/ppermute | solution.py:712
  13.8 6.1 %collective-permute-start.2 = (f32[34,128]{1,0:T(8,128)S(1)}, f32[34,128]{1,0:T(8,128)S(1)}, u32[]{:S(2)}, u32[]{:S(2)}) collective-permute-start(f32[34,128]{1,0:T(8,128)S(1)} %pad_maximum_fusion.2), channel_id=1, source_target_pairs={{0,1},{1,2},{2,3},{3,4},{4,5},{5,6},{6,7},{7,8},{8,9},{9,10},{10,1... | collective-permute-start | bytes 52232 | tf_op jit(solution)/shard_map/ppermute | solution.py:712
  17.5 3.4 %collective-permute-start.3 = (f32[34,128]{1,0:T(8,128)S(1)}, f32[34,128]{1,0:T(8,128)S(1)}, u32[]{:S(2)}, u32[]{:S(2)}) collective-permute-start(f32[34,128]{1,0:T(8,128)S(1)} %pad_maximum_fusion.3), channel_id=1, source_target_pairs={{0,15},{1,0},{2,1},{3,2},{4,3},{5,4},{6,5},{7,6},{8,7},{9,8},{10,9... | collective-permute-start | bytes 52232 | tf_op jit(solution)/shard_map/ppermute | solution.py:712
  20.9 24.5 %all-to-all-start.1 = ((f32[64,32,128]{2,1,0:T(8,128)}), f32[64,32,128]{2,1,0:T(8,128)S(1)}, u32[]{:S(2)}, u32[]{:S(2)}) async-start(f32[64,32,128]{2,1,0:T(8,128)} %bitcast.9), calls=%async_computation.1 | async-start | bytes 2097152 | tf_op jit(solution)/shard_map/all_to_all | solution.py:735
  27.1 23.1 %copy-start.15 = (f32[4,64,64]{2,1,0:T(8,128)S(1)}, f32[4,64,64]{2,1,0:T(8,128)}, u32[]{:S(2)}) copy-start(f32[4,64,64]{2,1,0:T(8,128)} %param.14) | copy-start | bytes 196612
  27.1 39.7 %copy-start.7 = (f32[128,128]{1,0:T(8,128)S(1)}, f32[128,128]{1,0:T(8,128)}, u32[]{:S(2)}) copy-start(f32[128,128]{1,0:T(8,128)} %out_ref.3) | copy-start | bytes 196612
  27.2 39.7 %copy-start.11 = (f32[128,384]{1,0:T(8,128)S(1)}, f32[128,384]{1,0:T(8,128)}, u32[]{:S(2)}) copy-start(f32[128,384]{1,0:T(8,128)} %qkv_ref.1) | copy-start | bytes 589828
  27.3 54.6 %copy-start.10 = (s32[4]{0:T(128)}, s32[4]{0:T(128)S(1)}, u32[]{:S(2)}) copy-start(s32[4]{0:T(128)S(1)} %add_convert_fusion.inside_ref) | copy-start | bytes 52
  45.5 21.4 %all-to-all-start = ((f32[64,32,128]{2,1,0:T(8,128)}), f32[64,32,128]{2,1,0:T(8,128)S(1)}, u32[]{:S(2)}, u32[]{:S(2)}) async-start(f32[64,32,128]{2,1,0:T(8,128)} %bitcast.8), calls=%async_computation | async-start | bytes 2097152 | tf_op jit(solution)/shard_map/all_to_all | solution.py:735
  81.9 21.8 %all-to-all-start.2 = ((f32[64,32,128]{2,1,0:T(8,128)}), f32[64,32,128]{2,1,0:T(8,128)}, u32[]{:S(2)}, u32[]{:S(2)}) async-start(f32[64,32,128]{2,1,0:T(8,128)} %get-tuple-element.62), calls=%async_computation.2 | async-start | bytes 2097152 | tf_op jit(solution)/shard_map/all_to_all | solution.py:735
  95.7 23.4 %copy-start.8 = (f32[128,128]{1,0:T(8,128)}, f32[128,128]{1,0:T(8,128)S(1)}, u32[]{:S(2)}) copy-start(f32[128,128]{1,0:T(8,128)S(1)} %get-tuple-element.88.out_ref) | copy-start | bytes 196612
  106.4 17.1 %copy-start.18 = (f32[32,512]{1,0:T(8,128)S(1)}, f32[32,512]{1,0:T(8,128)}, u32[]{:S(2)}) copy-start(f32[32,512]{1,0:T(8,128)} %get-tuple-element.79) | copy-start | bytes 196612
  106.4 12.7 %collective-permute-start.4 = (f32[64,512]{1,0:T(8,128)}, f32[64,512]{1,0:T(8,128)S(1)}, u32[]{:S(2)}, u32[]{:S(2)}) collective-permute-start(f32[64,512]{1,0:T(8,128)} %get-tuple-element.71), channel_id=1, source_target_pairs={{0,16},{16,32},{32,48},{48,64},{64,80},{80,96},{96,112},{112,0},{1... | collective-permute-start | bytes 393224 | tf_op jit(solution)/shard_map/ppermute | solution.py:712
  106.7 12.5 %collective-permute-start.5 = (f32[64,512]{1,0:T(8,128)}, f32[64,512]{1,0:T(8,128)S(1)}, u32[]{:S(2)}, u32[]{:S(2)}) collective-permute-start(f32[64,512]{1,0:T(8,128)} %get-tuple-element.72), channel_id=1, source_target_pairs={{0,112},{16,0},{32,16},{48,32},{64,48},{80,64},{96,80},{112,96},{1... | collective-permute-start | bytes 393224 | tf_op jit(solution)/shard_map/ppermute | solution.py:712
  119.1 16.4 %copy-start.13 = (f32[64,512]{1,0:T(8,128)}, f32[64,512]{1,0:T(8,128)S(1)}, u32[]{:S(2)}) copy-start(f32[64,512]{1,0:T(8,128)S(1)} %collective-permute-done.4.top) | copy-start | bytes 393220
  119.1 16.4 %copy-start.14 = (f32[64,512]{1,0:T(8,128)}, f32[64,512]{1,0:T(8,128)S(1)}, u32[]{:S(2)}) copy-start(f32[64,512]{1,0:T(8,128)S(1)} %collective-permute-done.5.bottom) | copy-start | bytes 393220
  119.2 5.8 %collective-permute-start.6 = (f32[34,512]{1,0:T(8,128)S(1)}, f32[34,512]{1,0:T(8,128)S(1)}, u32[]{:S(2)}, u32[]{:S(2)}) collective-permute-start(f32[34,512]{1,0:T(8,128)S(1)} %pad_maximum_fusion), channel_id=1, source_target_pairs={{0,1},{1,2},{2,3},{3,4},{4,5},{5,6},{6,7},{7,8},{8,9},{9,10},{10,1... | collective-permute-start | bytes 208904 | tf_op jit(solution)/shard_map/ppermute | solution.py:712
  123.5 3.9 %collective-permute-start.7 = (f32[34,512]{1,0:T(8,128)S(1)}, f32[34,512]{1,0:T(8,128)S(1)}, u32[]{:S(2)}, u32[]{:S(2)}) collective-permute-start(f32[34,512]{1,0:T(8,128)S(1)} %pad_maximum_fusion.1), channel_id=1, source_target_pairs={{0,15},{1,0},{2,1},{3,2},{4,3},{5,4},{6,5},{7,6},{8,7},{9,8},{10,9... | collective-permute-start | bytes 208904 | tf_op jit(solution)/shard_map/ppermute | solution.py:712
  127.5 25.8 %all-to-all-start.3 = ((f32[64,32,128]{2,1,0:T(8,128)}), f32[64,32,128]{2,1,0:T(8,128)S(1)}, u32[]{:S(2)}, u32[]{:S(2)}) async-start(f32[64,32,128]{2,1,0:T(8,128)} %get-tuple-element.93), calls=%async_computation.3 | async-start | bytes 2097152 | tf_op jit(solution)/shard_map/all_to_all | solution.py:735
  153.3 30.9 %copy-start.12 = (f32[64,32,128]{2,1,0:T(8,128)}, f32[64,32,128]{2,1,0:T(8,128)S(1)}, u32[]{:S(2)}) copy-start(f32[64,32,128]{2,1,0:T(8,128)S(1)} %all-to-all-done.3) | copy-start | bytes 3145732
  179.5 24.0 %all-to-all-start.5 = ((f32[128,16,128]{2,1,0:T(8,128)}), f32[128,16,128]{2,1,0:T(8,128)S(1)}, u32[]{:S(2)}, u32[]{:S(2)}) async-start(f32[128,16,128]{2,1,0:T(8,128)} %shard_map.151), calls=%async_computation.5 | async-start | bytes 2097152 | tf_op jit(solution)/shard_map/all_to_all | solution.py:704
  (9 other events, 53.6 us)

commit v5 on v4

--- a/solution.py
+++ b/solution.py
@@ -528,26 +528,23 @@
 SLOTS = 16
 
 
-def pack(refs, taps_ref, packed_ref):
-    size = refs[0].shape[0]
+def pack(refs, taps_ref, target, half):
+    size = refs[0].shape[0] // 2
+    own = pl.ds(pl.multiple_of(half * size, size), size)
     slot = 0
     for ref in refs:
-        for lane in range(0, ref.shape[1], size):
-            packed_ref[pl.ds(slot, size, stride=SLOTS), :] = ref[:, lane : lane + size]
+        for lane in range(0, ref.shape[1], 2 * size):
+            target[pl.ds(slot, size, stride=SLOTS), :] = ref[own, lane : lane + 2 * size]
             slot += 1
-    taps = taps_ref.shape[0]
-    empty = jnp.zeros((size, size), F32)
-    packed_ref[pl.ds(slot, size, stride=SLOTS), :] = empty
-    for k in range(taps_ref.shape[1] // size):
-        packed_ref[pl.ds(slot + SLOTS * taps * k, taps, stride=SLOTS), :] = taps_ref[:, k * size : (k + 1) * size]
+    target[pl.ds(slot, size, stride=SLOTS), :] = taps_ref[own, :]
     for spare in range(slot + 1, SLOTS):
-        packed_ref[pl.ds(spare, size, stride=SLOTS), :] = empty
+        target[pl.ds(spare, size, stride=SLOTS), :] = jnp.zeros((size, 2 * size), F32)
 
 
 def expand_back_body(
     inside_ref, grad_ref, before_ref, after_ref, top, bottom, left_ref, right_ref, pre_ref, field_ref, depth_ref,
     project_ref, qkv_ref, out_ref, bias_ref,
-    grad_pre_ref, packed_ref, padded, left, right, grad_expand_ref, grad_depth_ref,
+    grad_pre_ref, kept_ref, given_ref, padded, left, right, grad_expand_ref, grad_depth_ref, taps_ref,
 ):
     step = pl.program_id(0)
     last = pl.num_programs(0) - 1
@@ -591,7 +588,13 @@
 
     @pl.when(step == last)
     def _():
-        pack((grad_expand_ref, project_ref, qkv_ref, out_ref, bias_ref), grad_depth_ref, packed_ref)
+        taps_ref[...] = jnp.zeros_like(taps_ref)
+        taps, size = grad_depth_ref.shape[0], taps_ref.shape[1]
+        for k in range(wide // size):
+            taps_ref[k * taps : (k + 1) * taps, :] = grad_depth_ref[:, k * size : (k + 1) * size]
+        refs = (grad_expand_ref, project_ref, qkv_ref, out_ref, bias_ref)
+        pack(refs, taps_ref, kept_ref, inside_ref[4])
+        pack(refs, taps_ref, given_ref, 1 - inside_ref[4])
 
 
 def expand_back(flags, grad_depth_out, halo, pre, field, depth_weight, grads, count=8):
@@ -611,14 +614,15 @@
         + [whole(edge, wide)] * 2
         + [rows(count, tile_cols, wide), rows(count, tile_cols, channels), whole(9, wide)]
         + [whole(*a.shape) for a in grads],
-        [rows(count, tile_cols, wide), whole(channels * SLOTS, channels)],
-        [pltpu.HBM((tile_rows, tile_cols, wide), F32), shape(channels * SLOTS, channels)],
+        [rows(count, tile_cols, wide)] + [whole(channels // 2 * SLOTS, channels)] * 2,
+        [pltpu.HBM((tile_rows, tile_cols, wide), F32)] + [shape(channels // 2 * SLOTS, channels)] * 2,
         scratch=[
             pltpu.VMEM((count + 2, tile_cols + 16, wide), F32),
             pltpu.VMEM((edge, wide), F32),
             pltpu.VMEM((edge, wide), F32),
             pltpu.VMEM((channels, wide), F32),
             pltpu.VMEM((16, wide), F32),
+            pltpu.VMEM((channels, channels), F32),
         ],
         flops=6 * tile_rows * tile_cols * channels * wide,
         bytes_accessed=4 * tile_rows * tile_cols * (3 * wide + channels),
@@ -668,12 +672,15 @@
     total_ref[...] = jnp.broadcast_to(total, total_ref.shape)
 
 
-def unpack_body(packed_ref, expand_ref, project_ref, qkv_ref, out_ref, bias_ref, depth_ref):
+def unpack_body(inside_ref, mine_ref, other_ref, expand_ref, project_ref, qkv_ref, out_ref, bias_ref, depth_ref):
     size = out_ref.shape[0]
     places = bias_ref.shape[1]
 
-    def matrix(slot, count=size, first=0):
-        return packed_ref[pl.ds(slot + SLOTS * first, count, stride=SLOTS), :]
+    def matrix(slot):
+        here = pl.ds(slot, size // 2, stride=SLOTS)
+        mine, other = mine_ref[here, :], other_ref[here, :]
+        second = inside_ref[4] > 0
+        return jnp.concatenate([jnp.where(second, other, mine), jnp.where(second, mine, other)], axis=0)
 
     slot = 0
     for k in range(expand_ref.shape[1] // size):
@@ -690,22 +697,31 @@
     for h in range(HEADS):
         at, lane = divmod(h, 2)
         bias_ref[h] = bias[at * places : (at + 1) * places, lane * places : (lane + 1) * places].T
-    taps = 16
+    taps = matrix(slot + 2)
     for k in range(depth_ref.shape[1] // size):
-        depth_ref[:, k * size : (k + 1) * size] = matrix(slot + 2, taps, taps * k)[: depth_ref.shape[0]]
-
-
-def reduce_all(packed, like, after):
-    size = packed.shape[1]
+        depth_ref[:, k * size : (k + 1) * size] = taps[16 * k : 16 * k + depth_ref.shape[0]]
+
+
+def reduce_all(flags, kept, given, like, after, beside):
+    size = kept.shape[1]
+    chips = size // 2
     vmem = pl.BlockSpec(memory_space=pltpu.VMEM)
-    packed, after = lax.optimization_barrier((packed, after))
-    came = lax.all_to_all(packed.reshape(size, SLOTS, size), ALL, 0, 0, tiled=True)
-    total = call(total_body, (), [vmem], vmem, shape(size, SLOTS, size))(came)
-    came = lax.all_to_all(total, ALL, 0, 0, tiled=True)
-    totals = call(unpack_body, (), [vmem], [vmem] * 6, [shape(*a.shape) for a in like])(
-        came.reshape(size * SLOTS, size)
-    )
-    return totals, after
+    pair = [(0, 1), (1, 0)]
+    own = kept + lax.ppermute(given, "core", pair)
+    own, after = lax.optimization_barrier((own, after))
+    came = lax.all_to_all(own.reshape(chips, SLOTS, size), PAIRS, 0, 0, tiled=True)
+    total = call(total_body, (), [vmem], vmem, shape(chips, SLOTS, size))(came)
+    mine = lax.all_to_all(total, PAIRS, 0, 0, tiled=True).reshape(chips * SLOTS, size)
+    mine, others = lax.optimization_barrier((mine, beside(after)))
+    other = lax.ppermute(mine, "core", pair)
+    totals = call(
+        unpack_body,
+        (),
+        [pl.BlockSpec(memory_space=pltpu.SMEM), vmem, vmem],
+        [vmem] * 6,
+        [shape(*a.shape) for a in like],
+    )(flags, mine, other)
+    return totals, others
 
 
 def shift(values, axes, count, by):
@@ -714,7 +730,8 @@
 
 def inside(row_count, col_count):
     row, col = lax.axis_index("row"), lax.axis_index(COLS)
-    return jnp.stack([row > 0, row < row_count - 1, col > 0, col < col_count - 1]).astype(jnp.int32)
+    second = lax.axis_index("core") > 0
+    return jnp.stack([row > 0, row < row_count - 1, col > 0, col < col_count - 1, second]).astype(jnp.int32)
 
 
 def beyond_rows(first, last, row_count):
@@ -760,16 +777,18 @@
     halo += beyond_columns(*halo, left, right, col_count)
     halo, attended = lax.optimization_barrier((halo, attended))
     placed = swap(attended).reshape(sent.shape)
-    grad_pre, packed = expand_back(
+    grad_pre, kept, given = expand_back(
         flags, grad_depth_out, halo, pre, field, depth_weight, (grad_project, grad_qkv, grad_out, grad_bias)
     )
-    totals, placed = reduce_all(
-        packed,
+    totals, (block_out, grad_field) = reduce_all(
+        flags,
+        kept,
+        given,
         (expand_weight, project_weight, qkv_weight, out_weight, pos_bias, depth_weight),
         placed,
+        lambda placed: finish(grad_pre, field, grad_mixed, sent, placed, expand_weight),
     )
     grad_expand, grad_project, grad_qkv, grad_out, grad_bias, grad_depth = totals
-    block_out, grad_field = finish(grad_pre, field, grad_mixed, sent, placed, expand_weight)
     return (
         block_out,
         grad_field,

time: 206 us -> 199 us (0.966)
  waiting for transfers between devices: 56.4 us -> 48.5 us
  starting transfers between devices: 49 us -> 52.6 us
  blocking collectives: 25.1 us -> 21.7 us
    all_to_all x1, waiting for transfers between devices: 12.9 us -> 4.32 us  [reduce_all(): lax.all_to_all(total, PAIRS, 0, 0, tiled=True).reshape(chips * SLOTS, size)]
    ppermute x0 -> x2, waiting for transfers between devices: none -> 3.64 us  [the longest x1 2.11 us: reduce_all(): own = kept + lax.ppermute(given, 'core', pair)]
    all_to_all x1, blocking collectives: 25.1 us -> 21.7 us  [reduce_all(): lax.all_to_all(own.reshape(chips, SLOTS, size), PAIRS, 0, 0, tiled=True)]
    ppermute x0 -> x2, starting transfers between devices: none -> 3.3 us  [the longest x1 3.22 us: reduce_all(): other = lax.ppermute(mine, 'core', pair)]
    all_to_all x4, waiting for transfers between devices: 33.3 us -> 30.2 us  [swap(): return lax.all_to_all(flat, PAIRS, 0, 0, tiled=True)]
    unnamed x40 -> x42, local copies, waits for them, and re-layouts: 5.4 us -> 5.4 us
  transfers between devices with their start and end apart: 13 -> 15, of which waited for: 9 -> 10; matrix products, arithmetic and copies ran while one was open for 1% -> 1% of each run, Pallas kernels for 22% -> 23%
where the time goes in v5:
time: 199 us; the launch traced here: 198 us
  Pallas kernels  66.1 us (33%)
  starting transfers between devices  52.6 us (26%)
  waiting for transfers between devices  48.5 us (24%)
  blocking collectives  21.7 us (11%)
  local copies, waits for them, and re-layouts  7.42 us (4%)
    all_to_all x4, waiting for transfers between devices, swap(): return lax.all_to_all(flat, PAIRS, 0, 0, tiled=True)  30.2 us
    all_to_all x4, starting transfers between devices, swap(): return lax.all_to_all(flat, PAIRS, 0, 0, tiled=True)  25 us
    all_to_all x1, blocking collectives, reduce_all(): lax.all_to_all(own.reshape(chips, SLOTS, size), PAIRS, 0, 0, tiled=True)  21.7 us
    ppermute x8, starting transfers between devices, shift(): lax.ppermute(values, axes, [(i, (i + by) % count) for i in range(count)])  19.4 us
    pallas_call x1, Pallas kernels, attend(): call(attend_body, (), [vmem] * 5, [vmem] + [pl.BlockSpec(memory_space=pl....  15 us
    pallas_call x1, Pallas kernels, expand_back(): call(expand_back_body, (tile_rows // count,), [pl.BlockSpec(memory_space=...  14.7 us
    pallas_call x1, Pallas kernels, forward(): call(forward_body, (steps + 1,), [pl.BlockSpec(memory_space=pltpu.SMEM),...  12.4 us
    ppermute x8, waiting for transfers between devices, shift(): lax.ppermute(values, axes, [(i, (i + by) % count) for i in range(count)])  10.3 us
  transfers between devices with their start and end apart: 15, of which 10 were waited for; matrix products, arithmetic and copies ran while one was open for 1% of the time, Pallas kernels for 23%

profile of v5, /device:TPU:1, one launch (start us, length us, event | category | flops | bytes accessed | tf_op | source)
XLA Modules:
  0.0 198.4 jit_solution(5036280913995296573)
XLA Ops:
  1.5 5.9 %collective-permute-start.1 = (f32[64,128]{1,0:T(8,128)S(1)}, f32[64,128]{1,0:T(8,128)S(1)}, u32[]{:S(2)}, u32[]{:S(2)}) collective-permute-start(f32[64,128]{1,0:T(8,128)S(1)} %get-tuple-element.114), channel_id=1, source_target_pairs={{0,112},{16,0},{32,16},{48,32},{64,48},{80,64},{96,80},{112,96},{1... | collective-permute-start | bytes 98312 | tf_op jit(solution)/shard_map/ppermute | solution.py:728
  8.4 5.3 %collective-permute-done.top_ref = f32[64,128]{1,0:T(8,128)S(1)} collective-permute-done((f32[64,128]{1,0:T(8,128)S(1)}, f32[64,128]{1,0:T(8,128)S(1)}, u32[]{:S(2)}, u32[]{:S(2)}) %collective-permute-start) | collective-permute-done | bytes 32800 | tf_op jit(solution)/shard_map/ppermute | solution.py:728
  13.8 3.7 %collective-permute-start.2 = (f32[34,128]{1,0:T(8,128)S(1)}, f32[34,128]{1,0:T(8,128)S(1)}, u32[]{:S(2)}, u32[]{:S(2)}) collective-permute-start(f32[34,128]{1,0:T(8,128)S(1)} %pad_maximum_fusion.2), channel_id=1, source_target_pairs={{0,1},{1,2},{2,3},{3,4},{4,5},{5,6},{6,7},{7,8},{8,9},{9,10},{10,1... | collective-permute-start | bytes 52232 | tf_op jit(solution)/shard_map/ppermute | solution.py:728
  20.9 6.2 %all-to-all-start.1 = ((f32[64,32,128]{2,1,0:T(8,128)}), f32[64,32,128]{2,1,0:T(8,128)S(1)}, u32[]{:S(2)}, u32[]{:S(2)}) async-start(f32[64,32,128]{2,1,0:T(8,128)} %bitcast.10), calls=%async_computation.1 | async-start | bytes 2097152 | tf_op jit(solution)/shard_map/all_to_all | solution.py:752
  27.3 12.4 %shard_map.144 = (f32[8,256,128]{2,1,0:T(8,128)}, f32[32,64,512]{2,1,0:T(8,128)}, f32[32,64,512]{2,1,0:T(8,128)}, f32[64,512]{1,0:T(8,128)}, f32[64,512]{1,0:T(8...) custom-call(s32[5]{0:T(128)S(1)} %convert_element_type.3.inside_ref, f32[32,64,128]{2,1,0:T(8,128)S(1)} %copy-done.1, ...), custom_call_target="tpu_custom_call" | custom-call | flops 1610612736 | bytes 11534336 | tf_op jit(solution)/shard_map/pallas_call | solution.py:208
  39.7 5.8 %all-to-all-done.1.cot_ref = f32[64,32,128]{2,1,0:T(8,128)S(1)} async-done(((f32[64,32,128]{2,1,0:T(8,128)}), f32[64,32,128]{2,1,0:T(8,128)S(1)}, u32[]{:S(2)}, u32[]{:S(2)}) %all-to-all-start.1) | async-done | bytes 1048608 | tf_op jit(solution)/shard_map/all_to_all | solution.py:752
  45.5 4.8 %all-to-all-start = ((f32[64,32,128]{2,1,0:T(8,128)}), f32[64,32,128]{2,1,0:T(8,128)S(1)}, u32[]{:S(2)}, u32[]{:S(2)}) async-start(f32[64,32,128]{2,1,0:T(8,128)} %bitcast.9), calls=%async_computation | async-start | bytes 2097152 | tf_op jit(solution)/shard_map/all_to_all | solution.py:752
  50.3 16.5 %all-to-all-done.mixed_ref = f32[64,32,128]{2,1,0:T(8,128)S(1)} async-done(((f32[64,32,128]{2,1,0:T(8,128)}), f32[64,32,128]{2,1,0:T(8,128)S(1)}, u32[]{:S(2)}, u32[]{:S(2)}) %all-to-all-start) | async-done | bytes 1048608 | tf_op jit(solution)/shard_map/all_to_all | solution.py:752
  66.9 15.0 %shard_map.145 = (f32[64,32,128]{2,1,0:T(8,128)}, f32[2560,128]{1,0:T(8,128)}, f32[3,2560,128]{2,1,0:T(8,128)}, f32[128,128]{1,0:T(8,128)}) custom-call(f32[64,32,128]{2,1,0:T(8,128)S(1)} %all-to-all-done.mixed_ref, f32[64,32,128]{2,1,0:T(8,128)S(1)} %all-to-all-done.1.cot_ref, f32[128,384]{1,0:T(8,128)S(1)} %copy-done.12, f32[128,128]{1,0:T(8,128)S(1)} %copy-done.7, ...), custom_call_target="tpu_custom_call" | custom-call | flops 3019898880 | bytes 4194304 | tf_op jit(solution)/shard_map/pallas_call | solution.py:375
  81.9 5.9 %all-to-all-start.2 = ((f32[64,32,128]{2,1,0:T(8,128)}), f32[64,32,128]{2,1,0:T(8,128)}, u32[]{:S(2)}, u32[]{:S(2)}) async-start(f32[64,32,128]{2,1,0:T(8,128)} %get-tuple-element.66), calls=%async_computation.2 | async-start | bytes 2097152 | tf_op jit(solution)/shard_map/all_to_all | solution.py:752
  91.3 3.8 %shard_map.146 = (f32[64,32,128]{2,1,0:T(8,128)}, f32[128,384]{1,0:T(8,128)S(1)}, f32[128,128]{1,0:T(8,128)S(1)}) custom-call(f32[64,32,128]{2,1,0:T(8,128)S(1)} %all-to-all-done.mixed_ref, f32[64,32,128]{2,1,0:T(8,128)S(1)} %all-to-all-done.1.cot_ref, f32[2560,128]{1,0:T(8,128)S(1)} %copy-done.3, f32[3,2560,128]{2,1,0:T(8,128)S(1)} %copy-done.2, ...), custom_call_target="tpu_custom_call" | custom-call | flops 1006632960 | bytes 7340032 | tf_op jit(solution)/shard_map/pallas_call | solution.py:421
  95.8 7.9 %all-to-all-done.2 = f32[64,32,128]{2,1,0:T(8,128)} async-done(((f32[64,32,128]{2,1,0:T(8,128)}), f32[64,32,128]{2,1,0:T(8,128)}, u32[]{:S(2)}, u32[]{:S(2)}) %all-to-all-start.2) | async-done | bytes 1048608 | tf_op jit(solution)/shard_map/all_to_all | solution.py:752
  103.7 2.7 %shard_map.147 = (f32[64,512]{1,0:T(8,128)}, f32[64,512]{1,0:T(8,128)}, f32[32,512]{1,0:T(8,128)}, f32[32,512]{1,0:T(8,128)}) custom-call(f32[8,256,128]{2,1,0:T(8,128)} %bitcast.13.came_ref, f32[32,64,128]{2,1,0:T(8,128)} %cot_ref.3, f32[64,512]{1,0:T(8,128)} %get-tuple-element.71.top_ref, f32[64,512]{1,0:T(8,128)} %get-tuple-element.72.bottom_ref, ...), custom_call_target="tpu_custom_call" | custom-call | flops 75497472 | bytes 2097152 | tf_op jit(solution)/shard_map/pallas_call | solution.py:470
  106.7 5.1 %collective-permute-start.5 = (f32[64,512]{1,0:T(8,128)}, f32[64,512]{1,0:T(8,128)S(1)}, u32[]{:S(2)}, u32[]{:S(2)}) collective-permute-start(f32[64,512]{1,0:T(8,128)} %get-tuple-element.76), channel_id=1, source_target_pairs={{0,112},{16,0},{32,16},{48,32},{64,48},{80,64},{96,80},{112,96},{1... | collective-permute-start | bytes 393224 | tf_op jit(solution)/shard_map/ppermute | solution.py:728
  111.7 7.4 %shard_map.148 = (f32[32,64,128]{2,1,0:T(8,128)}, f32[32,64,512]{2,1,0:T(8,128)}, f32[128,512]{1,0:T(8,128)}) custom-call(f32[8,256,128]{2,1,0:T(8,128)} %bitcast.13.came_ref, f32[32,64,128]{2,1,0:T(8,128)} %cot_ref.3, f32[32,64,512]{2,1,0:T(8,128)} %get-tuple-element.77.depth_out_ref, f32[512,128]{1,0:T(8,128)} %weight_ref.5), custom_call_target="tpu_custom_call" | custom-call | flops 1610612736 | bytes 11534336 | tf_op jit(solution)/shard_map/pallas_call | solution.py:516
  119.2 4.3 %collective-permute-start.6 = (f32[34,512]{1,0:T(8,128)S(1)}, f32[34,512]{1,0:T(8,128)S(1)}, u32[]{:S(2)}, u32[]{:S(2)}) collective-permute-start(f32[34,512]{1,0:T(8,128)S(1)} %pad_maximum_fusion), channel_id=1, source_target_pairs={{0,1},{1,2},{2,3},{3,4},{4,5},{5,6},{6,7},{7,8},{8,9},{9,10},{10,1... | collective-permute-start | bytes 208904 | tf_op jit(solution)/shard_map/ppermute | solution.py:728
  125.0 2.5 %collective-permute-done.7.right_ref = f32[34,512]{1,0:T(8,128)S(1)} collective-permute-done((f32[34,512]{1,0:T(8,128)S(1)}, f32[34,512]{1,0:T(8,128)S(1)}, u32[]{:S(2)}, u32[]{:S(2)}) %collective-permute-start.7) | collective-permute-done | bytes 69664 | tf_op jit(solution)/shard_map/ppermute | solution.py:728
  127.5 8.0 %all-to-all-start.3 = ((f32[64,32,128]{2,1,0:T(8,128)}), f32[64,32,128]{2,1,0:T(8,128)S(1)}, u32[]{:S(2)}, u32[]{:S(2)}) async-start(f32[64,32,128]{2,1,0:T(8,128)} %get-tuple-element.96), calls=%async_computation.3 | async-start | bytes 2097152 | tf_op jit(solution)/shard_map/all_to_all | solution.py:752
  135.5 14.7 %shard_map.149 = (f32[32,64,512]{2,1,0:T(8,128)}, f32[1024,128]{1,0:T(8,128)}, f32[1024,128]{1,0:T(8,128)}) custom-call(s32[5]{0:T(128)} %copy-done.10, f32[32,64,512]{2,1,0:T(8,128)} %get-tuple-element.79.grad_ref.before_ref.after_ref, f32[32,64,512]{2,1,0:T(8,128)} %get-tuple-element.79.grad_ref.before_ref.after_ref, ...), custom_call_target="tpu_custom_call" | custom-call | flops 805306368 | bytes 13631488 | tf_op jit(solution)/shard_map/pallas_call | solution.py:604
  153.6 21.7 %all_to_all.30.came_ref = f32[64,16,128]{2,1,0:T(8,128)S(1)} all-to-all(f32[64,16,128]{2,1,0:T(8,128)S(1)} %bitcast.27), channel_id=1, replica_groups=mesh['row'=8,'ch'=8,'core'=2] {'row','ch'}, dimensions={0} | all-to-all | bytes 1048576 | tf_op jit(solution)/shard_map/all_to_all | solution.py:712
  176.2 4.9 %all-to-all-start.5 = ((f32[64,16,128]{2,1,0:T(8,128)}), f32[64,16,128]{2,1,0:T(8,128)S(1)}, u32[]{:S(2)}, u32[]{:S(2)}) async-start(f32[64,16,128]{2,1,0:T(8,128)} %shard_map.150), calls=%async_computation.5 | async-start | bytes 1048576 | tf_op jit(solution)/shard_map/all_to_all | solution.py:714
  181.1 6.5 %shard_map.151 = (f32[32,64,128]{2,1,0:T(8,128)}, f32[32,64,128]{2,1,0:T(8,128)}) custom-call(f32[32,64,512]{2,1,0:T(8,128)} %get-tuple-element.98.grad_pre_ref, f32[32,64,128]{2,1,0:T(8,128)} %field_ref.5, f32[32,64,128]{2,1,0:T(8,128)} %get-tuple-element.99.grad_mixed_ref, f32[8,256,128]{2,1,0:T(8,128)} %get-tuple-element.64.sent_ref, ...), custom_call_target="tpu_custom_call" | custom-call | flops 805306368 | bytes 10485760 | tf_op jit(solution)/shard_map/pallas_call | solution.py:658
  187.6 4.3 %all-to-all-done.5 = f32[64,16,128]{2,1,0:T(8,128)S(1)} async-done(((f32[64,16,128]{2,1,0:T(8,128)}), f32[64,16,128]{2,1,0:T(8,128)S(1)}, u32[]{:S(2)}, u32[]{:S(2)}) %all-to-all-start.5) | async-done | bytes 524320 | tf_op jit(solution)/shard_map/all_to_all | solution.py:714
  192.0 3.2 %collective-permute-start.9 = (f32[1024,128]{1,0:T(8,128)S(1)}, f32[1024,128]{1,0:T(8,128)S(1)}, u32[]{:S(2)}, u32[]{:S(2)}) collective-permute-start(f32[1024,128]{1,0:T(8,128)S(1)} %bitcast.24), channel_id=1, source_target_pairs={{0,1},{1,0},{2,3},{3,2},{4,5},{5,4},{6,7},{7,6},{8,9},{9,8},{10,11... | collective-permute-start | bytes 1572872 | tf_op jit(solution)/shard_map/ppermute | solution.py:716
  (72 shorter events, 18.8 us)
Async XLA Ops:
  0.6 26.7 %copy-start.4 = (f32[512,128]{1,0:T(8,128)S(1)}, f32[512,128]{1,0:T(8,128)}, u32[]{:S(2)}) copy-start(f32[512,128]{1,0:T(8,128)} %weight_ref.5) | copy-start | bytes 786436
  0.6 26.7 %copy-start.9 = (f32[9,512]{1,0:T(8,128)S(1)}, f32[9,512]{1,0:T(8,128)}, u32[]{:S(2)}) copy-start(f32[9,512]{1,0:T(8,128)} %depth_ref.3) | copy-start | bytes 55300
  1.5 7.0 %collective-permute-start.1 = (f32[64,128]{1,0:T(8,128)S(1)}, f32[64,128]{1,0:T(8,128)S(1)}, u32[]{:S(2)}, u32[]{:S(2)}) collective-permute-start(f32[64,128]{1,0:T(8,128)S(1)} %get-tuple-element.114), channel_id=1, source_target_pairs={{0,112},{16,0},{32,16},{48,32},{64,48},{80,64},{96,80},{112,96},{1... | collective-permute-start | bytes 98312 | tf_op jit(solution)/shard_map/ppermute | solution.py:728
  7.4 6.4 %collective-permute-start = (f32[64,128]{1,0:T(8,128)S(1)}, f32[64,128]{1,0:T(8,128)S(1)}, u32[]{:S(2)}, u32[]{:S(2)}) collective-permute-start(f32[64,128]{1,0:T(8,128)S(1)} %get-tuple-element.115), channel_id=1, source_target_pairs={{0,16},{16,32},{32,48},{48,64},{64,80},{80,96},{96,112},{112,0},{1... | collective-permute-start | bytes 98312 | tf_op jit(solution)/shard_map/ppermute | solution.py:728
  13.8 6.1 %collective-permute-start.2 = (f32[34,128]{1,0:T(8,128)S(1)}, f32[34,128]{1,0:T(8,128)S(1)}, u32[]{:S(2)}, u32[]{:S(2)}) collective-permute-start(f32[34,128]{1,0:T(8,128)S(1)} %pad_maximum_fusion.2), channel_id=1, source_target_pairs={{0,1},{1,2},{2,3},{3,4},{4,5},{5,6},{6,7},{7,8},{8,9},{9,10},{10,1... | collective-permute-start | bytes 52232 | tf_op jit(solution)/shard_map/ppermute | solution.py:728
  17.5 3.4 %collective-permute-start.3 = (f32[34,128]{1,0:T(8,128)S(1)}, f32[34,128]{1,0:T(8,128)S(1)}, u32[]{:S(2)}, u32[]{:S(2)}) collective-permute-start(f32[34,128]{1,0:T(8,128)S(1)} %pad_maximum_fusion.3), channel_id=1, source_target_pairs={{0,15},{1,0},{2,1},{3,2},{4,3},{5,4},{6,5},{7,6},{8,7},{9,8},{10,9... | collective-permute-start | bytes 52232 | tf_op jit(solution)/shard_map/ppermute | solution.py:728
  20.9 24.5 %all-to-all-start.1 = ((f32[64,32,128]{2,1,0:T(8,128)}), f32[64,32,128]{2,1,0:T(8,128)S(1)}, u32[]{:S(2)}, u32[]{:S(2)}) async-start(f32[64,32,128]{2,1,0:T(8,128)} %bitcast.10), calls=%async_computation.1 | async-start | bytes 2097152 | tf_op jit(solution)/shard_map/all_to_all | solution.py:752
  27.1 23.1 %copy-start.16 = (f32[4,64,64]{2,1,0:T(8,128)S(1)}, f32[4,64,64]{2,1,0:T(8,128)}, u32[]{:S(2)}) copy-start(f32[4,64,64]{2,1,0:T(8,128)} %param.14) | copy-start | bytes 196612
  27.1 39.7 %copy-start.7 = (f32[128,128]{1,0:T(8,128)S(1)}, f32[128,128]{1,0:T(8,128)}, u32[]{:S(2)}) copy-start(f32[128,128]{1,0:T(8,128)} %out_ref.3) | copy-start | bytes 196612
  27.2 39.7 %copy-start.12 = (f32[128,384]{1,0:T(8,128)S(1)}, f32[128,384]{1,0:T(8,128)}, u32[]{:S(2)}) copy-start(f32[128,384]{1,0:T(8,128)} %qkv_ref.1) | copy-start | bytes 589828
  27.3 54.5 %copy-start.10 = (s32[5]{0:T(128)}, s32[5]{0:T(128)S(1)}, u32[]{:S(2)}) copy-start(s32[5]{0:T(128)S(1)} %convert_element_type.3.inside_ref) | copy-start | bytes 64
  45.5 21.4 %all-to-all-start = ((f32[64,32,128]{2,1,0:T(8,128)}), f32[64,32,128]{2,1,0:T(8,128)S(1)}, u32[]{:S(2)}, u32[]{:S(2)}) async-start(f32[64,32,128]{2,1,0:T(8,128)} %bitcast.9), calls=%async_computation | async-start | bytes 2097152 | tf_op jit(solution)/shard_map/all_to_all | solution.py:752
  81.9 21.8 %all-to-all-start.2 = ((f32[64,32,128]{2,1,0:T(8,128)}), f32[64,32,128]{2,1,0:T(8,128)}, u32[]{:S(2)}, u32[]{:S(2)}) async-start(f32[64,32,128]{2,1,0:T(8,128)} %get-tuple-element.66), calls=%async_computation.2 | async-start | bytes 2097152 | tf_op jit(solution)/shard_map/all_to_all | solution.py:752
  95.8 23.4 %copy-start.8 = (f32[128,128]{1,0:T(8,128)}, f32[128,128]{1,0:T(8,128)S(1)}, u32[]{:S(2)}) copy-start(f32[128,128]{1,0:T(8,128)S(1)} %get-tuple-element.92.out_ref) | copy-start | bytes 196612
  106.4 17.1 %copy-start.19 = (f32[32,512]{1,0:T(8,128)S(1)}, f32[32,512]{1,0:T(8,128)}, u32[]{:S(2)}) copy-start(f32[32,512]{1,0:T(8,128)} %get-tuple-element.83) | copy-start | bytes 196612
  106.4 12.7 %collective-permute-start.4 = (f32[64,512]{1,0:T(8,128)}, f32[64,512]{1,0:T(8,128)S(1)}, u32[]{:S(2)}, u32[]{:S(2)}) collective-permute-start(f32[64,512]{1,0:T(8,128)} %get-tuple-element.75), channel_id=1, source_target_pairs={{0,16},{16,32},{32,48},{48,64},{64,80},{80,96},{96,112},{112,0},{1... | collective-permute-start | bytes 393224 | tf_op jit(solution)/shard_map/ppermute | solution.py:728
  106.7 12.5 %collective-permute-start.5 = (f32[64,512]{1,0:T(8,128)}, f32[64,512]{1,0:T(8,128)S(1)}, u32[]{:S(2)}, u32[]{:S(2)}) collective-permute-start(f32[64,512]{1,0:T(8,128)} %get-tuple-element.76), channel_id=1, source_target_pairs={{0,112},{16,0},{32,16},{48,32},{64,48},{80,64},{96,80},{112,96},{1... | collective-permute-start | bytes 393224 | tf_op jit(solution)/shard_map/ppermute | solution.py:728
  119.2 5.8 %collective-permute-start.6 = (f32[34,512]{1,0:T(8,128)S(1)}, f32[34,512]{1,0:T(8,128)S(1)}, u32[]{:S(2)}, u32[]{:S(2)}) collective-permute-start(f32[34,512]{1,0:T(8,128)S(1)} %pad_maximum_fusion), channel_id=1, source_target_pairs={{0,1},{1,2},{2,3},{3,4},{4,5},{5,6},{6,7},{7,8},{8,9},{9,10},{10,1... | collective-permute-start | bytes 208904 | tf_op jit(solution)/shard_map/ppermute | solution.py:728
  123.5 3.9 %collective-permute-start.7 = (f32[34,512]{1,0:T(8,128)S(1)}, f32[34,512]{1,0:T(8,128)S(1)}, u32[]{:S(2)}, u32[]{:S(2)}) collective-permute-start(f32[34,512]{1,0:T(8,128)S(1)} %pad_maximum_fusion.1), channel_id=1, source_target_pairs={{0,15},{1,0},{2,1},{3,2},{4,3},{5,4},{6,5},{7,6},{8,7},{9,8},{10,9... | collective-permute-start | bytes 208904 | tf_op jit(solution)/shard_map/ppermute | solution.py:728
  127.5 26.1 %all-to-all-start.3 = ((f32[64,32,128]{2,1,0:T(8,128)}), f32[64,32,128]{2,1,0:T(8,128)S(1)}, u32[]{:S(2)}, u32[]{:S(2)}) async-start(f32[64,32,128]{2,1,0:T(8,128)} %get-tuple-element.96), calls=%async_computation.3 | async-start | bytes 2097152 | tf_op jit(solution)/shard_map/all_to_all | solution.py:752
  150.3 2.2 %collective-permute-start.8 = (f32[1024,128]{1,0:T(8,128)}, f32[1024,128]{1,0:T(8,128)S(1)}, u32[]{:S(2)}, u32[]{:S(2)}) collective-permute-start(f32[1024,128]{1,0:T(8,128)} %get-tuple-element.95), channel_id=1, source_target_pairs={{0,1},{1,0},{2,3},{3,2},{4,5},{5,4},{6,7},{7,6},{8,9},{9,8},{10,11... | collective-permute-start | bytes 1572872 | tf_op jit(solution)/shard_map/ppermute | solution.py:710
  153.6 27.5 %copy-start.13 = (f32[64,32,128]{2,1,0:T(8,128)}, f32[64,32,128]{2,1,0:T(8,128)S(1)}, u32[]{:S(2)}) copy-start(f32[64,32,128]{2,1,0:T(8,128)S(1)} %all-to-all-done.3) | copy-start | bytes 3145732
  176.2 15.8 %all-to-all-start.5 = ((f32[64,16,128]{2,1,0:T(8,128)}), f32[64,16,128]{2,1,0:T(8,128)S(1)}, u32[]{:S(2)}, u32[]{:S(2)}) async-start(f32[64,16,128]{2,1,0:T(8,128)} %shard_map.150), calls=%async_computation.5 | async-start | bytes 1048576 | tf_op jit(solution)/shard_map/all_to_all | solution.py:714
  192.0 4.8 %collective-permute-start.9 = (f32[1024,128]{1,0:T(8,128)S(1)}, f32[1024,128]{1,0:T(8,128)S(1)}, u32[]{:S(2)}, u32[]{:S(2)}) collective-permute-start(f32[1024,128]{1,0:T(8,128)S(1)} %bitcast.24), channel_id=1, source_target_pairs={{0,1},{1,0},{2,3},{3,2},{4,5},{5,4},{6,7},{7,6},{8,9},{9,8},{10,11... | collective-permute-start | bytes 1572872 | tf_op jit(solution)/shard_map/ppermute | solution.py:716
  (12 other events, 102.0 us)

commit v6 on v5

--- a/solution.py
+++ b/solution.py
@@ -276,7 +276,7 @@
     pitch = groups + SPARE
     step = 32
     rows_in = step * groups
-    together = 4
+    together = 8
 
     def chunk(i, ref):
         return ref[pl.ds(i * step, step)].reshape(rows_in, channels)
@@ -667,6 +667,10 @@
     )(grad_pre, field, grad_mixed, sent, placed, expand_weight)
 
 
+def add_body(first_ref, second_ref, sum_ref):
+    sum_ref[...] = first_ref[...] + second_ref[...]
+
+
 def total_body(came_ref, total_ref):
     total = jnp.sum(came_ref[...], axis=0, keepdims=True)
     total_ref[...] = jnp.broadcast_to(total, total_ref.shape)
@@ -707,7 +711,7 @@
     chips = size // 2
     vmem = pl.BlockSpec(memory_space=pltpu.VMEM)
     pair = [(0, 1), (1, 0)]
-    own = kept + lax.ppermute(given, "core", pair)
+    own = call(add_body, (), [vmem] * 2, vmem, shape(*kept.shape))(kept, lax.ppermute(given, "core", pair))
     own, after = lax.optimization_barrier((own, after))
     came = lax.all_to_all(own.reshape(chips, SLOTS, size), PAIRS, 0, 0, tiled=True)
     total = call(total_body, (), [vmem], vmem, shape(chips, SLOTS, size))(came)

time: 199 us -> 198 us (level)
    unnamed x42 -> x44, local copies, waits for them, and re-layouts: 5.4 us -> 6.45 us
where the time goes in v6:
time: 198 us; the launch traced here: 197 us
  Pallas kernels  65.3 us (33%)
  starting transfers between devices  52.6 us (27%)
  waiting for transfers between devices  48.3 us (24%)
  blocking collectives  21.6 us (11%)
  local copies, waits for them, and re-layouts  8.46 us (4%)
    all_to_all x4, waiting for transfers between devices, swap(): return lax.all_to_all(flat, PAIRS, 0, 0, tiled=True)  30.1 us
    all_to_all x4, starting transfers between devices, swap(): return lax.all_to_all(flat, PAIRS, 0, 0, tiled=True)  25.2 us
    all_to_all x1, blocking collectives, reduce_all(): lax.all_to_all(own.reshape(chips, SLOTS, size), PAIRS, 0, 0, tiled=True)  21.6 us
    ppermute x8, starting transfers between devices, shift(): lax.ppermute(values, axes, [(i, (i + by) % count) for i in range(count)])  19.2 us
    pallas_call x1, Pallas kernels, expand_back(): call(expand_back_body, (tile_rows // count,), [pl.BlockSpec(memory_space=...  14.7 us
    pallas_call x1, Pallas kernels, attend(): call(attend_body, (), [vmem] * 5, [vmem] + [pl.BlockSpec(memory_space=pl....  14.2 us
    pallas_call x1, Pallas kernels, forward(): call(forward_body, (steps + 1,), [pl.BlockSpec(memory_space=pltpu.SMEM),...  12.4 us
    ppermute x8, waiting for transfers between devices, shift(): lax.ppermute(values, axes, [(i, (i + by) % count) for i in range(count)])  10.3 us
  transfers between devices with their start and end apart: 15, of which 10 were waited for; matrix products, arithmetic and copies ran while one was open for 1% of the time, Pallas kernels for 23%

profile of v6, /device:TPU:1, one launch (start us, length us, event | category | flops | bytes accessed | tf_op | source)
XLA Modules:
  0.0 197.4 jit_solution(16379306165285339915)
XLA Ops:
  1.5 5.9 %collective-permute-start.1 = (f32[64,128]{1,0:T(8,128)S(1)}, f32[64,128]{1,0:T(8,128)S(1)}, u32[]{:S(2)}, u32[]{:S(2)}) collective-permute-start(f32[64,128]{1,0:T(8,128)S(1)} %get-tuple-element.114), channel_id=1, source_target_pairs={{0,112},{16,0},{32,16},{48,32},{64,48},{80,64},{96,80},{112,96},{1... | collective-permute-start | bytes 98312 | tf_op jit(solution)/shard_map/ppermute | solution.py:732
  8.4 5.3 %collective-permute-done.top_ref = f32[64,128]{1,0:T(8,128)S(1)} collective-permute-done((f32[64,128]{1,0:T(8,128)S(1)}, f32[64,128]{1,0:T(8,128)S(1)}, u32[]{:S(2)}, u32[]{:S(2)}) %collective-permute-start) | collective-permute-done | bytes 32800 | tf_op jit(solution)/shard_map/ppermute | solution.py:732
  13.8 3.7 %collective-permute-start.2 = (f32[34,128]{1,0:T(8,128)S(1)}, f32[34,128]{1,0:T(8,128)S(1)}, u32[]{:S(2)}, u32[]{:S(2)}) collective-permute-start(f32[34,128]{1,0:T(8,128)S(1)} %pad_maximum_fusion.2), channel_id=1, source_target_pairs={{0,1},{1,2},{2,3},{3,4},{4,5},{5,6},{6,7},{7,8},{8,9},{9,10},{10,1... | collective-permute-start | bytes 52232 | tf_op jit(solution)/shard_map/ppermute | solution.py:732
  20.9 6.2 %all-to-all-start.1 = ((f32[64,32,128]{2,1,0:T(8,128)}), f32[64,32,128]{2,1,0:T(8,128)S(1)}, u32[]{:S(2)}, u32[]{:S(2)}) async-start(f32[64,32,128]{2,1,0:T(8,128)} %bitcast.10), calls=%async_computation.1 | async-start | bytes 2097152 | tf_op jit(solution)/shard_map/all_to_all | solution.py:756
  27.3 12.4 %shard_map.144 = (f32[8,256,128]{2,1,0:T(8,128)}, f32[32,64,512]{2,1,0:T(8,128)}, f32[32,64,512]{2,1,0:T(8,128)}, f32[64,512]{1,0:T(8,128)}, f32[64,512]{1,0:T(8...) custom-call(s32[5]{0:T(128)S(1)} %convert_element_type.3.inside_ref, f32[32,64,128]{2,1,0:T(8,128)S(1)} %copy-done.1, ...), custom_call_target="tpu_custom_call" | custom-call | flops 1610612736 | bytes 11534336 | tf_op jit(solution)/shard_map/pallas_call | solution.py:208
  39.7 5.8 %all-to-all-done.1.cot_ref = f32[64,32,128]{2,1,0:T(8,128)S(1)} async-done(((f32[64,32,128]{2,1,0:T(8,128)}), f32[64,32,128]{2,1,0:T(8,128)S(1)}, u32[]{:S(2)}, u32[]{:S(2)}) %all-to-all-start.1) | async-done | bytes 1048608 | tf_op jit(solution)/shard_map/all_to_all | solution.py:756
  45.5 4.8 %all-to-all-start = ((f32[64,32,128]{2,1,0:T(8,128)}), f32[64,32,128]{2,1,0:T(8,128)S(1)}, u32[]{:S(2)}, u32[]{:S(2)}) async-start(f32[64,32,128]{2,1,0:T(8,128)} %bitcast.9), calls=%async_computation | async-start | bytes 2097152 | tf_op jit(solution)/shard_map/all_to_all | solution.py:756
  50.3 16.5 %all-to-all-done.mixed_ref = f32[64,32,128]{2,1,0:T(8,128)S(1)} async-done(((f32[64,32,128]{2,1,0:T(8,128)}), f32[64,32,128]{2,1,0:T(8,128)S(1)}, u32[]{:S(2)}, u32[]{:S(2)}) %all-to-all-start) | async-done | bytes 1048608 | tf_op jit(solution)/shard_map/all_to_all | solution.py:756
  66.9 14.2 %shard_map.145 = (f32[64,32,128]{2,1,0:T(8,128)}, f32[2560,128]{1,0:T(8,128)}, f32[3,2560,128]{2,1,0:T(8,128)}, f32[128,128]{1,0:T(8,128)}) custom-call(f32[64,32,128]{2,1,0:T(8,128)S(1)} %all-to-all-done.mixed_ref, f32[64,32,128]{2,1,0:T(8,128)S(1)} %all-to-all-done.1.cot_ref, f32[128,384]{1,0:T(8,128)S(1)} %copy-done.13, f32[128,128]{1,0:T(8,128)S(1)} %copy-done.8, ...), custom_call_target="tpu_custom_call" | custom-call | flops 3019898880 | bytes 4194304 | tf_op jit(solution)/shard_map/pallas_call | solution.py:375
  81.1 6.1 %all-to-all-start.2 = ((f32[64,32,128]{2,1,0:T(8,128)}), f32[64,32,128]{2,1,0:T(8,128)}, u32[]{:S(2)}, u32[]{:S(2)}) async-start(f32[64,32,128]{2,1,0:T(8,128)} %get-tuple-element.66), calls=%async_computation.2 | async-start | bytes 2097152 | tf_op jit(solution)/shard_map/all_to_all | solution.py:756
  90.6 3.8 %shard_map.146 = (f32[64,32,128]{2,1,0:T(8,128)}, f32[128,384]{1,0:T(8,128)S(1)}, f32[128,128]{1,0:T(8,128)S(1)}) custom-call(f32[64,32,128]{2,1,0:T(8,128)S(1)} %all-to-all-done.mixed_ref, f32[64,32,128]{2,1,0:T(8,128)S(1)} %all-to-all-done.1.cot_ref, f32[2560,128]{1,0:T(8,128)S(1)} %copy-done.3, f32[3,2560,128]{2,1,0:T(8,128)S(1)} %copy-done.2, ...), custom_call_target="tpu_custom_call" | custom-call | flops 1006632960 | bytes 7340032 | tf_op jit(solution)/shard_map/pallas_call | solution.py:421
  95.1 7.8 %all-to-all-done.2 = f32[64,32,128]{2,1,0:T(8,128)} async-done(((f32[64,32,128]{2,1,0:T(8,128)}), f32[64,32,128]{2,1,0:T(8,128)}, u32[]{:S(2)}, u32[]{:S(2)}) %all-to-all-start.2) | async-done | bytes 1048608 | tf_op jit(solution)/shard_map/all_to_all | solution.py:756
  102.9 2.7 %shard_map.147 = (f32[64,512]{1,0:T(8,128)}, f32[64,512]{1,0:T(8,128)}, f32[32,512]{1,0:T(8,128)}, f32[32,512]{1,0:T(8,128)}) custom-call(f32[8,256,128]{2,1,0:T(8,128)} %bitcast.13.came_ref, f32[32,64,128]{2,1,0:T(8,128)} %cot_ref.3, f32[64,512]{1,0:T(8,128)} %get-tuple-element.71.top_ref, f32[64,512]{1,0:T(8,128)} %get-tuple-element.72.bottom_ref, ...), custom_call_target="tpu_custom_call" | custom-call | flops 75497472 | bytes 2097152 | tf_op jit(solution)/shard_map/pallas_call | solution.py:470
  105.7 5.1 %collective-permute-start.5 = (f32[64,512]{1,0:T(8,128)}, f32[64,512]{1,0:T(8,128)S(1)}, u32[]{:S(2)}, u32[]{:S(2)}) collective-permute-start(f32[64,512]{1,0:T(8,128)} %get-tuple-element.76), channel_id=1, source_target_pairs={{0,112},{16,0},{32,16},{48,32},{64,48},{80,64},{96,80},{112,96},{1... | collective-permute-start | bytes 393224 | tf_op jit(solution)/shard_map/ppermute | solution.py:732
  110.8 7.4 %shard_map.148 = (f32[32,64,128]{2,1,0:T(8,128)}, f32[32,64,512]{2,1,0:T(8,128)}, f32[128,512]{1,0:T(8,128)}) custom-call(f32[8,256,128]{2,1,0:T(8,128)} %bitcast.13.came_ref, f32[32,64,128]{2,1,0:T(8,128)} %cot_ref.3, f32[32,64,512]{2,1,0:T(8,128)} %get-tuple-element.77.depth_out_ref, f32[512,128]{1,0:T(8,128)} %weight_ref.5), custom_call_target="tpu_custom_call" | custom-call | flops 1610612736 | bytes 11534336 | tf_op jit(solution)/shard_map/pallas_call | solution.py:516
  118.2 4.3 %collective-permute-start.6 = (f32[34,512]{1,0:T(8,128)S(1)}, f32[34,512]{1,0:T(8,128)S(1)}, u32[]{:S(2)}, u32[]{:S(2)}) collective-permute-start(f32[34,512]{1,0:T(8,128)S(1)} %pad_maximum_fusion), channel_id=1, source_target_pairs={{0,1},{1,2},{2,3},{3,4},{4,5},{5,6},{6,7},{7,8},{8,9},{9,10},{10,1... | collective-permute-start | bytes 208904 | tf_op jit(solution)/shard_map/ppermute | solution.py:732
  124.0 2.5 %collective-permute-done.7.right_ref = f32[34,512]{1,0:T(8,128)S(1)} collective-permute-done((f32[34,512]{1,0:T(8,128)S(1)}, f32[34,512]{1,0:T(8,128)S(1)}, u32[]{:S(2)}, u32[]{:S(2)}) %collective-permute-start.7) | collective-permute-done | bytes 69664 | tf_op jit(solution)/shard_map/ppermute | solution.py:732
  126.5 8.0 %all-to-all-start.3 = ((f32[64,32,128]{2,1,0:T(8,128)}), f32[64,32,128]{2,1,0:T(8,128)S(1)}, u32[]{:S(2)}, u32[]{:S(2)}) async-start(f32[64,32,128]{2,1,0:T(8,128)} %get-tuple-element.96), calls=%async_computation.3 | async-start | bytes 2097152 | tf_op jit(solution)/shard_map/all_to_all | solution.py:756
  134.6 14.7 %shard_map.149 = (f32[32,64,512]{2,1,0:T(8,128)}, f32[1024,128]{1,0:T(8,128)}, f32[1024,128]{1,0:T(8,128)}) custom-call(s32[5]{0:T(128)} %copy-done.11, f32[32,64,512]{2,1,0:T(8,128)} %get-tuple-element.79.grad_ref.before_ref.after_ref, f32[32,64,512]{2,1,0:T(8,128)} %get-tuple-element.79.grad_ref.before_ref.after_ref, ...), custom_call_target="tpu_custom_call" | custom-call | flops 805306368 | bytes 13631488 | tf_op jit(solution)/shard_map/pallas_call | solution.py:604
  152.6 21.6 %all_to_all.30.came_ref = f32[64,16,128]{2,1,0:T(8,128)S(1)} all-to-all(f32[64,16,128]{2,1,0:T(8,128)S(1)} %bitcast.24), channel_id=1, replica_groups=mesh['row'=8,'ch'=8,'core'=2] {'row','ch'}, dimensions={0} | all-to-all | bytes 1048576 | tf_op jit(solution)/shard_map/all_to_all | solution.py:716
  175.2 4.9 %all-to-all-start.5 = ((f32[64,16,128]{2,1,0:T(8,128)}), f32[64,16,128]{2,1,0:T(8,128)S(1)}, u32[]{:S(2)}, u32[]{:S(2)}) async-start(f32[64,16,128]{2,1,0:T(8,128)} %shard_map.151), calls=%async_computation.5 | async-start | bytes 1048576 | tf_op jit(solution)/shard_map/all_to_all | solution.py:718
  180.2 6.5 %shard_map.152 = (f32[32,64,128]{2,1,0:T(8,128)}, f32[32,64,128]{2,1,0:T(8,128)}) custom-call(f32[32,64,512]{2,1,0:T(8,128)} %get-tuple-element.98.grad_pre_ref, f32[32,64,128]{2,1,0:T(8,128)} %field_ref.5, f32[32,64,128]{2,1,0:T(8,128)} %get-tuple-element.99.grad_mixed_ref, f32[8,256,128]{2,1,0:T(8,128)} %get-tuple-element.64.sent_ref, ...), custom_call_target="tpu_custom_call" | custom-call | flops 805306368 | bytes 10485760 | tf_op jit(solution)/shard_map/pallas_call | solution.py:658
  186.7 4.3 %all-to-all-done.5 = f32[64,16,128]{2,1,0:T(8,128)S(1)} async-done(((f32[64,16,128]{2,1,0:T(8,128)}), f32[64,16,128]{2,1,0:T(8,128)S(1)}, u32[]{:S(2)}, u32[]{:S(2)}) %all-to-all-start.5) | async-done | bytes 524320 | tf_op jit(solution)/shard_map/all_to_all | solution.py:718
  191.0 3.2 %collective-permute-start.9 = (f32[1024,128]{1,0:T(8,128)S(1)}, f32[1024,128]{1,0:T(8,128)S(1)}, u32[]{:S(2)}, u32[]{:S(2)}) collective-permute-start(f32[1024,128]{1,0:T(8,128)S(1)} %bitcast.25), channel_id=1, source_target_pairs={{0,1},{1,0},{2,3},{3,2},{4,5},{5,4},{6,7},{7,6},{8,9},{9,8},{10,11... | collective-permute-start | bytes 1572872 | tf_op jit(solution)/shard_map/ppermute | solution.py:720
  (74 shorter events, 18.6 us)
Async XLA Ops:
  0.6 26.7 %copy-start.4 = (f32[512,128]{1,0:T(8,128)S(1)}, f32[512,128]{1,0:T(8,128)}, u32[]{:S(2)}) copy-start(f32[512,128]{1,0:T(8,128)} %weight_ref.5) | copy-start | bytes 786436
  0.6 26.7 %copy-start.10 = (f32[9,512]{1,0:T(8,128)S(1)}, f32[9,512]{1,0:T(8,128)}, u32[]{:S(2)}) copy-start(f32[9,512]{1,0:T(8,128)} %depth_ref.3) | copy-start | bytes 55300
  1.5 7.0 %collective-permute-start.1 = (f32[64,128]{1,0:T(8,128)S(1)}, f32[64,128]{1,0:T(8,128)S(1)}, u32[]{:S(2)}, u32[]{:S(2)}) collective-permute-start(f32[64,128]{1,0:T(8,128)S(1)} %get-tuple-element.114), channel_id=1, source_target_pairs={{0,112},{16,0},{32,16},{48,32},{64,48},{80,64},{96,80},{112,96},{1... | collective-permute-start | bytes 98312 | tf_op jit(solution)/shard_map/ppermute | solution.py:732
  7.4 6.4 %collective-permute-start = (f32[64,128]{1,0:T(8,128)S(1)}, f32[64,128]{1,0:T(8,128)S(1)}, u32[]{:S(2)}, u32[]{:S(2)}) collective-permute-start(f32[64,128]{1,0:T(8,128)S(1)} %get-tuple-element.115), channel_id=1, source_target_pairs={{0,16},{16,32},{32,48},{48,64},{64,80},{80,96},{96,112},{112,0},{1... | collective-permute-start | bytes 98312 | tf_op jit(solution)/shard_map/ppermute | solution.py:732
  13.8 6.1 %collective-permute-start.2 = (f32[34,128]{1,0:T(8,128)S(1)}, f32[34,128]{1,0:T(8,128)S(1)}, u32[]{:S(2)}, u32[]{:S(2)}) collective-permute-start(f32[34,128]{1,0:T(8,128)S(1)} %pad_maximum_fusion.2), channel_id=1, source_target_pairs={{0,1},{1,2},{2,3},{3,4},{4,5},{5,6},{6,7},{7,8},{8,9},{9,10},{10,1... | collective-permute-start | bytes 52232 | tf_op jit(solution)/shard_map/ppermute | solution.py:732
  17.5 3.4 %collective-permute-start.3 = (f32[34,128]{1,0:T(8,128)S(1)}, f32[34,128]{1,0:T(8,128)S(1)}, u32[]{:S(2)}, u32[]{:S(2)}) collective-permute-start(f32[34,128]{1,0:T(8,128)S(1)} %pad_maximum_fusion.3), channel_id=1, source_target_pairs={{0,15},{1,0},{2,1},{3,2},{4,3},{5,4},{6,5},{7,6},{8,7},{9,8},{10,9... | collective-permute-start | bytes 52232 | tf_op jit(solution)/shard_map/ppermute | solution.py:732
  20.9 24.5 %all-to-all-start.1 = ((f32[64,32,128]{2,1,0:T(8,128)}), f32[64,32,128]{2,1,0:T(8,128)S(1)}, u32[]{:S(2)}, u32[]{:S(2)}) async-start(f32[64,32,128]{2,1,0:T(8,128)} %bitcast.10), calls=%async_computation.1 | async-start | bytes 2097152 | tf_op jit(solution)/shard_map/all_to_all | solution.py:756
  27.1 23.1 %copy-start.17 = (f32[4,64,64]{2,1,0:T(8,128)S(1)}, f32[4,64,64]{2,1,0:T(8,128)}, u32[]{:S(2)}) copy-start(f32[4,64,64]{2,1,0:T(8,128)} %param.14) | copy-start | bytes 196612
  27.1 39.7 %copy-start.8 = (f32[128,128]{1,0:T(8,128)S(1)}, f32[128,128]{1,0:T(8,128)}, u32[]{:S(2)}) copy-start(f32[128,128]{1,0:T(8,128)} %out_ref.3) | copy-start | bytes 196612
  27.2 39.7 %copy-start.13 = (f32[128,384]{1,0:T(8,128)S(1)}, f32[128,384]{1,0:T(8,128)}, u32[]{:S(2)}) copy-start(f32[128,384]{1,0:T(8,128)} %qkv_ref.1) | copy-start | bytes 589828
  27.3 53.7 %copy-start.11 = (s32[5]{0:T(128)}, s32[5]{0:T(128)S(1)}, u32[]{:S(2)}) copy-start(s32[5]{0:T(128)S(1)} %convert_element_type.3.inside_ref) | copy-start | bytes 64
  45.5 21.4 %all-to-all-start = ((f32[64,32,128]{2,1,0:T(8,128)}), f32[64,32,128]{2,1,0:T(8,128)S(1)}, u32[]{:S(2)}, u32[]{:S(2)}) async-start(f32[64,32,128]{2,1,0:T(8,128)} %bitcast.9), calls=%async_computation | async-start | bytes 2097152 | tf_op jit(solution)/shard_map/all_to_all | solution.py:756
  81.1 21.8 %all-to-all-start.2 = ((f32[64,32,128]{2,1,0:T(8,128)}), f32[64,32,128]{2,1,0:T(8,128)}, u32[]{:S(2)}, u32[]{:S(2)}) async-start(f32[64,32,128]{2,1,0:T(8,128)} %get-tuple-element.66), calls=%async_computation.2 | async-start | bytes 2097152 | tf_op jit(solution)/shard_map/all_to_all | solution.py:756
  95.1 23.0 %copy-start.9 = (f32[128,128]{1,0:T(8,128)}, f32[128,128]{1,0:T(8,128)S(1)}, u32[]{:S(2)}) copy-start(f32[128,128]{1,0:T(8,128)S(1)} %get-tuple-element.92.out_ref) | copy-start | bytes 196612
  105.6 16.9 %copy-start.20 = (f32[32,512]{1,0:T(8,128)S(1)}, f32[32,512]{1,0:T(8,128)}, u32[]{:S(2)}) copy-start(f32[32,512]{1,0:T(8,128)} %get-tuple-element.83) | copy-start | bytes 196612
  105.6 12.5 %collective-permute-start.4 = (f32[64,512]{1,0:T(8,128)}, f32[64,512]{1,0:T(8,128)S(1)}, u32[]{:S(2)}, u32[]{:S(2)}) collective-permute-start(f32[64,512]{1,0:T(8,128)} %get-tuple-element.75), channel_id=1, source_target_pairs={{0,16},{16,32},{32,48},{48,64},{64,80},{80,96},{96,112},{112,0},{1... | collective-permute-start | bytes 393224 | tf_op jit(solution)/shard_map/ppermute | solution.py:732
  105.7 12.5 %collective-permute-start.5 = (f32[64,512]{1,0:T(8,128)}, f32[64,512]{1,0:T(8,128)S(1)}, u32[]{:S(2)}, u32[]{:S(2)}) collective-permute-start(f32[64,512]{1,0:T(8,128)} %get-tuple-element.76), channel_id=1, source_target_pairs={{0,112},{16,0},{32,16},{48,32},{64,48},{80,64},{96,80},{112,96},{1... | collective-permute-start | bytes 393224 | tf_op jit(solution)/shard_map/ppermute | solution.py:732
  118.2 5.8 %collective-permute-start.6 = (f32[34,512]{1,0:T(8,128)S(1)}, f32[34,512]{1,0:T(8,128)S(1)}, u32[]{:S(2)}, u32[]{:S(2)}) collective-permute-start(f32[34,512]{1,0:T(8,128)S(1)} %pad_maximum_fusion), channel_id=1, source_target_pairs={{0,1},{1,2},{2,3},{3,4},{4,5},{5,6},{6,7},{7,8},{8,9},{9,10},{10,1... | collective-permute-start | bytes 208904 | tf_op jit(solution)/shard_map/ppermute | solution.py:732
  122.6 3.9 %collective-permute-start.7 = (f32[34,512]{1,0:T(8,128)S(1)}, f32[34,512]{1,0:T(8,128)S(1)}, u32[]{:S(2)}, u32[]{:S(2)}) collective-permute-start(f32[34,512]{1,0:T(8,128)S(1)} %pad_maximum_fusion.1), channel_id=1, source_target_pairs={{0,15},{1,0},{2,1},{3,2},{4,3},{5,4},{6,5},{7,6},{8,7},{9,8},{10,9... | collective-permute-start | bytes 208904 | tf_op jit(solution)/shard_map/ppermute | solution.py:732
  126.5 26.1 %all-to-all-start.3 = ((f32[64,32,128]{2,1,0:T(8,128)}), f32[64,32,128]{2,1,0:T(8,128)S(1)}, u32[]{:S(2)}, u32[]{:S(2)}) async-start(f32[64,32,128]{2,1,0:T(8,128)} %get-tuple-element.96), calls=%async_computation.3 | async-start | bytes 2097152 | tf_op jit(solution)/shard_map/all_to_all | solution.py:756
  149.3 2.2 %collective-permute-start.8 = (f32[1024,128]{1,0:T(8,128)}, f32[1024,128]{1,0:T(8,128)S(1)}, u32[]{:S(2)}, u32[]{:S(2)}) collective-permute-start(f32[1024,128]{1,0:T(8,128)} %get-tuple-element.95), channel_id=1, source_target_pairs={{0,1},{1,0},{2,3},{3,2},{4,5},{5,4},{6,7},{7,6},{8,9},{9,8},{10,11... | collective-permute-start | bytes 1572872 | tf_op jit(solution)/shard_map/ppermute | solution.py:714
  152.6 27.5 %copy-start.14 = (f32[64,32,128]{2,1,0:T(8,128)}, f32[64,32,128]{2,1,0:T(8,128)S(1)}, u32[]{:S(2)}) copy-start(f32[64,32,128]{2,1,0:T(8,128)S(1)} %all-to-all-done.3) | copy-start | bytes 3145732
  175.2 15.8 %all-to-all-start.5 = ((f32[64,16,128]{2,1,0:T(8,128)}), f32[64,16,128]{2,1,0:T(8,128)S(1)}, u32[]{:S(2)}, u32[]{:S(2)}) async-start(f32[64,16,128]{2,1,0:T(8,128)} %shard_map.151), calls=%async_computation.5 | async-start | bytes 1048576 | tf_op jit(solution)/shard_map/all_to_all | solution.py:718
  191.0 4.8 %collective-permute-start.9 = (f32[1024,128]{1,0:T(8,128)S(1)}, f32[1024,128]{1,0:T(8,128)S(1)}, u32[]{:S(2)}, u32[]{:S(2)}) collective-permute-start(f32[1024,128]{1,0:T(8,128)S(1)} %bitcast.25), channel_id=1, source_target_pairs={{0,1},{1,0},{2,3},{3,2},{4,5},{5,4},{6,7},{7,6},{8,9},{9,8},{10,11... | collective-permute-start | bytes 1572872 | tf_op jit(solution)/shard_map/ppermute | solution.py:720
  (13 other events, 102.8 us)
